TPU v7x, 32 devices: a whole 2x2x4 slice. The times are simulated.
32 devices in a mesh: dp: 8 (over y, x, core), branch: 4 (over z).
Axes of the slice: x: 2, y: 2, z: 4, core: 2. Of those that a mesh axis runs over, the one named last changes fastest.
Arguments:
- frames: bfloat16 [8, 16, 14, 14, 832], P('dp', None, None, None, 'branch'), may hold values from -200 to 200
- lengths: int32 [8], P('dp'), may hold values from 2 to 16, as said below
- cotangent: bfloat16 [8, 8, 7, 7, 832], P('dp'), may hold values from -6 to 6
- pointwise: bfloat16 [2, 832, 576], replicated, may hold values from -0.21875 to 0.21875
- conv_mid: bfloat16 [2, 27, 160, 320], replicated, may hold values from -0.09375 to 0.09375
- conv_small: bfloat16 [2, 27, 32, 128], replicated, may hold values from -0.21875 to 0.21875
- gains: float32 [2, 1024], replicated, may hold values from 0.5 to 1.5
- shifts: float32 [2, 1024], replicated, may hold values from -2 to 2
Outputs:
- activations: bfloat16 [8, 8, 7, 7, 832], P('dp')
- input_grad: bfloat16 [8, 16, 14, 14, 832], P('dp', None, None, None, 'branch')
- pointwise_grad: float32 [2, 832, 576], replicated
- mid_grad: float32 [2, 27, 160, 320], replicated
- small_grad: float32 [2, 27, 32, 128], replicated
- gain_grad: float32 [2, 1024], replicated
- shift_grad: float32 [2, 1024], replicated
Inputs may be any that keep to these rules, and one draw needn't show every extreme that they name: `lengths`: every length is even; some clip has all 16 frames.
All inputs are finite; a program needn't handle non-finite values.
Results may differ from a plain program's by a relative error of at most 0.013.
Values may be sent and summed in bfloat16 or wider, within the bound.
No kernel may reach another device: no remote copies, remote signals or barrier semaphores. Data moves between devices by JAX's collectives and lax.ppermute only.
A program may use at most 384 MiB of HBM per device.

v0:
```python
import jax
import jax.numpy as jnp
from jax import lax
from jax.sharding import PartitionSpec as P

DIRECT = 256
MID_IN = 160
MID_OUT = 320
SMALL_IN = 32
SMALL_OUT = 128
POOLED = 128
SQUEEZED = 576
NORMED = 1024
LANE = 128
SLOT_RED = 20


epsilon = 1e-05


def shortened(value):
    return jax.tree.map(lambda a: a.astype(jnp.bfloat16) if a.dtype == jnp.float32 else a, value)


def slot_tables():
    half_width = DIRECT // 2
    quarter = MID_OUT // 4
    kind_list = [0, 0, 1, 1, 1, 1, 2, 3]
    main_columns = [0, half_width, 0, 0, 0, 0, DIRECT + MID_IN, DIRECT + MID_IN + SMALL_IN]
    main_widths = [half_width, half_width, 0, 0, 0, 0, SMALL_IN, POOLED]
    second_offsets = (
        [0, 0] + [SQUEEZED + quarter * number for number in range(4)] + [SQUEEZED + MID_OUT, 0]
    )
    second_widths = [0, 0, quarter, quarter, quarter, quarter, SMALL_OUT, 0]
    slab_widths = [half_width, half_width, quarter, quarter, quarter, quarter, SMALL_OUT, POOLED]
    slab_offsets = []
    running = 0
    for slab_width in slab_widths:
        slab_offsets.append(running)
        running = running + slab_width
    return (
        kind_list,
        main_columns,
        main_widths,
        second_offsets,
        second_widths,
        slab_offsets,
        slab_widths,
    )


def pick_entry(table_rows, index_value):
    entries = jnp.asarray(table_rows, jnp.int32)
    return jnp.sum(
        jnp.where(jnp.arange(len(table_rows), dtype=jnp.int32) == index_value, entries, 0)
    )


def box_sum(values):
    for dimension in (1, 2, 3):
        extent = values.shape[dimension]
        widths = [(0, 0)] * 5
        widths[dimension] = (1, 1)
        padded = jnp.pad(values, widths)
        values = (
            lax.slice_in_dim(padded, 0, extent, axis=dimension)
            + lax.slice_in_dim(padded, 1, extent + 1, axis=dimension)
            + lax.slice_in_dim(padded, 2, extent + 2, axis=dimension)
        )
    return values


def cell_counts(values, frame_mask):
    return jnp.maximum(box_sum(jnp.broadcast_to(frame_mask, values.shape[:4] + (1,))), 1.0)


def pool_mean(values, frame_mask):
    return box_sum(values) / cell_counts(values, frame_mask)


def pool_adjoint(values, frame_mask):
    return box_sum(values / cell_counts(values, frame_mask))


def keep_same(values, frame_mask):
    return values


def pad_cells(values):
    return jnp.pad(values, ((0, 0), (1, 1), (1, 1), (1, 1), (0, 0)))


def pad_lanes(values, target):
    return jnp.pad(values, ((0, 0),) * 4 + ((0, target - values.shape[-1]),))


def tap_window(padded, stencil, extent):
    along_time, along_rows, along_cols = (stencil // 9, stencil // 3 % 3, stencil % 3)
    return padded[
        :,
        along_time : along_time + extent[0],
        along_rows : along_rows + extent[1],
        along_cols : along_cols + extent[2],
        :,
    ]


def conv_forward(act_low, kernel):
    extent = act_low.shape[1:4]
    padded = pad_cells(act_low)
    result = jnp.zeros(act_low.shape[:4] + (kernel.shape[2],), jnp.float32)
    for stencil in range(27):
        result = result + jnp.dot(
            tap_window(padded, stencil, extent), kernel[stencil], preferred_element_type=jnp.float32
        )
    return result


def conv_backward(act_low, kernel, grad_low):
    extent = act_low.shape[1:4]
    padded_act = pad_cells(act_low)
    padded_grad = pad_cells(grad_low)
    d_act = jnp.zeros(act_low.shape, jnp.float32)
    pieces = []
    for stencil in range(27):
        d_act = d_act + jnp.einsum(
            "abcdo,io->abcdi",
            tap_window(padded_grad, 26 - stencil, extent),
            kernel[stencil],
            preferred_element_type=jnp.float32,
        )
        pieces.append(
            jnp.einsum(
                "abcdi,abcdo->io",
                tap_window(padded_act, stencil, extent),
                grad_low,
                preferred_element_type=jnp.float32,
            )
        )
    return (d_act, jnp.stack(pieces))


def plain_branch(inputs, weights, frame_mask):
    return jnp.dot(inputs, weights, preferred_element_type=jnp.float32)


def empty_branch(inputs, weights, frame_mask):
    return jnp.zeros(inputs.shape[:4] + (weights.shape[1],), jnp.float32)


def pooled_branch(inputs, weights, frame_mask):
    return pool_mean(jnp.dot(inputs, weights, preferred_element_type=jnp.float32), frame_mask)


def second_none(reduced, first_low, mid_kernel, small_kernel):
    return jnp.zeros(reduced.shape[:4] + (LANE,), jnp.float32)


def second_mid(reduced, first_low, mid_kernel, small_kernel):
    return pad_lanes(conv_forward(reduced, mid_kernel), LANE)


def second_small(reduced, first_low, mid_kernel, small_kernel):
    return pad_lanes(conv_forward(first_low[..., :SMALL_IN], small_kernel), LANE)


def back_none(reduced, first_low, mid_kernel, small_kernel, grad_low):
    return (
        jnp.zeros(reduced.shape, jnp.float32),
        jnp.zeros(reduced.shape[:4] + (LANE,), jnp.float32),
        jnp.zeros(mid_kernel.shape, jnp.float32),
        jnp.zeros(small_kernel.shape, jnp.float32),
    )


def back_mid(reduced, first_low, mid_kernel, small_kernel, grad_low):
    d_act, d_kernel = conv_backward(reduced, mid_kernel, grad_low[..., : mid_kernel.shape[2]])
    return (
        d_act,
        jnp.zeros(reduced.shape[:4] + (LANE,), jnp.float32),
        d_kernel,
        jnp.zeros(small_kernel.shape, jnp.float32),
    )


def back_small(reduced, first_low, mid_kernel, small_kernel, grad_low):
    d_act, d_kernel = conv_backward(
        first_low[..., :SMALL_IN], small_kernel, grad_low[..., :SMALL_OUT]
    )
    return (
        jnp.zeros(reduced.shape, jnp.float32),
        pad_lanes(d_act, LANE),
        jnp.zeros(mid_kernel.shape, jnp.float32),
        d_kernel,
    )


def voxel_sum(values):
    return jnp.sum(values, axis=(0, 1, 2, 3))


def silu_slope(shifted):
    sigmoid_value = jax.nn.sigmoid(shifted)
    return sigmoid_value * (1.0 + shifted * (1.0 - sigmoid_value))


def normalized(record, section_name, stat_sums, squares, voxel_count, frame_mask):
    center = stat_sums / voxel_count
    inverse = lax.rsqrt(squares / voxel_count - center * center + epsilon)
    scaled = (record["pre_" + section_name] - center) * inverse
    shifted = record["gain_" + section_name] * scaled + record["shift_" + section_name]
    record["inverse_" + section_name] = inverse
    record["scaled_" + section_name] = scaled
    record["shifted_" + section_name] = shifted
    record["act_" + section_name] = (
        jax.nn.silu(shifted) * frame_mask * record["lane_" + section_name]
    ).astype(jnp.bfloat16)


def norm_back(error_term, record, section_name, total_g, total_gx, voxel_count, frame_mask):
    return (
        record["gain_" + section_name]
        * record["inverse_" + section_name]
        * (error_term - (total_g + record["scaled_" + section_name] * total_gx) / voxel_count)
        * frame_mask
    )


def input_product(inputs, grad_low):
    return jnp.einsum("abcdi,abcdo->io", inputs, grad_low, preferred_element_type=jnp.float32)


def zero_product(inputs, grad_low):
    return jnp.zeros((inputs.shape[-1], grad_low.shape[-1]), jnp.float32)


def weight_back(grad_low, weights):
    return jnp.einsum("abcdo,io->abcdi", grad_low, weights, preferred_element_type=jnp.float32)


def zero_back(grad_low, weights):
    return jnp.zeros(grad_low.shape[:4] + (weights.shape[0],), jnp.float32)


def place_vector(values, start_index):
    return lax.dynamic_update_slice(
        jnp.zeros((NORMED + LANE,), jnp.float32), values, (start_index,)
    )


def flat_join(arrays, groups):
    flat = jnp.concatenate([array.reshape(-1) for array in arrays])
    length = flat.shape[0]
    padded = -(-length // groups) * groups
    return jnp.pad(flat, (0, padded - length))


def flat_split(flat, shapes):
    pieces = []
    start = 0
    for shape in shapes:
        count = 1
        for extent in shape:
            count = count * extent
        pieces.append(flat[start : start + count].reshape(shape))
        start = start + count
    return pieces


def forward_block(inputs, frame_mask, weights, branch_index, hosted):
    pointwise, conv_mid, conv_small, gains, shifts = weights
    (
        kind_list,
        main_columns,
        main_widths,
        second_offsets,
        second_widths,
        slab_offsets,
        slab_widths,
    ) = slot_tables()
    quarter = MID_OUT // 4
    wide_point = jnp.pad(pointwise, ((0, 0), (0, LANE)))
    wide_gains = jnp.pad(gains, (0, LANE))
    wide_shifts = jnp.pad(shifts, (0, LANE))
    side_count = inputs.shape[2]
    local_count = jnp.sum(frame_mask) * float(side_count * side_count)
    lane_ids = jnp.arange(LANE, dtype=jnp.int32)
    records = []
    for virtual in range(hosted):
        virtual_slot = branch_index * hosted + virtual
        branch_kind = pick_entry(kind_list, virtual_slot)
        column = pick_entry(main_columns, virtual_slot)
        reduce_start = DIRECT + SLOT_RED * virtual_slot
        main_weights = lax.dynamic_slice_in_dim(wide_point, column, LANE, 1)
        reduce_weights = lax.dynamic_slice_in_dim(pointwise, reduce_start, SLOT_RED, 1)
        main_pre = lax.switch(
            branch_kind,
            [plain_branch, empty_branch, plain_branch, pooled_branch],
            inputs,
            main_weights,
            frame_mask,
        )
        reduce_pre = jnp.dot(inputs, reduce_weights, preferred_element_type=jnp.float32)
        records.append(
            {
                "slot": virtual_slot,
                "kind": branch_kind,
                "column": column,
                "reduce_start": reduce_start,
                "main_weights": main_weights,
                "reduce_weights": reduce_weights,
                "pre_first": jnp.concatenate([main_pre, reduce_pre], axis=-1),
                "gain_first": jnp.concatenate(
                    [
                        lax.dynamic_slice_in_dim(wide_gains, column, LANE),
                        lax.dynamic_slice_in_dim(gains, reduce_start, SLOT_RED),
                    ]
                ),
                "shift_first": jnp.concatenate(
                    [
                        lax.dynamic_slice_in_dim(wide_shifts, column, LANE),
                        lax.dynamic_slice_in_dim(shifts, reduce_start, SLOT_RED),
                    ]
                ),
                "lane_first": jnp.concatenate(
                    [
                        (lane_ids < pick_entry(main_widths, virtual_slot)).astype(jnp.float32),
                        jnp.ones((SLOT_RED,), jnp.float32),
                    ]
                ),
            }
        )
    stat_sums = jnp.stack([voxel_sum(record["pre_first"] * frame_mask) for record in records])
    squares = jnp.stack(
        [voxel_sum(record["pre_first"] * record["pre_first"] * frame_mask) for record in records]
    )
    stat_sums, squares, voxel_count = lax.psum((stat_sums, squares, local_count), "dp")
    for virtual, record in enumerate(records):
        normalized(record, "first", stat_sums[virtual], squares[virtual], voxel_count, frame_mask)
    reduced = lax.all_gather(
        shortened(
            jnp.concatenate([record["act_first"][..., LANE:] for record in records], axis=-1)
        ),
        "branch",
        axis=4,
        tiled=True,
    )
    for record in records:
        virtual_slot = record["slot"]
        record["mid_start"] = quarter * jnp.clip(virtual_slot - 2, 0, 3)
        record["mid_kernel"] = lax.dynamic_slice_in_dim(conv_mid, record["mid_start"], quarter, 2)
        record["pre_second"] = lax.switch(
            record["kind"],
            [second_none, second_mid, second_small, second_none],
            reduced,
            record["act_first"],
            record["mid_kernel"],
            conv_small,
        )
        offset = pick_entry(second_offsets, virtual_slot)
        record["offset"] = offset
        record["gain_second"] = lax.dynamic_slice_in_dim(wide_gains, offset, LANE)
        record["shift_second"] = lax.dynamic_slice_in_dim(wide_shifts, offset, LANE)
        record["lane_second"] = (lane_ids < pick_entry(second_widths, virtual_slot)).astype(
            jnp.float32
        )
    stat_sums = jnp.stack([voxel_sum(record["pre_second"] * frame_mask) for record in records])
    squares = jnp.stack(
        [voxel_sum(record["pre_second"] * record["pre_second"] * frame_mask) for record in records]
    )
    stat_sums, squares = lax.psum((stat_sums, squares), "dp")
    slab_list = []
    for virtual, record in enumerate(records):
        normalized(record, "second", stat_sums[virtual], squares[virtual], voxel_count, frame_mask)
        sectioned = (record["kind"] == 1) | (record["kind"] == 2)
        slab_list.append(
            jnp.where(sectioned, record["act_second"], record["act_first"][..., :LANE])
        )
    gathered = lax.all_gather(
        shortened(jnp.concatenate(slab_list, axis=-1)), "branch", axis=4, tiled=True
    )
    output = jnp.concatenate(
        [
            gathered[..., LANE * position : LANE * position + slab_width]
            for position, slab_width in enumerate(slab_widths)
        ],
        axis=-1,
    )
    return (output, (records, reduced, voxel_count))


def backward_block(inputs, frame_mask, weights, saved, slab_grads):
    pointwise, conv_mid, conv_small, gains, shifts = weights
    records, reduced, voxel_count = saved
    second_error = [
        slab_grads[virtual]
        * silu_slope(record["shifted_second"])
        * frame_mask
        * record["lane_second"]
        for virtual, record in enumerate(records)
    ]
    local_g2 = jnp.stack([voxel_sum(error_term) for error_term in second_error])
    local_gx2 = jnp.stack(
        [
            voxel_sum(error_term * record["scaled_second"])
            for error_term, record in zip(second_error, records)
        ]
    )
    total_g2, total_gx2 = lax.psum((local_g2, local_gx2), "dp")
    grad_reduced = jnp.zeros(reduced.shape, jnp.float32)
    for virtual, record in enumerate(records):
        d_pre = norm_back(
            second_error[virtual],
            record,
            "second",
            total_g2[virtual],
            total_gx2[virtual],
            voxel_count,
            frame_mask,
        )
        back_parts = lax.switch(
            record["kind"],
            [back_none, back_mid, back_small, back_none],
            reduced,
            record["act_first"],
            record["mid_kernel"],
            conv_small,
            d_pre.astype(jnp.bfloat16),
        )
        grad_reduced = grad_reduced + back_parts[0]
        record["back_small"] = back_parts[1]
        record["grad_mid"] = back_parts[2]
        record["grad_small"] = back_parts[3]
    own_reduced = lax.psum_scatter(grad_reduced, "branch", scatter_dimension=4, tiled=True)
    first_error = []
    for virtual, record in enumerate(records):
        branch_kind = record["kind"]
        direct = (
            jnp.where((branch_kind == 0) | (branch_kind == 3), slab_grads[virtual], 0.0)
            + record["back_small"]
        )
        incoming = jnp.concatenate(
            [direct, own_reduced[..., SLOT_RED * virtual : SLOT_RED * virtual + SLOT_RED]], axis=-1
        )
        first_error.append(
            incoming * silu_slope(record["shifted_first"]) * frame_mask * record["lane_first"]
        )
    local_g1 = jnp.stack([voxel_sum(error_term) for error_term in first_error])
    local_gx1 = jnp.stack(
        [
            voxel_sum(error_term * record["scaled_first"])
            for error_term, record in zip(first_error, records)
        ]
    )
    total_g1, total_gx1 = lax.psum((local_g1, local_gx1), "dp")
    channels = inputs.shape[-1]
    zero_index = jnp.zeros((), jnp.int32)
    grad_point = jnp.zeros((channels, SQUEEZED + LANE), jnp.float32)
    grad_mid = jnp.zeros(conv_mid.shape, jnp.float32)
    grad_small = jnp.zeros(conv_small.shape, jnp.float32)
    grad_gain = jnp.zeros((NORMED + LANE,), jnp.float32)
    grad_shift = jnp.zeros((NORMED + LANE,), jnp.float32)
    input_back = jnp.zeros(inputs.shape, jnp.float32)
    dz_mains = []
    dz_reduces = []
    for virtual, record in enumerate(records):
        branch_kind = record["kind"]
        d_pre = norm_back(
            first_error[virtual],
            record,
            "first",
            total_g1[virtual],
            total_gx1[virtual],
            voxel_count,
            frame_mask,
        )
        dz_main = lax.cond(
            branch_kind == 3, pool_adjoint, keep_same, d_pre[..., :LANE], frame_mask
        ).astype(jnp.bfloat16)
        dz_reduce = d_pre[..., LANE:].astype(jnp.bfloat16)
        dz_mains.append(dz_main)
        dz_reduces.append(dz_reduce)
        main_grad = lax.cond(branch_kind == 1, zero_product, input_product, inputs, dz_main)
        grad_point = (
            grad_point
            + lax.dynamic_update_slice(
                jnp.zeros((channels, SQUEEZED + LANE), jnp.float32),
                main_grad,
                (zero_index, record["column"]),
            )
            + lax.dynamic_update_slice(
                jnp.zeros((channels, SQUEEZED + LANE), jnp.float32),
                input_product(inputs, dz_reduce),
                (zero_index, record["reduce_start"]),
            )
        )
        grad_mid = grad_mid + lax.dynamic_update_slice(
            jnp.zeros(conv_mid.shape, jnp.float32),
            record["grad_mid"],
            (zero_index, zero_index, record["mid_start"]),
        )
        grad_small = grad_small + record["grad_small"]
        grad_gain = (
            grad_gain
            + place_vector(local_gx1[virtual][:LANE], record["column"])
            + place_vector(local_gx1[virtual][LANE:], record["reduce_start"])
            + place_vector(local_gx2[virtual], record["offset"])
        )
        grad_shift = (
            grad_shift
            + place_vector(local_g1[virtual][:LANE], record["column"])
            + place_vector(local_g1[virtual][LANE:], record["reduce_start"])
            + place_vector(local_g2[virtual], record["offset"])
        )
        input_back = (
            input_back
            + lax.cond(branch_kind == 1, zero_back, weight_back, dz_main, record["main_weights"])
            + weight_back(dz_reduce, record["reduce_weights"])
        )
    input_back = input_back * frame_mask
    return (
        input_back,
        dz_mains,
        dz_reduces,
        (grad_point[:, :SQUEEZED], grad_mid, grad_small, grad_gain[:NORMED], grad_shift[:NORMED]),
    )


def on_device(frames, lengths, cotangent, pointwise, conv_mid, conv_small, gains, shifts):
    (
        kind_list,
        main_columns,
        main_widths,
        second_offsets,
        second_widths,
        slab_offsets,
        slab_widths,
    ) = slot_tables()
    branches = lax.axis_size("branch")
    hosted = 8 // branches
    branch_index = lax.axis_index("branch")
    frame_count = frames.shape[1]
    frame_ids = jnp.arange(frame_count, dtype=jnp.int32)
    mask_first = (frame_ids[None, :] < lengths[:, None]).astype(jnp.float32)[:, :, None, None, None]
    mask_second = (frame_ids[None, : frame_count // 2] < (lengths // 2)[:, None]).astype(
        jnp.float32
    )[:, :, None, None, None]
    masked = frames * mask_first.astype(jnp.bfloat16)
    inputs = lax.all_gather(masked, "branch", axis=4, tiled=True)
    weights_first = (pointwise[0], conv_mid[0], conv_small[0], gains[0], shifts[0])
    weights_second = (pointwise[1], conv_mid[1], conv_small[1], gains[1], shifts[1])
    hidden, saved_first = forward_block(inputs, mask_first, weights_first, branch_index, hosted)
    clip_count, full_frames, full_side = (hidden.shape[0], hidden.shape[1], hidden.shape[2])
    channels = hidden.shape[-1]
    grouped = hidden.astype(jnp.float32).reshape(
        clip_count, full_frames // 2, 2, full_side // 2, 2, full_side // 2, 2, channels
    )
    pooled = jnp.mean(grouped, axis=(2, 4, 6)).astype(jnp.bfloat16)
    output, saved_second = forward_block(pooled, mask_second, weights_second, branch_index, hosted)
    lane_ids = jnp.arange(LANE, dtype=jnp.int32)
    wide_cotangent = jnp.pad(cotangent, ((0, 0),) * 4 + ((0, LANE),))
    slab_grads = []
    for virtual in range(hosted):
        virtual_slot = branch_index * hosted + virtual
        piece = lax.dynamic_slice_in_dim(
            wide_cotangent, pick_entry(slab_offsets, virtual_slot), LANE, 4
        ).astype(jnp.float32)
        slab_grads.append(
            piece * (lane_ids < pick_entry(slab_widths, virtual_slot)).astype(jnp.float32)
        )
    dx_second, unused_mains, unused_reduces, grads_second = backward_block(
        pooled, mask_second, weights_second, saved_second, slab_grads
    )
    spread = jnp.concatenate(
        [
            pad_lanes(dx_second[..., slab_start : slab_start + slab_width], LANE)
            for slab_start, slab_width in zip(slab_offsets, slab_widths)
        ],
        axis=-1,
    )
    own_slabs = lax.psum_scatter(spread, "branch", scatter_dimension=4, tiled=True)
    half_frames, half_side, slab_lanes = (
        own_slabs.shape[1],
        own_slabs.shape[2],
        own_slabs.shape[-1],
    )
    expanded = jnp.broadcast_to(
        own_slabs[:, :, None, :, None, :, None, :],
        (clip_count, half_frames, 2, half_side, 2, half_side, 2, slab_lanes),
    )
    upsampled = (
        expanded.reshape(clip_count, 2 * half_frames, 2 * half_side, 2 * half_side, slab_lanes)
        * 0.125
    )
    slab_first = [
        upsampled[..., LANE * virtual : LANE * virtual + LANE] for virtual in range(hosted)
    ]
    dx_full, unused_mains, unused_reduces, grads_first = backward_block(
        inputs, mask_first, weights_first, saved_first, slab_first
    )
    dx_first = lax.psum_scatter(dx_full, "branch", scatter_dimension=4, tiled=True)
    input_grad = dx_first.astype(jnp.bfloat16)
    grad_list = [jnp.stack([grads_first[number], grads_second[number]]) for number in range(5)]
    shapes = [grad_item.shape for grad_item in grad_list]
    groups = lax.axis_size("dp") * lax.axis_size("branch")
    flat = flat_join(grad_list, groups)
    share = lax.psum_scatter(flat, ("dp", "branch"), scatter_dimension=0, tiled=True)
    whole_flat = lax.all_gather(share, ("dp", "branch"), axis=0, tiled=True)
    summed = flat_split(whole_flat, shapes)
    return (output, input_grad, summed[0], summed[1], summed[2], summed[3], summed[4])


def solution(mesh):
    return jax.shard_map(
        on_device,
        mesh=mesh,
        in_specs=(
            P("dp", None, None, None, "branch"),
            P("dp"),
            P("dp", None, None, None, None),
            P(),
            P(),
            P(),
            P(),
            P(),
        ),
        out_specs=(
            P("dp", None, None, None, None),
            P("dp", None, None, None, "branch"),
            P(),
            P(),
            P(),
            P(),
            P(),
        ),
        check_vma=False,
    )
```

profile of v0, /device:TPU:0, one launch (start us, length us, event | category | flops | bytes accessed | tf_op | source)
XLA Modules:
  0.0 3157.0 jit_solution(12114974036380149063)
XLA Ops:
  9.5 9.4 copy.209
  55.4 759.6 %all-gather.5.cloned.1.call-done = bf16[1,16,14,14,832]{3,1,2,0,4:T(8,128)(2,1)} async-done(((bf16[1,16,14,14,208]{3,1,2,0,4:T(8,128)(2,1)}), bf16[1,16,14,14,832]{3,1,2,0,4:T(8,128)(2,1)}) %all-gather.5.cloned.1.call-update) | async-done | bytes 5218320 | tf_op jit(solution)/shard_map/all_gather | solution.py:549
  815.0 48.3 %copy.214 = bf16[1,16,14,14,832]{4,1,3,2,0:T(8,128)(2,1)} copy(bf16[1,16,14,14,832]{3,1,2,0,4:T(8,128)(2,1)} %all-gather.5.cloned.1.call-done) | data formatting | bytes 10436608 | tf_op jit(solution)/shard_map/all_gather | solution.py:549
  870.9 62.9 %conditional.25 = (f32[1,16,14,14,128]{4,1,3,2,0:T(8,128)}) conditional(s32[]{:T(128)} %clamp.10, (bf16[1,16,14,14,832]{3,1,2,0,4:T(8,128)(2,1)}, bf16[832,128]{1,0:T(8,128)(2,1)}) %tuple.285, () %tuple.286, (bf16[1,16,14,14,832]{3,1,2,0,4:T(8,128)(2,1)}, bf16[832,128]{1,0:T(8,128)(2,1)}) %tuple.285, ...), branch_computations={%region_13.14_spmd, %region_14.15_spmd, %region_15.16_spmd, %regio... | conditional | flops 670768448 | bytes 27182792 | solution.py:296
  870.9 48.8 %copy.216 = bf16[1,16,14,14,832]{4,1,3,2,0:T(8,128)(2,1)} copy(bf16[1,16,14,14,832]{3,1,2,0,4:T(8,128)(2,1)} %get-tuple-element.635) | data formatting | bytes 10436608 | tf_op jit(solution)/shard_map
  933.9 53.6 %conditional.24 = (f32[1,16,14,14,128]{4,1,3,2,0:T(8,128)}) conditional(s32[]{:T(128)} %clamp.8, (bf16[1,16,14,14,832]{3,1,2,0,4:T(8,128)(2,1)}, bf16[832,128]{1,0:T(8,128)(2,1)}) %tuple.282, () %tuple.283, (bf16[1,16,14,14,832]{3,1,2,0,4:T(8,128)(2,1)}, bf16[832,128]{1,0:T(8,128)(2,1)}) %tuple.282, ...), branch_computations={%region_6.7_spmd, %region_7.8_spmd, %region_8.9_spmd, %region_9.10... | conditional | flops 670768448 | bytes 27182792 | solution.py:296
  933.9 48.2 %copy.211 = bf16[1,16,14,14,832]{4,1,3,2,0:T(8,128)(2,1)} copy(bf16[1,16,14,14,832]{3,1,2,0,4:T(8,128)(2,1)} %get-tuple-element.628) | data formatting | bytes 10436608 | tf_op jit(solution)/shard_map
  990.4 14.6 all-reduce.104
  1016.2 148.6 %all_gather.19 = bf16[1,16,14,14,160]{3,1,2,0,4:T(8,128)(2,1)} all-gather(bf16[1,16,14,14,40]{3,1,2,0,4:T(8,128)(2,1)S(1)} %copy.220), channel_id=1, replica_groups=mesh['dp'=8,'branch'=4] {'branch'}, dimensions={4}, use_global_device_ids=true | all-gather | bytes 1254400 | tf_op jit(solution)/shard_map/all_gather | solution.py:340
  1164.8 20.2 conditional.27
  1185.0 17.3 conditional.26
  1202.9 20.4 all-reduce.103
  1249.4 208.0 %all-gather.7.cloned.1.call-done = bf16[1,16,14,14,1024]{4,1,3,2,0:T(8,128)(2,1)} async-done(((bf16[1,16,14,14,256]{4,1,3,2,0:T(8,128)(2,1)}), bf16[1,16,14,14,1024]{4,1,3,2,0:T(8,128)(2,1)}) %all-gather.7.cloned.1.call-update) | async-done | bytes 6422544 | tf_op jit(solution)/shard_map/all_gather | solution.py:379
  1476.1 30.9 concatenate.366
  1507.0 45.9 %convert_reduce_fusion = f32[8,7,7,832]{3,0,2,1:T(8,128)S(1)} fusion(bf16[1,8,2,7,2,7,2,832]{7,2,1,6,5,4,3,0:T(2,128)(2,1)} %concatenate.366), kind=kLoop, calls=%fused_computation.4253 | loop fusion | flops 4892160 | bytes 6522880 | tf_op jit(solution)/shard_map/reduce_sum | solution.py:558
  1558.2 14.6 all-reduce.102
  1577.7 39.6 %all_gather.21 = bf16[1,8,7,7,160]{3,1,2,0,4:T(8,128)(2,1)S(1)} all-gather(bf16[1,8,7,7,40]{3,1,2,0,4:T(8,128)(2,1)} %copy.226), channel_id=1, replica_groups=mesh['dp'=8,'branch'=4] {'branch'}, dimensions={4}, use_global_device_ids=true | all-gather | bytes 156800 | tf_op jit(solution)/shard_map/all_gather | solution.py:340
  1623.9 12.7 all-reduce.101
  1640.3 11.8 all-reduce.100
  1662.2 15.5 conditional.32
  1692.4 10.7 dynamic_update_slice.137
  1707.4 10.6 add.3250
  1721.1 47.1 %reduce-scatter.11.cloned.1.call-done = f32[40,392]{1,0:T(8,128)} async-done(((f32[160,392]{1,0:T(8,128)}), f32[40,392]{1,0:T(8,128)}) %reduce-scatter.11.cloned.1.call-update) | async-done | bytes 62736
  1774.5 12.0 all-reduce.99
  1814.9 35.0 %reduce-scatter.9.cloned.1.call-done = f32[1,8,7,7,256]{4,1,3,2,0:T(8,128)} async-done(((f32[1,8,7,7,1024]{4,1,3,2,0:T(8,128)}), f32[1,8,7,7,256]{4,1,3,2,0:T(8,128)}) %reduce-scatter.9.cloned.1.call-update) | async-done | bytes 401424 | tf_op jit(solution)/shard_map/reduce_scatter | solution.py:581
  1864.4 13.4 all-reduce.98
  1884.6 27.7 conditional.39
  1912.4 27.4 conditional.38
  1951.8 10.5 dynamic_update_slice.134
  1965.9 10.5 add.3249
  1976.4 10.7 pad_maximum_fusion
  1987.0 14.7 reshape.5082
  2008.7 325.5 %all-reduce.108.cloned.1.call-done = f32[1,16,14,14,160]{4,1,3,2,0:T(8,128)} async-done(((f32[1,16,14,14,160]{4,1,3,2,0:T(8,128)}), f32[1,16,14,14,160]{4,1,3,2,0:T(8,128)}) %all-reduce.108.cloned.1.call-update) | async-done | bytes 2007056
  2345.0 13.6 all-reduce.97
  2372.1 52.1 %conditional.44 = (f32[832,128]{0,1:T(8,128)S(1)}) conditional(s32[]{:T(128)} %convert_element_type.404, (bf16[1,16,14,14,832]{3,1,2,0,4:T(8,128)(2,1)}, bf16[1,16,14,14,128]{4,1,3,2,0:T(8,128)(2,1)}) %tuple.336, () %tuple.337), branch_computations={%region_145.146_spmd, %region_146.147_spmd} | conditional | flops 667942912 | bytes 16883720 | solution.py:483
  2372.1 48.2 %copy.249 = bf16[1,16,14,14,832]{4,1,3,2,0:T(8,128)(2,1)} copy(bf16[1,16,14,14,832]{3,1,2,0,4:T(8,128)(2,1)} %get-tuple-element.670) | data formatting | bytes 10436608 | tf_op jit(solution)/shard_map
  2439.2 52.3 %conditional.45 = (f32[832,128]{0,1:T(8,128)S(1)}) conditional(s32[]{:T(128)} %convert_element_type.415, (bf16[1,16,14,14,832]{3,1,2,0,4:T(8,128)(2,1)}, bf16[1,16,14,14,128]{4,1,3,2,0:T(8,128)(2,1)}) %tuple.338, () %tuple.339), branch_computations={%region_147.148_spmd, %region_148.149_spmd} | conditional | flops 667942912 | bytes 16883720 | solution.py:483
  2439.2 48.2 %copy.251 = bf16[1,16,14,14,832]{4,1,3,2,0:T(8,128)(2,1)} copy(bf16[1,16,14,14,832]{3,1,2,0,4:T(8,128)(2,1)} %get-tuple-element.672) | data formatting | bytes 10436608 | tf_op jit(solution)/shard_map
  2554.2 17.1 fusion.4010
  2571.3 50.0 %copy.937 = f32[1,16,14,14,832]{1,3,2,0,4:T(8,128)} copy(f32[1,16,14,14,832]{4,1,3,2,0:T(8,128)} %fusion.4010) | data formatting | bytes 20873216
  2621.3 55.0 %reshape.5771 = f32[832,3136]{1,0:T(8,128)} reshape(f32[832,1,14,14,16]{4,3,2,1,0:T(8,128)} %bitcast.2860) | data formatting | bytes 20873216
  2676.6 122.2 %all-reduce.110.cloned.1.call-done = f32[3948544]{0:T(1024)} async-done(((f32[3948544]{0:T(1024)}), f32[3948544]{0:T(1024)}) %all-reduce.110.cloned.1.call-update) | async-done | bytes 15794192
  2801.6 26.8 all_gather.22
  2830.7 160.2 %reduce-scatter.13.cloned.1.call-done = f32[208,3136]{1,0:T(8,128)} async-done(((f32[832,3136]{1,0:T(8,128)}), f32[208,3136]{1,0:T(8,128)}) %reduce-scatter.13.cloned.1.call-update) | async-done | bytes 2609168
  2990.9 14.7 reshape.5772
  3005.6 11.5 copy.938
  3017.1 89.9 %all-gather.9.cloned.1.call-done = f32[32,1,123392]{2,1,0:T(1,128)} async-done(((f32[1,1,123392]{2,1,0:T(1,128)}), f32[32,1,123392]{2,1,0:T(1,128)}) %all-gather.9.cloned.1.call-update) | async-done | bytes 15794192 | tf_op jit(solution)/shard_map/all_gather | solution.py:608
  3123.3 14.5 reshape.5087
  (677 shorter events, 408.2 us)
Async XLA Ops:
  7.2 807.8 %all-gather.5.cloned.1.call-start = ((), (), s32[]{:S(2)}) async-start(), calls=%async_computation.3 | async-start | bytes 59637760 | tf_op jit(solution)/shard_map/all_gather | solution.py:549
  18.9 1438.5 %all-gather.7.cloned.1.call-start = ((), (), s32[]{:S(2)}) async-start(), calls=%async_computation.4 | async-start | bytes 8028160 | tf_op jit(solution)/shard_map/all_gather | solution.py:379
  33.5 829.8 %copy-start.37 = (bf16[1,832,576]{2,1,0:T(8,128)(2,1)}, bf16[1,832,576]{2,1,0:T(8,128)(2,1)S(1)}, u32[]{:S(2)}) copy-start(bf16[1,832,576]{2,1,0:T(8,128)(2,1)S(1)} %copy.971) | copy-start | bytes 2875396
  38.9 895.0 %copy-start.205 = (f32[1,16,1,1,1]{1,4,3,2,0:T(1,128)}, f32[1,16,1,1,1]{1,4,3,2,0:T(1,128)S(1)}, u32[]{:S(2)}) copy-start(f32[1,16,1,1,1]{1,4,3,2,0:T(1,128)S(1)} %compare_convert_fusion.6) | copy-start | bytes 196
  38.9 1839.0 %copy-start.89 = (f32[16]{0:T(128)}, f32[16]{0:T(128)S(1)}, u32[]{:S(2)}) copy-start(f32[16]{0:T(128)S(1)} %compare_convert_fusion.7) | copy-start | bytes 196
  43.3 964.2 %copy-start.107 = (f32[148]{0:T(256)}, f32[148]{0:T(256)S(1)}, u32[]{:S(2)}) copy-start(f32[148]{0:T(256)S(1)} %pad_convert_fusion) | copy-start | bytes 1780
  43.4 964.1 %copy-start.110 = (f32[148]{0:T(256)}, f32[148]{0:T(256)S(1)}, u32[]{:S(2)}) copy-start(f32[148]{0:T(256)S(1)} %pad_convert_fusion.1) | copy-start | bytes 1780
  44.9 962.7 %copy-start.115 = (f32[148]{0:T(256)}, f32[148]{0:T(256)S(1)}, u32[]{:S(2)}) copy-start(f32[148]{0:T(256)S(1)} %pad_maximum_fusion.23) | copy-start | bytes 1780
  44.9 962.6 %copy-start.117 = (f32[148]{0:T(256)}, f32[148]{0:T(256)S(1)}, u32[]{:S(2)}) copy-start(f32[148]{0:T(256)S(1)} %pad_maximum_fusion.21) | copy-start | bytes 1780
  55.4 1129.5 %copy-start.44 = (bf16[27,32,128]{2,1,0:T(8,128)(2,1)}, bf16[27,32,128]{2,1,0:T(8,128)(2,1)S(1)}, u32[]{:S(2)}) copy-start(bf16[27,32,128]{2,1,0:T(8,128)(2,1)S(1)} %get-tuple-element.831) | copy-start | bytes 663556
  867.8 139.7 %copy-start.2 = (f32[1,16,14,14,20]{4,1,3,2,0:T(8,128)}, f32[1,16,14,14,20]{4,1,3,2,0:T(8,128)S(1)}, u32[]{:S(2)}) copy-start(f32[1,16,14,14,20]{4,1,3,2,0:T(8,128)S(1)} %fusion.4027) | copy-start | bytes 752644
  870.9 136.6 %copy-start.4 = (f32[1,16,14,14,20]{4,1,3,2,0:T(8,128)}, f32[1,16,14,14,20]{4,1,3,2,0:T(8,128)S(1)}, u32[]{:S(2)}) copy-start(f32[1,16,14,14,20]{4,1,3,2,0:T(8,128)S(1)} %fusion.4024) | copy-start | bytes 752644
  1185.0 39.7 %copy-start.8 = (f32[1,16,14,14,128]{4,1,3,2,0:T(8,128)}, f32[1,16,14,14,128]{4,1,3,2,0:T(8,128)S(1)}, u32[]{:S(2)}) copy-start(f32[1,16,14,14,128]{4,1,3,2,0:T(8,128)S(1)} %get-tuple-element.1001) | copy-start | bytes 4816900
  1202.3 22.4 copy-start.10
  1202.3 22.4 copy-start.129
  1202.3 22.4 copy-start.133
  1229.1 539.1 %reduce-scatter.11.cloned.1.call-start = ((), (), s32[]{:S(2)}) async-start(), calls=%async_computation.7 | async-start | bytes 409600
  1238.5 556.5 %copy-start.87 = (f32[8]{0:T(128)}, f32[8]{0:T(128)S(1)}, u32[]{:S(2)}) copy-start(f32[8]{0:T(128)S(1)} %get-tuple-element.794) | copy-start | bytes 100
  1247.3 309.2 %copy-start.47 = (bf16[832,128]{1,0:T(8,128)(2,1)}, bf16[832,128]{1,0:T(8,128)(2,1)S(1)}, u32[]{:S(2)}) copy-start(bf16[832,128]{1,0:T(8,128)(2,1)S(1)} %get-tuple-element.821) | copy-start | bytes 638980
  1575.3 42.0 %copy-start.113 = (f32[148]{0:T(256)}, f32[148]{0:T(256)S(1)}, u32[]{:S(2)}) copy-start(f32[148]{0:T(256)S(1)} %get-tuple-element.894) | copy-start | bytes 1780
  1576.4 40.8 %copy-start.46 = (bf16[27,32,128]{2,1,0:T(8,128)(2,1)S(1)}, bf16[27,32,128]{2,1,0:T(8,128)(2,1)}, u32[]{:S(2)}) copy-start(bf16[27,32,128]{2,1,0:T(8,128)(2,1)} %get-tuple-element.830) | copy-start | bytes 663556
  1688.9 161.0 %reduce-scatter.9.cloned.1.call-start = ((), (), s32[]{:S(2)}) async-start(), calls=%async_computation.5 | async-start | bytes 2007040 | tf_op jit(solution)/shard_map/reduce_scatter | solution.py:581
  1799.0 535.2 %all-reduce.108.cloned.1.call-start = ((), (), s32[]{:S(2)}) async-start(), calls=%async_computation.9 | async-start | bytes 6422528
  1945.2 853.6 %all-reduce.110.cloned.1.call-start = ((), (), s32[]{:S(2)}) async-start(), calls=%async_computation.10 | async-start | bytes 31588352
  2008.7 329.4 %copy-start.5 = (f32[1,16,14,14,20]{4,1,3,2,0:T(8,128)S(1)}, f32[1,16,14,14,20]{4,1,3,2,0:T(8,128)}, u32[]{:S(2)}) copy-start(f32[1,16,14,14,20]{4,1,3,2,0:T(8,128)} %copy-done.4) | copy-start | bytes 752644
  2008.7 329.4 %copy-start.90 = (f32[16]{0:T(128)S(1)}, f32[16]{0:T(128)}, u32[]{:S(2)}) copy-start(f32[16]{0:T(128)} %copy-done.89) | copy-start | bytes 196
  2008.7 329.4 %copy-start.96 = (f32[1,148]{1,0:T(1,128)S(1)}, f32[1,148]{1,0:T(1,128)}, u32[]{:S(2)}) copy-start(f32[1,148]{1,0:T(1,128)} %copy-done.95) | copy-start | bytes 1780
  2008.7 329.5 %copy-start.106 = (f32[148]{0:T(256)S(1)}, f32[148]{0:T(256)}, u32[]{:S(2)}) copy-start(f32[148]{0:T(256)} %copy-done.105) | copy-start | bytes 1780
  2008.7 329.5 %copy-start.112 = (f32[148]{0:T(256)S(1)}, f32[148]{0:T(256)}, u32[]{:S(2)}) copy-start(f32[148]{0:T(256)} %copy-done.110) | copy-start | bytes 1780
  2008.7 329.5 %copy-start.118 = (f32[148]{0:T(256)S(1)}, f32[148]{0:T(256)}, u32[]{:S(2)}) copy-start(f32[148]{0:T(256)} %copy-done.117) | copy-start | bytes 1780
  2008.7 329.5 %copy-start.122 = (f32[148]{0:T(256)S(1)}, f32[148]{0:T(256)}, u32[]{:S(2)}) copy-start(f32[148]{0:T(256)} %copy-done.121) | copy-start | bytes 1780
  2532.1 458.8 %reduce-scatter.13.cloned.1.call-start = ((), (), s32[]{:S(2)}) async-start(), calls=%async_computation.8 | async-start | bytes 13312000
  2676.3 124.8 %copy-start.56 = (f32[1,8,7,7,128]{4,1,3,2,0:T(8,128)S(1)}, f32[1,8,7,7,128]{4,1,3,2,0:T(8,128)}, u32[]{:S(2)}) copy-start(f32[1,8,7,7,128]{4,1,3,2,0:T(8,128)} %copy-done.54) | copy-start | bytes 602116
  2676.4 124.8 %copy-start.57 = (f32[1,8,7,7,128]{4,1,3,2,0:T(8,128)S(1)}, f32[1,8,7,7,128]{4,1,3,2,0:T(8,128)}, u32[]{:S(2)}) copy-start(f32[1,8,7,7,128]{4,1,3,2,0:T(8,128)} %get-tuple-element.1004) | copy-start | bytes 602116
  2676.4 124.8 %copy-start.69 = (bf16[1,8,7,7,148]{4,1,3,2,0:T(8,128)(2,1)S(1)}, bf16[1,8,7,7,148]{4,1,3,2,0:T(8,128)(2,1)}, u32[]{:S(2)}) copy-start(bf16[1,8,7,7,148]{4,1,3,2,0:T(8,128)(2,1)} %copy-done.68) | copy-start | bytes 348100
  2676.4 124.8 %copy-start.73 = (bf16[1,8,7,7,148]{4,1,3,2,0:T(8,128)(2,1)S(1)}, bf16[1,8,7,7,148]{4,1,3,2,0:T(8,128)(2,1)}, u32[]{:S(2)}) copy-start(bf16[1,8,7,7,148]{4,1,3,2,0:T(8,128)(2,1)} %copy-done.72) | copy-start | bytes 348100
  2676.4 124.8 %copy-start.88 = (f32[8]{0:T(128)S(1)}, f32[8]{0:T(128)}, u32[]{:S(2)}) copy-start(f32[8]{0:T(128)} %copy-done.87) | copy-start | bytes 100
  2676.4 124.8 %copy-start.124 = (f32[128]{0:T(128)S(1)}, f32[128]{0:T(128)}, u32[]{:S(2)}) copy-start(f32[128]{0:T(128)} %copy-done.123) | copy-start | bytes 1540
  2676.4 124.8 %copy-start.126 = (f32[128]{0:T(128)S(1)}, f32[128]{0:T(128)}, u32[]{:S(2)}) copy-start(f32[128]{0:T(128)} %copy-done.125) | copy-start | bytes 1540
  2676.4 124.8 %copy-start.132 = (f32[128]{0:T(128)S(1)}, f32[128]{0:T(128)}, u32[]{:S(2)}) copy-start(f32[128]{0:T(128)} %compare_convert_fusion.3) | copy-start | bytes 1540
  2676.4 124.8 %copy-start.136 = (f32[128]{0:T(128)S(1)}, f32[128]{0:T(128)}, u32[]{:S(2)}) copy-start(f32[128]{0:T(128)} %compare_convert_fusion.4) | copy-start | bytes 1540
  2676.4 124.8 %copy-start.150 = (f32[128]{0:T(128)S(1)}, f32[128]{0:T(128)}, u32[]{:S(2)}) copy-start(f32[128]{0:T(128)} %copy-done.149) | copy-start | bytes 1540
  2676.4 124.8 %copy-start.152 = (f32[128]{0:T(128)S(1)}, f32[128]{0:T(128)}, u32[]{:S(2)}) copy-start(f32[128]{0:T(128)} %copy-done.151) | copy-start | bytes 1540
  2676.5 124.8 %copy-start.154 = (f32[128]{0:T(128)S(1)}, f32[128]{0:T(128)}, u32[]{:S(2)}) copy-start(f32[128]{0:T(128)} %get-tuple-element.844) | copy-start | bytes 1540
  2676.5 124.8 %copy-start.156 = (f32[128]{0:T(128)S(1)}, f32[128]{0:T(128)}, u32[]{:S(2)}) copy-start(f32[128]{0:T(128)} %get-tuple-element.846) | copy-start | bytes 1540
  2676.5 124.8 %copy-start.158 = (f32[128]{0:T(128)S(1)}, f32[128]{0:T(128)}, u32[]{:S(2)}) copy-start(f32[128]{0:T(128)} %copy-done.157) | copy-start | bytes 1540
  2676.5 124.8 %copy-start.160 = (f32[128]{0:T(128)S(1)}, f32[128]{0:T(128)}, u32[]{:S(2)}) copy-start(f32[128]{0:T(128)} %copy-done.159) | copy-start | bytes 1540
  2676.5 430.5 %all-gather.9.cloned.1.call-start = ((), (), s32[]{:S(2)}) async-start(), calls=%async_computation.6 | async-start | bytes 16287744 | tf_op jit(solution)/shard_map/all_gather | solution.py:608
  (149 other events, 1251.7 us)
Sparse Core Ops, SparseCore 0:
  19.0 795.9 all-gather.4
  1229.2 228.1 all-gather.6
  1689.0 79.1 reduce-scatter.10
  1799.1 50.6 reduce-scatter.8
  1945.3 388.8 all-reduce.107
  2532.2 266.5 all-reduce.109
  2801.8 189.0 reduce-scatter.12
  2994.9 112.1 all-gather.8
where the time goes:
time: 3180 us; the launch traced here: 3160 us
  waiting for transfers between devices  1750 us (55%)
  local copies, waits for them, and re-layouts  690 us (22%)
  blocking collectives  328 us (10%)
  other arithmetic  152 us (5%)
  loops' own time  111 us (3%)
  matrix products  86.9 us (3%)
  between operations  40.5 us (1%)
    all_gather x1, waiting for transfers between devices, on_device(): inputs = lax.all_gather(masked, 'branch', axis=4, tiled=True)  760 us
    unnamed x12, waiting for transfers between devices  655 us
    another operation x32, local copies, waits for them, and re-layouts  223 us
    all_gather x1, waiting for transfers between devices, forward_block(): lax.all_gather(shortened(jnp.concatenate(slab_list, axis=-1)), 'branch',...  208 us
    all_gather x2, blocking collectives, forward_block(): lax.all_gather(shortened(jnp.concatenate([record['act_first'][..., LANE:]...  188 us
    unnamed x402, local copies, waits for them, and re-layouts  186 us
    all_gather x1, waiting for transfers between devices, on_device(): whole_flat = lax.all_gather(share, ('dp', 'branch'), axis=0, tiled=True)  89.9 us
  transfers between devices with their start and end apart: 8, of which 8 were waited for; matrix products, arithmetic and copies ran while one was open for 10% of the time, Pallas kernels for 0%

commit v1 on v0

v1 whole, which is shorter than its diff:
```python
import functools

import jax
import jax.numpy as jnp
from jax import lax
from jax.experimental import pallas as pl
from jax.experimental.pallas import tpu as pltpu
from jax.sharding import PartitionSpec as P

DIRECT = 256
MID_IN = 160
MID_OUT = 320
SMALL_IN = 32
SMALL_OUT = 128
TAPS = 27
CHANNELS = 832
SQUEEZED = 576
PITCH = 16
REDUCED = 256
POOLED = 128
FIRST = 640
SECOND = 512
OUTER = 896
TAP_ROWS = 432
EPSILON = 1e-05
F32 = jnp.float32
BF16 = jnp.bfloat16
VMEM_BYTES = 58 * 2**20


def call(body, out_shape, scratch=(), scalars=0, flops=10**9):
    def run(*operands):
        specs = [
            pl.BlockSpec(memory_space=pltpu.SMEM if number < scalars else pltpu.VMEM)
            for number in range(len(operands))
        ]
        return pl.pallas_call(
            body,
            out_shape=out_shape,
            in_specs=specs,
            out_specs=jax.tree.map(lambda _: pl.BlockSpec(memory_space=pltpu.VMEM), out_shape),
            scratch_shapes=list(scratch),
            compiler_params=pltpu.CompilerParams(vmem_limit_bytes=VMEM_BYTES),
            cost_estimate=pl.CostEstimate(
                flops=flops, bytes_accessed=16 * 2**20, transcendentals=0
            ),
        )(*operands)

    return run


def shape(dims, dtype):
    return jax.ShapeDtypeStruct(tuple(dims), dtype)


def rows_at(start, size):
    return pl.ds(pl.multiple_of(start, 16), size)


def frame_flag(frame, length):
    return jnp.where(frame < length, 1.0, 0.0).astype(F32)


def row_geometry(side, width):
    row = lax.broadcasted_iota(jnp.int32, (side * PITCH, width), 0)
    column, line = (row & (PITCH - 1), row >> 4)
    valid = jnp.where(column < side, 1.0, 0.0)

    def near(place):
        return 3.0 - jnp.where(place == 0, 1.0, 0.0) - jnp.where(place == side - 1, 1.0, 0.0)

    return (valid, near(line) * near(column))


def plane_box(values):
    rows = values.shape[0]
    across = values + pltpu.roll(values, 1, 0) + pltpu.roll(values, rows - 1, 0)
    edge = jnp.zeros((PITCH, values.shape[1]), values.dtype)
    return (
        across
        + jnp.concatenate([across[PITCH:], edge], axis=0)
        + jnp.concatenate([edge, across[:-PITCH]], axis=0)
    )


def box_scale(frame, length, window):
    frames = frame_flag(frame, length) + frame_flag(frame + 1, length)
    frames = frames + jnp.where(frame > 0, frame_flag(frame - 1, length), 0.0)
    return 1.0 / jnp.maximum(frames * window, 1.0)


def sigmoid(value):
    return 0.5 * jnp.tanh(0.5 * value) + 0.5


def silu(value):
    return value * sigmoid(value)


def silu_slope(value):
    gate = sigmoid(value)
    return gate * (1.0 + value * (1.0 - gate))


def partial_sum(values):
    rows, width = values.shape
    return jnp.sum(values.reshape(rows // 8, 8, width), axis=0)


def moments(total, square, count):
    center = total / count
    return (center, lax.rsqrt(square / count - center * center + EPSILON))


def total_of(gathered):
    total = gathered[0]
    for number in range(1, gathered.shape[0]):
        total = total + gathered[number]
    return total


def pool_matrix(side, transposed):
    wide = 2 * side
    few, many = (side * PITCH, 2 * wide * PITCH)
    dims = (many, few) if transposed else (few, many)
    coarse = lax.broadcasted_iota(jnp.int32, dims, 1 if transposed else 0)
    fine = lax.broadcasted_iota(jnp.int32, dims, 0 if transposed else 1)
    fine = jnp.where(fine >= wide * PITCH, fine - wide * PITCH, fine)
    same = (
        ((fine >> 4) >> 1 == coarse >> 4)
        & ((fine & (PITCH - 1)) >> 1 == coarse & (PITCH - 1))
        & ((fine & (PITCH - 1)) < wide)
    )
    return jnp.where(same, 0.125, 0.0).astype(BF16)


class Grid:
    def __init__(self, frames, side):
        self.frames, self.side = (frames, side)
        self.frame_rows = side * PITCH
        self.rows = frames * self.frame_rows
        self.pitch = (side + 1) * PITCH
        self.lead = self.pitch + PITCH
        self.padded = (frames + 2) * self.pitch + 2 * PITCH
        self.group = 2 if side > 8 else 4


def zero_rows(ref):
    rows = ref.shape[0]
    step = 16
    while rows % (step * 2) == 0 and step < 256:
        step = step * 2

    @pl.loop(0, rows // step)
    def _(number):
        ref[rows_at(number * step, step), :] = jnp.zeros((step, ref.shape[1]), ref.dtype)


def store_taps(grid, taps_ref, frame, act):
    rows = grid.frame_rows
    at = rows_at(grid.lead + frame * grid.pitch, rows)
    taps_ref[at, 0:REDUCED] = pltpu.roll(act, 1, 0).astype(BF16)
    taps_ref[at, REDUCED : 2 * REDUCED] = act.astype(BF16)
    taps_ref[at, 2 * REDUCED : 3 * REDUCED] = pltpu.roll(act, rows - 1, 0).astype(BF16)


def convolve(grid, taps_ref, kernel_ref, acc_ref, e_ref, sums_ref, length, valid):
    group_rows = grid.group * grid.pitch
    sums_ref[...] = jnp.zeros_like(sums_ref)
    wide_valid = jnp.concatenate([valid] * (SECOND // 128), axis=1)

    @pl.loop(0, grid.frames // grid.group)
    def _(group):
        base = grid.lead + group * group_rows
        for tap in range(9):
            start = base + (tap // 3 - 1) * grid.pitch + (tap % 3 - 1) * PITCH
            part = jnp.dot(
                taps_ref[rows_at(start, group_rows), :], kernel_ref[tap], preferred_element_type=F32
            )
            acc_ref[...] = part if tap == 0 else acc_ref[...] + part
        for number in range(grid.group):
            frame = group * grid.group + number
            values = acc_ref[number * grid.pitch : number * grid.pitch + grid.frame_rows, :]
            e_ref[rows_at(frame * grid.frame_rows, grid.frame_rows), :] = values
            masked = values * (wide_valid * frame_flag(frame, length))
            sums_ref[0:8] += partial_sum(masked)
            sums_ref[8:16] += partial_sum(masked * values)


def write_sums(out_ref, sums_ref, lo, hi):
    for number in range(2):
        out_ref[number : number + 1, lo:hi] = jnp.sum(
            sums_ref[8 * number : 8 * number + 8], axis=0, keepdims=True
        )


def first_pointwise(grid, local, parts, count_ref, x_ref, p_ref, mid_ref, pool_ref, direct_ref, sums_ref, u_ref):
    rows = local * grid.frame_rows
    wide = 2 * grid.frame_rows
    count = count_ref[0]

    @pl.loop(0, local // 2)
    def _(pair):
        at = rows_at(pair * wide, wide)
        total = jnp.dot(x_ref[0, at, :], p_ref[0], preferred_element_type=F32)
        for part in range(1, parts):
            total = total + jnp.dot(x_ref[part, at, :], p_ref[part], preferred_element_type=F32)
        u_ref[at, :] = total

    def summed(pair, carry):
        values = u_ref[rows_at(pair * wide, wide), :]
        return (carry[0] + partial_sum(values), carry[1] + partial_sum(values * values))

    zero = jnp.zeros((8, FIRST), F32)
    total, square = lax.fori_loop(0, local // 2, summed, (zero, zero))
    total = jnp.sum(total, axis=0, keepdims=True)
    square = jnp.sum(square, axis=0, keepdims=True)
    sums_ref[0:1, :] = total[:, :SECOND]
    sums_ref[1:2, :] = square[:, :SECOND]
    sums_ref[2:3, :] = jnp.full((1, SECOND), count, F32)
    offset = (total / jnp.full((1, FIRST), jnp.maximum(count, 1.0), F32)).astype(BF16)
    wide_offset = offset.astype(F32)
    tail = jnp.broadcast_to(wide_offset, (PITCH, FIRST)).astype(BF16)
    places = ((direct_ref, 0, DIRECT), (mid_ref, DIRECT, 2 * DIRECT), (pool_ref, SECOND, FIRST))
    for ref, lo, hi in places:
        ref[rows : rows + PITCH, :] = tail[:, lo:hi]

    @pl.loop(0, local)
    def _(frame):
        at = rows_at(frame * grid.frame_rows, grid.frame_rows)
        for ref, lo, hi in places:
            ref[at, :] = (u_ref[at, lo:hi] - wide_offset[:, lo:hi]).astype(BF16)


def each_frame(grid, local, parts, place, refs, visit):
    rows = local * grid.frame_rows
    for step, ref in enumerate(refs):
        source = lax.rem(place - step + parts, parts)
        offset = ref[rows : rows + PITCH, :].astype(F32)[0:1]

        @pl.loop(0, local)
        def _(number):
            at = rows_at(number * grid.frame_rows, grid.frame_rows)
            visit(source * local + number, ref[at, :].astype(F32) + offset)


def first_convolve(grid, local, parts, length_ref, place_ref, *refs):
    mids, sums, (gain_ref, shift_ref, kernel_ref), rest = (
        refs[:parts],
        refs[parts : 2 * parts],
        refs[2 * parts : 2 * parts + 3],
        refs[2 * parts + 3 :],
    )
    h_ref, taps_ref, e_ref, out_sums_ref, moment_ref, acc_ref, sums_ref = rest
    length = length_ref[0]
    total = sums[0][...]
    for ref in sums[1:]:
        total = total + ref[...]
    count = total[2:3]
    center, inverse = moments(total[0:1], total[1:2], count)
    moment_ref[0:1, :] = center
    moment_ref[1:2, :] = inverse
    moment_ref[2:3, :] = count
    center, inverse = (center[:, DIRECT:SECOND], inverse[:, DIRECT:SECOND])
    valid, _ = row_geometry(grid.side, 128)
    wide_valid = jnp.concatenate([valid, valid], axis=1)
    zero_rows(taps_ref)

    def visit(frame, values):
        scaled = (values - center) * inverse
        h_ref[rows_at(frame * grid.frame_rows, grid.frame_rows), :] = scaled.astype(BF16)
        act = silu(gain_ref[...] * scaled + shift_ref[...])
        store_taps(grid, taps_ref, frame, act * (wide_valid * frame_flag(frame, length)))

    each_frame(grid, local, parts, place_ref[0], mids, visit)
    convolve(grid, taps_ref, kernel_ref, acc_ref, e_ref, sums_ref, length, valid)
    write_sums(out_sums_ref, sums_ref, 0, SECOND)


def pool_planes(grid, plane_ref, q_ref, lo, sums_ref, length, valid, window):
    rows = grid.frame_rows
    sums_ref[...] = jnp.zeros_like(sums_ref)

    @pl.loop(0, grid.frames)
    def _(frame):
        start = frame * rows
        values = (
            plane_ref[rows_at(start, rows), :]
            + plane_ref[rows_at(start + rows, rows), :]
            + plane_ref[rows_at(start + 2 * rows, rows), :]
        ) * box_scale(frame, length, window)
        q_ref[rows_at(start, rows), lo : lo + POOLED] = values
        masked = values * (valid * frame_flag(frame, length))
        sums_ref[0:8] += partial_sum(masked)
        sums_ref[8:16] += partial_sum(masked * values)


def first_pool(grid, local, parts, length_ref, place_ref, *refs):
    pools, (q_ref, out_sums_ref, plane_ref, sums_ref) = (refs[:parts], refs[parts:])
    length = length_ref[0]
    valid, window = row_geometry(grid.side, POOLED)
    rows = grid.frame_rows
    plane_ref[0:rows] = jnp.zeros((rows, POOLED), F32)
    plane_ref[grid.rows + rows : grid.rows + 2 * rows] = jnp.zeros((rows, POOLED), F32)

    def visit(frame, values):
        plane_ref[rows_at((frame + 1) * rows, rows), :] = plane_box(values)

    each_frame(grid, local, parts, place_ref[0], pools, visit)
    pool_planes(grid, plane_ref, q_ref, 0, sums_ref, length, valid, window)
    write_sums(out_sums_ref, sums_ref, 0, POOLED)


def outer_moments(first_moment, second_sums, pool_at):
    count = first_moment[2:3, 0:1]
    total = total_of(second_sums)
    center, inverse = moments(total[0:1], total[1:2], first_moment[2:3, 0:128][:, 0:1])
    return (center, inverse, count)


def first_output(grid, small, local, parts, length_ref, place_ref, *refs):
    directs, rest = (refs[:parts], refs[parts:])
    q_ref, e_ref, moment_ref, sums_ref, gain_ref, shift_ref, pooled_ref, h_ref, outer_ref = rest
    length = length_ref[0]
    valid, _ = row_geometry(grid.side, 128)
    wide_valid = jnp.concatenate([valid] * (OUTER // 128), axis=1)
    total = total_of(sums_ref)
    count = jnp.concatenate([moment_ref[2:3, 0:128]] * 7, axis=1)
    center, inverse = moments(total[0:1], total[1:2], count[:, :FIRST])
    center = jnp.concatenate([moment_ref[0:1, :DIRECT], center], axis=1)
    inverse = jnp.concatenate([moment_ref[1:2, :DIRECT], inverse], axis=1)
    outer_ref[0:1, :] = center
    outer_ref[1:2, :] = inverse
    outer_ref[2:3, :] = count
    matrix = pool_matrix(small.side, False)
    rows = grid.frame_rows
    local_rows = local * rows
    for step, ref in enumerate(directs):
        source = lax.rem(place_ref[0] - step + parts, parts)
        offset = ref[local_rows : local_rows + PITCH, :].astype(F32)[0:1]

        @pl.loop(0, local // 2)
        def _(pair):
            acts = []
            for number in range(2):
                frame = source * local + 2 * pair + number
                at = rows_at(frame * rows, rows)
                direct = ref[rows_at((2 * pair + number) * rows, rows), :].astype(F32) + offset
                values = jnp.concatenate([direct, e_ref[at, :], q_ref[at, :]], axis=1)
                scaled = (values - center) * inverse
                h_ref[at, :] = scaled.astype(BF16)
                act = silu(gain_ref[...] * scaled + shift_ref[...])
                acts.append((act * (wide_valid * frame_flag(frame, length))).astype(BF16))
            coarse = source * (local // 2) + pair
            pooled_ref[rows_at(coarse * small.frame_rows, small.frame_rows), :] = jnp.dot(
                matrix, jnp.concatenate(acts, axis=0), preferred_element_type=F32
            ).astype(BF16)


def second_pointwise(grid, length_ref, count_ref, x_ref, p_ref, q_ref, out_sums_ref, plane_ref, sums_ref, pool_sums_ref):
    length = length_ref[0]
    rows = grid.frame_rows
    wide = 2 * rows
    valid, window = row_geometry(grid.side, POOLED)
    sums_ref[...] = jnp.zeros_like(sums_ref)
    plane_ref[0:rows] = jnp.zeros((rows, POOLED), F32)
    plane_ref[grid.rows + rows : grid.rows + 2 * rows] = jnp.zeros((rows, POOLED), F32)

    @pl.loop(0, grid.frames // 2)
    def _(pair):
        at = rows_at(pair * wide, wide)
        values = jnp.dot(x_ref[at, :], p_ref[...], preferred_element_type=F32)
        q_ref[at, 0:SECOND] = values[:, :SECOND]
        sums_ref[0:8] += partial_sum(values[:, :SECOND])
        sums_ref[8:16] += partial_sum(values[:, :SECOND] * values[:, :SECOND])
        for number in range(2):
            plane_ref[rows_at((2 * pair + number + 1) * rows, rows), :] = plane_box(
                values[number * rows : (number + 1) * rows, SECOND:]
            )

    pool_planes(grid, plane_ref, q_ref, SECOND, pool_sums_ref, length, valid, window)
    write_sums(out_sums_ref, sums_ref, 0, SECOND)
    write_sums(out_sums_ref, pool_sums_ref, SECOND, FIRST)
    out_sums_ref[2:3, :] = jnp.full((1, FIRST), count_ref[0], F32)


def second_convolve(grid, length_ref, q_ref, sums_in_ref, gain_ref, shift_ref, kernel_ref, h_ref, taps_ref, e_ref, out_sums_ref, moment_ref, acc_ref, sums_ref):
    length = length_ref[0]
    total = total_of(sums_in_ref)
    count = total[2:3]
    center, inverse = moments(total[0:1], total[1:2], count)
    moment_ref[0:1, :] = center
    moment_ref[1:2, :] = inverse
    moment_ref[2:3, :] = count
    center, inverse = (center[:, DIRECT:SECOND], inverse[:, DIRECT:SECOND])
    valid, _ = row_geometry(grid.side, 128)
    wide_valid = jnp.concatenate([valid, valid], axis=1)
    zero_rows(taps_ref)

    @pl.loop(0, grid.frames)
    def _(frame):
        at = rows_at(frame * grid.frame_rows, grid.frame_rows)
        scaled = (q_ref[at, DIRECT:SECOND] - center) * inverse
        h_ref[at, :] = scaled.astype(BF16)
        act = silu(gain_ref[...] * scaled + shift_ref[...])
        store_taps(grid, taps_ref, frame, act * (wide_valid * frame_flag(frame, length)))

    convolve(grid, taps_ref, kernel_ref, acc_ref, e_ref, sums_ref, length, valid)
    write_sums(out_sums_ref, sums_ref, 0, SECOND)


def second_output(grid, length_ref, q_ref, e_ref, moment_ref, sums_in_ref, gain_ref, shift_ref, cot_ref, act_ref, h_ref, outer_ref, out_sums_ref, sums_ref):
    length = length_ref[0]
    valid, _ = row_geometry(grid.side, 128)
    wide_valid = jnp.concatenate([valid] * (OUTER // 128), axis=1)
    total = total_of(sums_in_ref)
    count = jnp.concatenate([moment_ref[2:3, 0:128]] * 7, axis=1)
    center, inverse = moments(total[0:1], total[1:2], count[:, :SECOND])
    center = jnp.concatenate([moment_ref[0:1, :DIRECT], center, moment_ref[0:1, SECOND:]], axis=1)
    inverse = jnp.concatenate([moment_ref[1:2, :DIRECT], inverse, moment_ref[1:2, SECOND:]], axis=1)
    outer_ref[0:1, :] = center
    outer_ref[1:2, :] = inverse
    outer_ref[2:3, :] = count
    sums_ref[...] = jnp.zeros_like(sums_ref)

    @pl.loop(0, grid.frames)
    def _(frame):
        at = rows_at(frame * grid.frame_rows, grid.frame_rows)
        values = jnp.concatenate([q_ref[at, :DIRECT], e_ref[at, :], q_ref[at, SECOND:]], axis=1)
        scaled = (values - center) * inverse
        h_ref[at, :] = scaled.astype(BF16)
        mask = wide_valid * frame_flag(frame, length)
        shifted = gain_ref[...] * scaled + shift_ref[...]
        gate = sigmoid(shifted)
        act_ref[at, :] = (shifted * gate * mask).astype(BF16)
        slope = gate * (1.0 + shifted * (1.0 - gate))
        error = cot_ref[at, :].astype(F32) * slope * mask
        sums_ref[0:8] += partial_sum(error)
        sums_ref[8:16] += partial_sum(error * scaled)

    write_sums(out_sums_ref, sums_ref, 0, OUTER)


def outer_gradient(grid, small, grad_ref, matrix, frame, lo, hi):
    if small is None:
        return grad_ref[rows_at(frame * grid.frame_rows, grid.frame_rows), lo:hi].astype(F32)
    coarse = grad_ref[rows_at((frame // 2) * small.frame_rows, small.frame_rows), lo:hi]
    return jnp.dot(matrix, coarse, preferred_element_type=F32)


def spread_matrix(grid, small):
    return None if small is None else pool_matrix(small.side, True)[: grid.frame_rows]


def first_outer_sums(grid, small, length_ref, h_ref, gain_ref, shift_ref, grad_ref, out_sums_ref, sums_ref):
    length = length_ref[0]
    valid, _ = row_geometry(grid.side, 128)
    wide_valid = jnp.concatenate([valid] * (OUTER // 128), axis=1)
    matrix = spread_matrix(grid, small)
    sums_ref[...] = jnp.zeros_like(sums_ref)

    @pl.loop(0, grid.frames)
    def _(frame):
        at = rows_at(frame * grid.frame_rows, grid.frame_rows)
        scaled = h_ref[at, :].astype(F32)
        slope = silu_slope(gain_ref[...] * scaled + shift_ref[...])
        grad = outer_gradient(grid, small, grad_ref, matrix, frame, 0, OUTER)
        error = grad * slope * (wide_valid * frame_flag(frame, length))
        sums_ref[0:8] += partial_sum(error)
        sums_ref[8:16] += partial_sum(error * scaled)

    write_sums(out_sums_ref, sums_ref, 0, OUTER)


def conv_back(grid, small, length_ref, h_ref, outer_ref, sums_in_ref, gain_ref, shift_ref, grad_ref, kernel_ref, reduced_ref, reduced_gain_ref, reduced_shift_ref, d_ref, r_ref, out_sums_ref, total_ref, acc_ref, sums_ref):
    length = length_ref[0]
    valid, _ = row_geometry(grid.side, 128)
    total = total_of(sums_in_ref)
    total_ref[...] = total
    lo, hi = (DIRECT, DIRECT + SECOND)
    count = outer_ref[2:3, lo:hi]
    mean_r = total[0:1, lo:hi] / count
    mean_rh = total[1:2, lo:hi] / count
    gain, shift = (gain_ref[:, lo:hi], shift_ref[:, lo:hi])
    factor = gain * outer_ref[1:2, lo:hi]
    wide_valid = jnp.concatenate([valid] * (SECOND // 128), axis=1)
    matrix = spread_matrix(grid, small)
    zero_rows(d_ref)

    @pl.loop(0, grid.frames)
    def _(frame):
        at = rows_at(frame * grid.frame_rows, grid.frame_rows)
        scaled = h_ref[at, lo:hi].astype(F32)
        grad = outer_gradient(grid, small, grad_ref, matrix, frame, lo, hi)
        error = grad * silu_slope(gain * scaled + shift)
        back = factor * (error - mean_r - scaled * mean_rh)
        d_ref[rows_at(grid.lead + frame * grid.pitch, grid.frame_rows), :] = (
            back * (wide_valid * frame_flag(frame, length))
        ).astype(BF16)

    group_rows = grid.group * grid.pitch
    sums_ref[...] = jnp.zeros_like(sums_ref)
    reduced_valid = jnp.concatenate([valid, valid], axis=1)

    @pl.loop(0, grid.frames // grid.group)
    def _(group):
        base = grid.lead + group * group_rows
        for tap in range(9):
            start = base - (tap // 3 - 1) * grid.pitch - (tap % 3 - 1) * PITCH
            part = lax.dot_general(
                d_ref[rows_at(start, group_rows), :],
                kernel_ref[tap],
                (((1,), (1,)), ((), ())),
                preferred_element_type=F32,
            )
            acc_ref[...] = part if tap == 0 else acc_ref[...] + part
        for number in range(grid.group):
            frame = group * grid.group + number
            rows = grid.frame_rows
            lines = slice(number * grid.pitch, number * grid.pitch + rows)
            back = (
                pltpu.roll(acc_ref[lines, 0:REDUCED], rows - 1, 0)
                + acc_ref[lines, REDUCED : 2 * REDUCED]
                + pltpu.roll(acc_ref[lines, 2 * REDUCED : 3 * REDUCED], 1, 0)
            )
            at = rows_at(frame * rows, rows)
            scaled = reduced_ref[at, :].astype(F32)
            slope = silu_slope(reduced_gain_ref[...] * scaled + reduced_shift_ref[...])
            error = back * slope * (reduced_valid * frame_flag(frame, length))
            r_ref[at, :] = error.astype(BF16)
            sums_ref[0:8] += partial_sum(error)
            sums_ref[8:16] += partial_sum(error * scaled)

    write_sums(out_sums_ref, sums_ref, 0, REDUCED)


def kernel_grads(grid, slots, first_ref, taps_ref, d_ref, out_ref, acc_ref):
    group_rows = grid.group * grid.pitch
    acc_ref[...] = jnp.zeros_like(acc_ref)

    @pl.loop(0, grid.frames // grid.group)
    def _(group):
        base = grid.lead + group * group_rows
        right = d_ref[rows_at(base, group_rows), :]
        for slot in range(slots):
            tap = jnp.minimum(first_ref[0] + slot, TAPS - 1)
            start = base + (tap // 9 - 1) * grid.pitch + (lax.rem(tap // 3, 3) - 1) * PITCH
            lanes = pl.ds(pl.multiple_of(lax.rem(tap, 3) * REDUCED, REDUCED), REDUCED)
            left = taps_ref[rows_at(start, group_rows), lanes]
            acc_ref[slot] += lax.dot_general(
                left, right, (((0,), (0,)), ((), ())), preferred_element_type=F32
            )

    for slot in range(slots):
        base = slot * TAP_ROWS
        for tile in range(2):
            out_ref[base + MID_IN * tile : base + MID_IN * (tile + 1), :] = acc_ref[
                slot, 0:MID_IN, 128 * tile : 128 * (tile + 1)
            ].astype(BF16)
        half = MID_IN // 2
        folded = acc_ref[slot, 0:half, 256:384] + pltpu.roll(
            acc_ref[slot, half:MID_IN, 256:384], 64, 1
        )
        base = base + 2 * MID_IN
        out_ref[base : base + half, :] = folded.astype(BF16)
        base = base + half
        out_ref[base : base + SMALL_IN, :] = acc_ref[
            slot, MID_IN : MID_IN + SMALL_IN, 384:512
        ].astype(BF16)
    used = slots * TAP_ROWS
    if out_ref.shape[0] > used:
        out_ref[used:, :] = jnp.zeros((out_ref.shape[0] - used, 128), BF16)


def point_back(grid, small, kept, length_ref, place_ref, h_ref, outer_ref, total_ref, gain_ref, shift_ref, grad_ref, reduced_ref, r_ref, moment_ref, sums_in_ref, reduced_gain_ref, x_ref, p_ref, dx_ref, dp_ref, reduced_total_ref, du_ref, plane_ref, acc_ref):
    length = length_ref[0]
    rows = grid.frame_rows
    valid, window = row_geometry(grid.side, 128)
    matrix = spread_matrix(grid, small)
    total = total_of(sums_in_ref)
    reduced_total_ref[...] = total
    count = outer_ref[2:3, 0:128]
    count = jnp.concatenate([count, count], axis=1)
    mid_r, mid_rh = (total[0:1] / count, total[1:2] / count)
    mid_factor = reduced_gain_ref[...] * moment_ref[1:2, DIRECT:SECOND]
    two = jnp.concatenate([valid, valid], axis=1)
    plane_ref[0:rows] = jnp.zeros((rows, POOLED), F32)
    plane_ref[grid.rows + rows : grid.rows + 2 * rows] = jnp.zeros((rows, POOLED), F32)

    def section(frame, lo, hi, mask):
        at = rows_at(frame * rows, rows)
        scaled = h_ref[at, lo:hi].astype(F32)
        gain, shift = (gain_ref[:, lo:hi], shift_ref[:, lo:hi])
        grad = outer_gradient(grid, small, grad_ref, matrix, frame, lo, hi)
        error = grad * silu_slope(gain * scaled + shift)
        size = outer_ref[2:3, lo:hi]
        inner = error - total_ref[0:1, lo:hi] / size - scaled * (total_ref[1:2, lo:hi] / size)
        return (gain * outer_ref[1:2, lo:hi]) * inner * mask

    @pl.loop(0, grid.frames)
    def _(frame):
        at = rows_at(frame * rows, rows)
        flag = frame_flag(frame, length)
        du_ref[at, 0:DIRECT] = section(frame, 0, DIRECT, two * flag).astype(BF16)
        scaled = reduced_ref[at, :].astype(F32)
        inner = r_ref[at, :].astype(F32) - mid_r - scaled * mid_rh
        du_ref[at, DIRECT:SECOND] = (mid_factor * inner * (two * flag)).astype(BF16)
        pool = section(frame, OUTER - POOLED, OUTER, valid * flag)
        plane_ref[rows_at((frame + 1) * rows, rows), :] = plane_box(
            pool * box_scale(frame, length, window)
        )

    wide = 2 * rows
    acc_ref[...] = jnp.zeros_like(acc_ref)

    @pl.loop(0, grid.frames // 2)
    def _(pair):
        start = pair * wide
        at = rows_at(start, wide)
        pool = (
            plane_ref[at, :]
            + plane_ref[rows_at(start + rows, wide), :]
            + plane_ref[rows_at(start + 2 * rows, wide), :]
        ) * jnp.concatenate([valid, valid], axis=0)
        du = jnp.concatenate([du_ref[at, 0:SECOND], pool.astype(BF16)], axis=1)
        dx_ref[at, :] = lax.dot_general(
            du, p_ref[...], (((1,), (1,)), ((), ())), preferred_element_type=F32
        ).astype(BF16)
        acc_ref[...] += lax.dot_general(
            x_ref[at, :], du, (((0,), (0,)), ((), ())), preferred_element_type=F32
        )

    first = pl.multiple_of(place_ref[0] * kept, 16) if kept < acc_ref.shape[0] else 0
    own = acc_ref[pl.ds(first, kept), :]
    for tile in range(FIRST // 128):
        dp_ref[kept * tile : kept * (tile + 1), :] = own[:, 128 * tile : 128 * (tile + 1)].astype(
            BF16
        )
    used = (FIRST // 128) * kept
    if dp_ref.shape[0] > used:
        dp_ref[used:, :] = jnp.zeros((dp_ref.shape[0] - used, 128), BF16)


def unpack_taps(first_ref, second_ref, mid_ref, small_ref):
    half = MID_IN // 2
    for number, ref in enumerate((first_ref, second_ref)):
        values = ref[0].astype(F32)
        folded = values[2 * MID_IN : 2 * MID_IN + half]
        mid_ref[number, 0, :, 0:128] = values[0:MID_IN]
        mid_ref[number, 0, :, 128:256] = values[MID_IN : 2 * MID_IN]
        mid_ref[number, 0, 0:half, 256:320] = folded[:, 0:64]
        mid_ref[number, 0, half:MID_IN, 256:320] = pltpu.roll(folded, 64, 1)[:, 0:64]
        small_ref[number, 0] = values[2 * MID_IN + half : TAP_ROWS]


def unpack_point(parts, first_ref, second_ref, out_ref):
    kept = CHANNELS // parts
    for part in range(parts):
        for tile in range(FIRST // 128):
            values = first_ref[part, kept * tile : kept * (tile + 1), :].astype(F32)
            at = slice(kept * part, kept * (part + 1))
            place_columns(out_ref, 0, at, tile, values)
    kept = OUTER // parts
    for part in range(parts):
        for tile in range(FIRST // 128):
            start = kept * part
            while start < kept * (part + 1):
                stop = kept * (part + 1)
                if start < SQUEEZED:
                    stop, moved = (min(stop, SQUEEZED), 0)
                elif start < FIRST:
                    start = min(stop, FIRST)
                    continue
                else:
                    moved = 64
                source = kept * tile + start - kept * part
                values = second_ref[part, source : source + stop - start, :].astype(F32)
                place_columns(out_ref, 1, slice(start - moved, stop - moved), tile, values)
                start = stop


def place_columns(out_ref, block, at, tile, values):
    if tile < 3:
        out_ref[block, at, 128 * tile : 128 * (tile + 1)] = values
    elif tile == 3:
        out_ref[block, at, 384:448] = values[:, 0:64]
    else:
        out_ref[block, at, 448:576] = values


def outer_vector(values):
    gap = jnp.zeros((64,), F32)
    return jnp.concatenate(
        [values[:256], values[576:896], gap, values[896:1024], values[448:576]]
    ).reshape(1, OUTER)


def reduced_vector(values):
    return jnp.pad(values[256:448], (0, 64)).reshape(1, REDUCED)


def norm_vector(outer, reduced):
    return jnp.concatenate(
        [outer[:256], reduced[:192], outer[768:896], outer[256:576], outer[640:768]]
    )


def wide_kernels(conv_mid, conv_small):
    mid = jnp.pad(conv_mid, ((0, 0), (0, 96), (0, 192)))
    small = jnp.pad(conv_small, ((0, 0), (160, 64), (384, 0)))
    return (mid + small).reshape(9, 3 * REDUCED, SECOND)


def point_columns(point):
    gap = jnp.zeros((point.shape[0], 64), point.dtype)
    return jnp.concatenate([point[:, :448], gap, point[:, 448:]], axis=1)


def round_up(value, unit):
    return -(-value // unit) * unit


def spread_over(values, axis, size):
    received = [values]
    for step in range(1, size):
        perm = [(source, (source + step) % size) for source in range(size)]
        received.append(lax.ppermute(values, axis, perm))
    return received


def after(values, earlier):
    return lax.optimization_barrier((values, earlier))[0]


def summed_everywhere(packed):
    share = lax.psum_scatter(packed, "dp", scatter_dimension=0, tiled=True)
    whole = lax.all_gather(share, ("branch", "dp"), axis=0, tiled=True)
    return whole.reshape(-1, packed.shape[0], 128)


def on_device(frames, lengths, cotangent, pointwise, conv_mid, conv_small, gains, shifts):
    parts = lax.axis_size("branch")
    clips = lax.axis_size("dp")
    place = lax.axis_index("branch").astype(jnp.int32)
    count_frames, side = (frames.shape[1], frames.shape[2])
    grid, small = (Grid(count_frames, side), Grid(count_frames // 2, side // 2))
    local = count_frames // parts
    own_channels = frames.shape[-1]
    length = lengths.astype(jnp.int32)
    half_length = length // 2
    place_one = place.reshape(1)

    ids = jnp.arange(count_frames, dtype=jnp.int32)
    mask = (ids < length[0]).astype(BF16)[:, None, None, None]
    own = jnp.pad(frames[0] * mask, ((0, 0), (0, 0), (0, PITCH - side), (0, 0)))
    own = own.reshape(grid.rows, own_channels)
    by_frames = lax.all_to_all(
        own.reshape(parts, local * grid.frame_rows, own_channels), "branch", 0, 0, tiled=True
    )

    columns = [point_columns(pointwise[0]), point_columns(pointwise[1])]
    point_first = columns[0].reshape(parts, own_channels, FIRST)
    point_own = lax.dynamic_slice_in_dim(columns[0], place * own_channels, own_channels, 0)
    point_second = jnp.concatenate(
        [columns[1][:576], jnp.zeros((64, FIRST), BF16), columns[1][576:]], axis=0
    )
    kernels = [wide_kernels(conv_mid[number], conv_small[number]) for number in range(2)]
    outer_gain = [outer_vector(gains[number]) for number in range(2)]
    outer_shift = [outer_vector(shifts[number]) for number in range(2)]
    reduced_gain = [reduced_vector(gains[number]) for number in range(2)]
    reduced_shift = [reduced_vector(shifts[number]) for number in range(2)]
    cot = cotangent[0]
    cot = jnp.concatenate(
        [cot[..., :576], jnp.zeros(cot.shape[:3] + (64,), BF16), cot[..., 576:]], axis=-1
    )
    cot = jnp.pad(cot, ((0, 0), (0, 0), (0, PITCH - small.side), (0, 0))).reshape(small.rows, OUTER)

    local_rows = local * grid.frame_rows
    valid_frames = jnp.clip(length - place * local, 0, local)
    local_count = valid_frames.astype(F32) * float(side * side)
    mid, pool, direct, sums = call(
        functools.partial(first_pointwise, grid, local, parts),
        (
            shape((local_rows + PITCH, REDUCED), BF16),
            shape((local_rows + PITCH, POOLED), BF16),
            shape((local_rows + PITCH, DIRECT), BF16),
            shape((3, SECOND), F32),
        ),
        [pltpu.VMEM((local_rows, FIRST), F32)],
        scalars=1,
    )(local_count, by_frames, point_first)
    mids = spread_over(mid, "branch", parts)
    sums = jnp.sum(lax.all_gather(sums, "dp"), axis=0)
    all_sums = spread_over(sums, "branch", parts)
    pools = spread_over(after(pool, mids), "branch", parts)
    directs = spread_over(after(direct, pools), "branch", parts)
    group_rows = grid.group * grid.pitch
    h_reduced, taps, e, e_sums, moment = call(
        functools.partial(first_convolve, grid, local, parts),
        (
            shape((grid.rows, REDUCED), BF16),
            shape((grid.padded, 3 * REDUCED), BF16),
            shape((grid.rows, SECOND), F32),
            shape((2, SECOND), F32),
            shape((3, SECOND), F32),
        ),
        [pltpu.VMEM((group_rows, SECOND), F32), pltpu.VMEM((16, SECOND), F32)],
        scalars=2,
        flops=2 * 10**10,
    )(length, place_one, *mids, *all_sums, reduced_gain[0], reduced_shift[0], kernels[0])
    q_pool, pool_sums = call(
        functools.partial(first_pool, grid, local, parts),
        (shape((grid.rows, POOLED), F32), shape((2, POOLED), F32)),
        [
            pltpu.VMEM((grid.rows + 2 * grid.frame_rows, POOLED), F32),
            pltpu.VMEM((16, POOLED), F32),
        ],
        scalars=2,
    )(length, place_one, *pools)
    second_sums = lax.all_gather(jnp.concatenate([e_sums, pool_sums], axis=1), "dp")
    pooled, h_outer, outer = call(
        functools.partial(first_output, grid, small, local, parts),
        (
            shape((small.rows, OUTER), BF16),
            shape((grid.rows, OUTER), BF16),
            shape((3, OUTER), F32),
        ),
        scalars=2,
    )(length, place_one, *directs, q_pool, e, moment, second_sums, outer_gain[0], outer_shift[0])

    small_count = half_length.astype(F32) * float(small.side * small.side)
    q_small, sums_small = call(
        functools.partial(second_pointwise, small),
        (shape((small.rows, FIRST), F32), shape((3, FIRST), F32)),
        [
            pltpu.VMEM((small.rows + 2 * small.frame_rows, POOLED), F32),
            pltpu.VMEM((16, SECOND), F32),
            pltpu.VMEM((16, POOLED), F32),
        ],
        scalars=2,
    )(half_length, small_count, pooled, point_second)
    sums_small = lax.all_gather(sums_small, "dp")
    small_group = small.group * small.pitch
    h_reduced_small, taps_small, e_small, e_sums_small, moment_small = call(
        functools.partial(second_convolve, small),
        (
            shape((small.rows, REDUCED), BF16),
            shape((small.padded, 3 * REDUCED), BF16),
            shape((small.rows, SECOND), F32),
            shape((2, SECOND), F32),
            shape((3, FIRST), F32),
        ),
        [pltpu.VMEM((small_group, SECOND), F32), pltpu.VMEM((16, SECOND), F32)],
        scalars=1,
    )(half_length, q_small, sums_small, reduced_gain[1], reduced_shift[1], kernels[1])
    e_sums_small = lax.all_gather(e_sums_small, "dp")
    act, h_outer_small, outer_small, outer_sums_small = call(
        functools.partial(second_output, small),
        (
            shape((small.rows, OUTER), BF16),
            shape((small.rows, OUTER), BF16),
            shape((3, OUTER), F32),
            shape((2, OUTER), F32),
        ),
        [pltpu.VMEM((16, OUTER), F32)],
        scalars=1,
    )(half_length, q_small, e_small, moment_small, e_sums_small, outer_gain[1], outer_shift[1], cot)

    slots = -(-TAPS // parts)
    tap_rows = round_up(slots * TAP_ROWS, 16 * clips)
    first_tap = place_one * slots

    def back(at, coarse, number, span, h_out, outer_moment, outer_sums, grad, h_red, taps_of, moment_of, x, point, kept):
        gathered = lax.all_gather(outer_sums, "dp")
        rows = at.group * at.pitch
        d_low, r_low, sums_low, total = call(
            functools.partial(conv_back, at, coarse),
            (
                shape((at.padded, SECOND), BF16),
                shape((at.rows, REDUCED), BF16),
                shape((2, REDUCED), F32),
                shape((2, OUTER), F32),
            ),
            [pltpu.VMEM((rows, 3 * REDUCED), F32), pltpu.VMEM((16, REDUCED), F32)],
            scalars=1,
            flops=2 * 10**10 if coarse is not None else 10**9,
        )(
            span,
            h_out,
            outer_moment,
            gathered,
            outer_gain[number],
            outer_shift[number],
            grad,
            kernels[number],
            h_red,
            reduced_gain[number],
            reduced_shift[number],
        )
        packed_taps = call(
            functools.partial(kernel_grads, at, slots),
            shape((tap_rows, 128), BF16),
            [pltpu.VMEM((slots, REDUCED, SECOND), F32)],
            scalars=1,
        )(first_tap, taps_of, d_low)
        gathered = lax.all_gather(sums_low, "dp")
        point_rows = round_up(kept * (FIRST // 128), 16 * clips)
        dx, packed_point, reduced_total = call(
            functools.partial(point_back, at, coarse, kept),
            (
                shape((at.rows, x.shape[1]), BF16),
                shape((point_rows, 128), BF16),
                shape((2, REDUCED), F32),
            ),
            [
                pltpu.VMEM((at.rows, SECOND), BF16),
                pltpu.VMEM((at.rows + 2 * at.frame_rows, POOLED), F32),
                pltpu.VMEM((x.shape[1], FIRST), F32),
            ],
            scalars=2,
        )(
            span,
            place_one,
            h_out,
            outer_moment,
            total,
            outer_gain[number],
            outer_shift[number],
            grad,
            h_red,
            r_low,
            moment_of,
            gathered,
            reduced_gain[number],
            x,
            point,
        )
        norms = [norm_vector(total[row], reduced_total[row]) for row in range(2)]
        return (dx, packed_taps, packed_point, norms)

    dx_small, taps_packed_small, point_packed_small, norms_small = back(
        small, None, 1, half_length, h_outer_small, outer_small, outer_sums_small, cot,
        h_reduced_small, taps_small, moment_small, pooled, point_second, OUTER // parts,
    )
    outer_sums = call(
        functools.partial(first_outer_sums, grid, small),
        shape((2, OUTER), F32),
        [pltpu.VMEM((16, OUTER), F32)],
        scalars=1,
    )(length, h_outer, outer_gain[0], outer_shift[0], dx_small)
    dx, taps_packed, point_packed, norms = back(
        grid, small, 0, length, h_outer, outer, outer_sums, dx_small,
        h_reduced, taps, moment, own, point_own, own_channels,
    )

    taps_small_whole = summed_everywhere(taps_packed_small)
    point_small_whole = summed_everywhere(point_packed_small)
    taps_whole = summed_everywhere(taps_packed)
    point_whole = summed_everywhere(point_packed)
    block = pl.BlockSpec((1, TAP_ROWS, 128), lambda tap: (tap // slots, tap % slots, 0))
    mid_grad, small_grad = pl.pallas_call(
        unpack_taps,
        grid=(TAPS,),
        in_specs=[block, block],
        out_specs=(
            pl.BlockSpec((2, 1, MID_IN, MID_OUT), lambda tap: (0, tap, 0, 0)),
            pl.BlockSpec((2, 1, SMALL_IN, SMALL_OUT), lambda tap: (0, tap, 0, 0)),
        ),
        out_shape=(
            shape((2, TAPS, MID_IN, MID_OUT), F32),
            shape((2, TAPS, SMALL_IN, SMALL_OUT), F32),
        ),
    )(taps_whole, taps_small_whole)
    point_grad = call(
        functools.partial(unpack_point, parts), shape((2, CHANNELS, SQUEEZED), F32)
    )(point_whole, point_small_whole)
    act = act.reshape(1, small.frames, small.side, PITCH, OUTER)[:, :, :, : small.side]
    act = jnp.concatenate([act[..., :576], act[..., 640:]], axis=-1)
    input_grad = dx.reshape(1, grid.frames, side, PITCH, own_channels)[:, :, :, :side]
    input_grad = input_grad * mask[None]
    gain_grad = jnp.stack([norms[1], norms_small[1]])
    shift_grad = jnp.stack([norms[0], norms_small[0]])
    return (act, input_grad, point_grad, mid_grad, small_grad, gain_grad, shift_grad)


def solution(mesh):
    split = P("dp", None, None, None, "branch")
    whole = P("dp", None, None, None, None)
    return jax.shard_map(
        on_device,
        mesh=mesh,
        in_specs=(split, P("dp"), whole, P(), P(), P(), P(), P()),
        out_specs=(whole, split, P(), P(), P(), P(), P()),
        check_vma=False,
    )
```

time: 3180 us -> 813 us (0.26)
  waiting for transfers between devices: 1750 us -> 383 us
  local copies, waits for them, and re-layouts: 690 us -> 44.1 us
  blocking collectives: 328 us -> 78.5 us
  Pallas kernels: 0 us -> 229 us
  other arithmetic: 152 us -> 17.4 us
  loops' own time: 111 us -> 0 us
  matrix products: 86.9 us -> 0 us
  starting transfers between devices: 0.33 us -> 35.9 us
    all_gather x3 -> x4, waiting for transfers between devices: 1060 us -> 218 us  [summed_everywhere(): whole = lax.all_gather(share, ('branch', 'dp'), axis=0, tiled=True)]
    unnamed x12 -> x8, waiting for transfers between devices: 655 us -> 0.81 us
    another operation x35 -> x3, local copies, waits for them, and re-layouts: 232 us -> 2.39 us  [the longest x1 2.38 us: on_device(): own.reshape(parts, local * grid.frame_rows, own_channels)]
    pallas_call x0 -> x16, Pallas kernels: none -> 229 us  [the longest x15 211 us: run(): pl.pallas_call(body, out_shape=out_shape, in_specs=specs, out_specs=jax.t...]
    unnamed x402 -> x63, local copies, waits for them, and re-layouts: 186 us -> 12.1 us
    all_gather x3 -> x8, blocking collectives: 215 us -> 78.5 us  [the longest x2 20 us: back(): gathered = lax.all_gather(outer_sums, 'dp')]
    psum x8 -> x0, blocking collectives: 113 us -> none  [the longest x2 33.1 us: forward_block(): stat_sums, squares = lax.psum((stat_sums, squares), 'dp')]
    another operation x24 -> x0, loops' own time: 111 us -> none  [the longest x4 60.3 us: backward_block(): lax.switch(record['kind'], [back_none, back_mid, back_small, back_none],...]
  transfers between devices with their start and end apart: 8 -> 21, of which waited for: 8 -> 11; matrix products, arithmetic and copies ran while one was open for 10% -> 6% of each run, Pallas kernels for 0% -> 8%
where the time goes in v1:
time: 813 us; the launch traced here: 804 us
  waiting for transfers between devices  383 us (47%)
  Pallas kernels  229 us (28%)
  blocking collectives  78.5 us (10%)
  local copies, waits for them, and re-layouts  44.1 us (5%)
  starting transfers between devices  35.9 us (4%)
  other arithmetic  17.4 us (2%)
  between operations  15.7 us (2%)
    all_gather x4, waiting for transfers between devices, summed_everywhere(): whole = lax.all_gather(share, ('branch', 'dp'), axis=0, tiled=True)  218 us
    pallas_call x15, Pallas kernels, run(): pl.pallas_call(body, out_shape=out_shape, in_specs=specs, out_specs=jax.t...  211 us
    reduce_scatter x4, waiting for transfers between devices, summed_everywhere(): share = lax.psum_scatter(packed, 'dp', scatter_dimension=0, tiled=True)  123 us
    ppermute x12, starting transfers between devices, spread_over(): received.append(lax.ppermute(values, axis, perm))  29 us
    ppermute x12, waiting for transfers between devices, spread_over(): received.append(lax.ppermute(values, axis, perm))  26.1 us
    all_gather x2, blocking collectives, back(): gathered = lax.all_gather(outer_sums, 'dp')  20 us
    all_gather x2, blocking collectives, back(): gathered = lax.all_gather(sums_low, 'dp')  19.2 us
    pallas_call x1, Pallas kernels, on_device(): pl.pallas_call(unpack_taps, grid=(TAPS,), in_specs=[block, block], out_sp...  18.3 us
  transfers between devices with their start and end apart: 21, of which 11 were waited for; matrix products, arithmetic and copies ran while one was open for 6% of the time, Pallas kernels for 8%

profile of v1, /device:TPU:0, one launch (start us, length us, event | category | flops | bytes accessed | tf_op | source)
XLA Modules:
  0.0 804.1 jit_solution(9443020443464990412)
XLA Ops:
  11.0 2.4 copy.34
  13.4 6.3 all-to-all-start
  32.1 3.6 slice_bitcast_fusion
  35.7 3.8 pad_add_fusion.1
  39.5 15.5 %all-to-all-done = bf16[4,896,208]{1,2,0:T(8,128)(2,1)} async-done(((bf16[4,896,208]{1,2,0:T(8,128)(2,1)}), bf16[4,896,208]{1,2,0:T(8,128)(2,1)}, u32[]{:S(2)}, u32[]{:S(2)}) %all-to-all-start) | async-done | bytes 1490976 | tf_op jit(solution)/shard_map/all_to_all | solution.py:757
  55.0 3.5 copy.36.x_ref
  58.6 4.9 shard_map.135
  63.5 2.0 collective-permute-start.1
  65.5 1.8 collective-permute-start.2
  67.3 3.9 pad_add_fusion
  71.3 8.0 collective-permute-done.refs_1_
  79.2 18.1 %collective-permute-done.1.refs_2_ = bf16[912,256]{1,0:T(8,128)(2,1)S(1)} collective-permute-done((bf16[912,256]{1,0:T(8,128)(2,1)}, bf16[912,256]{1,0:T(8,128)(2,1)S(1)}, u32[]{:S(2)}, u32[]{:S(2)}) %collective-permute-start.1) | collective-permute-done | bytes 466976 | tf_op jit(solution)/shard_map/ppermute | solution.py:727
  97.4 14.5 %collective-permute-start.3 = (bf16[912,128]{1,0:T(8,128)(2,1)}, bf16[912,128]{1,0:T(8,128)(2,1)S(1)}, u32[]{:S(2)}, u32[]{:S(2)}) collective-permute-start(bf16[912,128]{1,0:T(8,128)(2,1)} %get-tuple-element.53.refs_0_), channel_id=1, source_target_pairs={{0,1},{1,2},{2,3},{3,0},{4,5},{5,6},{6,7},{7,4},{8,9},{9,10},{10,1... | collective-permute-start | bytes 700424 | tf_op jit(solution)/shard_map/ppermute | solution.py:727
  113.6 2.5 collective-permute-start.5
  116.2 9.2 %all-gather.8 = f32[8,3,512]{2,1,0:T(4,128)S(1)} all-gather(f32[1,3,512]{2,1,0:T(4,128)S(1)} %bitcast.129), channel_id=2, replica_groups=mesh['dp'=8,'branch'=4] {'dp'}, dimensions={0}, use_global_device_ids=true | all-gather | bytes 55296 | tf_op jit(solution)/shard_map/all_gather | solution.py:793
  141.3 2.6 collective-permute-start.6
  147.2 38.5 %shard_map.137 = (bf16[3584,256]{1,0:T(8,128)(2,1)}, bf16[4352,768]{1,0:T(8,128)(2,1)}, f32[3584,512]{1,0:T(8,128)}, f32[2,512]{1,0:T(2,128)}, f32[3,512]{1,0:T(4,128)}) custom-call(s32[1]{0:T(128)} %copy.52.length_ref, s32[1]{0:T(128)} %bitcast.place_ref, bf16[912,256]{1,0:T(8,128)(2,1)} %get-tuple-element.52.refs_0_, bf16[912,256]{1,0:T(8,128)(2,1)} %copy-done.19, ...), custom_call_target="tpu_custom_call" | custom-call | flops 20000000000 | bytes 16777216 | tf_op jit(solution)/shard_map/pallas_call | solution.py:37
  185.7 4.1 shard_map.136
  190.5 10.1 %all-gather.9.refs_7_ = f32[8,2,640]{2,1,0:T(2,128)} all-gather(f32[1,2,640]{2,1,0:T(2,128)S(1)} %maximum_bitcast_fusion), channel_id=3, replica_groups=mesh['dp'=8,'branch'=4] {'dp'}, dimensions={0}, use_global_device_ids=true | all-gather | bytes 46080 | tf_op jit(solution)/shard_map/all_gather | solution.py:820
  201.7 14.0 %shard_map.138 = (bf16[896,896]{1,0:T(8,128)(2,1)}, bf16[3584,896]{1,0:T(8,128)(2,1)}, f32[3,896]{1,0:T(4,128)}) custom-call(s32[1]{0:T(128)} %copy.52.length_ref, s32[1]{0:T(128)} %bitcast.place_ref, bf16[912,256]{1,0:T(8,128)(2,1)} %get-tuple-element.54.refs_0_, bf16[912,256]{1,0:T(8,128)(2,1)} %copy-done.4, bf16[912,256]{1,0:T(8,128)(2,1)} %copy-done.5, ...), custom_call_target="tpu_custom_call" | custom-call | flops 1000000000 | bytes 16777216 | tf_op jit(solution)/shard_map/pallas_call | solution.py:37
  215.6 5.5 shard_map.139
  221.1 10.1 %all-gather.10.sums_in_ref = f32[8,3,640]{2,1,0:T(4,128)} all-gather(f32[1,3,640]{2,1,0:T(4,128)} %bitcast.126), channel_id=4, replica_groups=mesh['dp'=8,'branch'=4] {'dp'}, dimensions={0}, use_global_device_ids=true | all-gather | bytes 69120 | tf_op jit(solution)/shard_map/all_gather | solution.py:842
  231.2 13.5 %shard_map.140 = (bf16[896,256]{1,0:T(8,128)(2,1)}, bf16[1312,768]{1,0:T(8,128)(2,1)}, f32[896,512]{1,0:T(8,128)}, f32[2,512]{1,0:T(2,128)}, f32[3,640]{1,0:T(4,128)}) custom-call(s32[1]{0:T(128)S(6)} %select_n.8.length_ref, f32[896,640]{1,0:T(8,128)} %get-tuple-element.62.q_ref, f32[8,3,640]{2,1,0:T(4,128)} %all-gather.10.sums_in_ref, f32[1,256]{1,0:T(1,128)} %bitcast.123, ...), custom_call_target="tpu_custom_call" | custom-call | flops 1000000000 | bytes 16777216 | tf_op jit(solution)/shard_map/pallas_call | solution.py:37
  244.7 9.8 %all-gather.11.sums_in_ref = f32[8,2,512]{2,1,0:T(2,128)} all-gather(f32[1,2,512]{2,1,0:T(2,128)} %bitcast.134), channel_id=5, replica_groups=mesh['dp'=8,'branch'=4] {'dp'}, dimensions={0}, use_global_device_ids=true | all-gather | bytes 36864 | tf_op jit(solution)/shard_map/all_gather | solution.py:856
  254.5 6.8 shard_map.141
  261.3 10.1 %all-gather.12.sums_in_ref = f32[8,2,896]{2,1,0:T(2,128)} all-gather(f32[1,2,896]{2,1,0:T(2,128)} %bitcast.130), channel_id=6, replica_groups=mesh['dp'=8,'branch'=4] {'dp'}, dimensions={0}, use_global_device_ids=true | all-gather | bytes 64512 | tf_op jit(solution)/shard_map/all_gather | solution.py:874
  271.4 14.8 %shard_map.142 = (bf16[1312,512]{1,0:T(8,128)(2,1)}, bf16[896,256]{1,0:T(8,128)(2,1)}, f32[2,256]{1,0:T(2,128)}, f32[2,896]{1,0:T(2,128)}) custom-call(s32[1]{0:T(128)S(6)} %select_n.8.length_ref, bf16[896,896]{1,0:T(8,128)(2,1)} %get-tuple-element.70.h_ref, f32[3,896]{1,0:T(4,128)} %get-tuple-element.71.outer_ref, f32[8,2,896]{2,1,0:T(2,128)} %all-gather.12.sums_in_ref, ...), custom_call_target="tpu_custom_call" | custom-call | flops 1000000000 | bytes 16777216 | tf_op jit(solution)/shard_map/pallas_call | solution.py:37
  286.2 9.6 %all-gather.13.sums_in_ref = f32[8,2,256]{2,1,0:T(2,128)} all-gather(f32[1,2,256]{2,1,0:T(2,128)} %bitcast.151), channel_id=7, replica_groups=mesh['dp'=8,'branch'=4] {'dp'}, dimensions={0}, use_global_device_ids=true | all-gather | bytes 18432 | tf_op jit(solution)/shard_map/all_gather | solution.py:906
  295.8 9.3 %shard_map.143 = (bf16[896,896]{1,0:T(8,128)(2,1)}, bf16[1152,128]{1,0:T(8,128)(2,1)}, f32[2,256]{1,0:T(2,128)}) custom-call(s32[1]{0:T(128)S(6)} %select_n.8.length_ref, s32[1]{0:T(128)} %bitcast.place_ref, bf16[896,896]{1,0:T(8,128)(2,1)} %get-tuple-element.70.h_ref, f32[3,896]{1,0:T(4,128)} %get-tuple-element.71.outer_ref, ...), custom_call_target="tpu_custom_call" | custom-call | flops 1000000000 | bytes 16777216 | tf_op jit(solution)/shard_map/pallas_call | solution.py:37
  305.1 12.6 %shard_map.144 = f32[2,896]{1,0:T(2,128)} custom-call(s32[1]{0:T(128)} %copy.52.length_ref, bf16[3584,896]{1,0:T(8,128)(2,1)} %get-tuple-element.68.h_ref, f32[1,896]{1,0:T(1,128)} %reshape.135.refs_8_.gain_ref, f32[1,896]{1,0:T(1,128)} %reshape.136.refs_9_.shift_ref, bf16[896,896]{1,0:T(8,128)(2,1)} %get-tuple-element.77.grad_ref), custom_call_target="tpu_custom_call" | custom-call | flops 1000000000 | bytes 16777216 | tf_op jit(solution)/shard_map/pallas_call | solution.py:37
  317.8 9.9 %all-gather.14.sums_in_ref = f32[8,2,896]{2,1,0:T(2,128)} all-gather(f32[1,2,896]{2,1,0:T(2,128)} %bitcast.118), channel_id=8, replica_groups=mesh['dp'=8,'branch'=4] {'dp'}, dimensions={0}, use_global_device_ids=true | all-gather | bytes 64512 | tf_op jit(solution)/shard_map/all_gather | solution.py:874
  327.7 44.9 %shard_map.145 = (bf16[4352,512]{1,0:T(8,128)(2,1)}, bf16[3584,256]{1,0:T(8,128)(2,1)}, f32[2,256]{1,0:T(2,128)}, f32[2,896]{1,0:T(2,128)}) custom-call(s32[1]{0:T(128)} %copy.52.length_ref, bf16[3584,896]{1,0:T(8,128)(2,1)} %get-tuple-element.68.h_ref, f32[3,896]{1,0:T(4,128)} %get-tuple-element.69.outer_ref, f32[8,2,896]{2,1,0:T(2,128)} %all-gather.14.sums_in_ref, ...), custom_call_target="tpu_custom_call" | custom-call | flops 20000000000 | bytes 16777216 | tf_op jit(solution)/shard_map/pallas_call | solution.py:37
  372.5 9.6 %all-gather.15.sums_in_ref = f32[8,2,256]{2,1,0:T(2,128)} all-gather(f32[1,2,256]{2,1,0:T(2,128)} %bitcast.152), channel_id=9, replica_groups=mesh['dp'=8,'branch'=4] {'dp'}, dimensions={0}, use_global_device_ids=true | all-gather | bytes 18432 | tf_op jit(solution)/shard_map/all_gather | solution.py:906
  382.2 17.3 %shard_map.146 = (bf16[3584,208]{1,0:T(8,128)(2,1)}, bf16[1152,128]{1,0:T(8,128)(2,1)}, f32[2,256]{1,0:T(2,128)}) custom-call(s32[1]{0:T(128)} %copy.52.length_ref, s32[1]{0:T(128)} %bitcast.place_ref, bf16[3584,896]{1,0:T(8,128)(2,1)} %get-tuple-element.68.h_ref, f32[3,896]{1,0:T(4,128)} %get-tuple-element.69.outer_ref, ...), custom_call_target="tpu_custom_call" | custom-call | flops 1000000000 | bytes 16777216 | tf_op jit(solution)/shard_map/pallas_call | solution.py:37
  400.2 5.6 shard_map.149
  406.1 15.0 %shard_map.148 = bf16[3072,128]{1,0:T(8,128)(2,1)} custom-call(s32[1]{0:T(128)S(6)} %mul.39.first_ref, bf16[4352,768]{1,0:T(8,128)(2,1)} %get-tuple-element.85.taps_ref, bf16[4352,512]{1,0:T(8,128)(2,1)} %get-tuple-element.86.d_ref), custom_call_target="tpu_custom_call" | custom-call | flops 1000000000 | bytes 16777216 | tf_op jit(solution)/shard_map/pallas_call | solution.py:37
  421.2 9.9 %reduce-scatter.5.cloned.1.call-done = bf16[144,128]{1,0:T(8,128)(2,1)} async-done(((bf16[1152,128]{1,0:T(8,128)(2,1)}), bf16[144,128]{1,0:T(8,128)(2,1)}) %reduce-scatter.5.cloned.1.call-update) | async-done | bytes 36880 | tf_op jit(solution)/shard_map/reduce_scatter | solution.py:736
  431.2 35.9 %reduce-scatter.7.cloned.1.call-done = bf16[144,128]{1,0:T(8,128)(2,1)} async-done(((bf16[1152,128]{1,0:T(8,128)(2,1)}), bf16[144,128]{1,0:T(8,128)(2,1)}) %reduce-scatter.7.cloned.1.call-update) | async-done | bytes 36880 | tf_op jit(solution)/shard_map/reduce_scatter | solution.py:736
  467.2 38.7 %reduce-scatter.11.cloned.1.call-done = bf16[384,128]{1,0:T(8,128)(2,1)} async-done(((bf16[3072,128]{1,0:T(8,128)(2,1)}), bf16[384,128]{1,0:T(8,128)(2,1)}) %reduce-scatter.11.cloned.1.call-update) | async-done | bytes 98320 | tf_op jit(solution)/shard_map/reduce_scatter | solution.py:736
  505.9 38.5 %reduce-scatter.9.cloned.1.call-done = bf16[384,128]{1,0:T(8,128)(2,1)} async-done(((bf16[3072,128]{1,0:T(8,128)(2,1)}), bf16[384,128]{1,0:T(8,128)(2,1)}) %reduce-scatter.9.cloned.1.call-update) | async-done | bytes 98320 | tf_op jit(solution)/shard_map/reduce_scatter | solution.py:736
  548.9 2.0 copy_multiply_fusion
  551.0 50.3 %all-gather.21.cloned.1.call-done = bf16[4608,128]{1,0:T(8,128)(2,1)} async-done(((bf16[144,128]{1,0:T(8,128)(2,1)}), bf16[4608,128]{1,0:T(8,128)(2,1)}) %all-gather.21.cloned.1.call-update) | async-done | bytes 1179664 | tf_op jit(solution)/shard_map/all_gather | solution.py:737
  601.3 55.8 %all-gather.23.cloned.1.call-done = bf16[4608,128]{1,0:T(8,128)(2,1)} async-done(((bf16[144,128]{1,0:T(8,128)(2,1)}), bf16[4608,128]{1,0:T(8,128)(2,1)}) %all-gather.23.cloned.1.call-update) | async-done | bytes 1179664 | tf_op jit(solution)/shard_map/all_gather | solution.py:737
  657.0 4.0 shard_map.147
  661.0 5.5 copy.43
  666.5 51.3 %all-gather.27.cloned.1.call-done = bf16[12288,128]{1,0:T(8,128)(2,1)} async-done(((bf16[384,128]{1,0:T(8,128)(2,1)}), bf16[12288,128]{1,0:T(8,128)(2,1)}) %all-gather.27.cloned.1.call-update) | async-done | bytes 3145744 | tf_op jit(solution)/shard_map/all_gather | solution.py:737
  717.8 60.7 %all-gather.25.cloned.1.call-done = bf16[12288,128]{1,0:T(8,128)(2,1)} async-done(((bf16[384,128]{1,0:T(8,128)(2,1)}), bf16[12288,128]{1,0:T(8,128)(2,1)}) %all-gather.25.cloned.1.call-update) | async-done | bytes 3145744 | tf_op jit(solution)/shard_map/all_gather | solution.py:737
  778.4 18.3 %shard_map.150 = (f32[2,27,160,320]{3,2,1,0:T(8,128)}, f32[2,27,32,128]{3,2,1,0:T(8,128)}) custom-call(bf16[4,3072,128]{2,1,0:T(8,128)(2,1)} %bitcast.109, bf16[4,3072,128]{2,1,0:T(8,128)(2,1)} %bitcast.108), custom_call_target="tpu_custom_call" | custom-call | tf_op jit(solution)/shard_map/pallas_call | solution.py:961
  (155 shorter events, 43.7 us)
Async XLA Ops:
  11.0 2.4 copy-start
  13.4 41.6 %all-to-all-start = ((bf16[4,896,208]{1,2,0:T(8,128)(2,1)}), bf16[4,896,208]{1,2,0:T(8,128)(2,1)}, u32[]{:S(2)}, u32[]{:S(2)}) async-start(bf16[4,896,208]{1,2,0:T(8,128)(2,1)} %copy.34), calls=%async_computation | async-start | bytes 2981888 | tf_op jit(solution)/shard_map/all_to_all | solution.py:757
  19.7 411.4 %reduce-scatter.5.cloned.1.call-start = ((), (), s32[]{:S(2)}) async-start(), calls=%async_computation.5 | async-start | bytes 331776 | tf_op jit(solution)/shard_map/reduce_scatter | solution.py:736
  22.7 1.3 copy-start.10
  22.7 2.5 copy-start.11
  27.3 1.1 copy-start.2
  27.3 2.5 copy-start.7
  63.5 15.7 %collective-permute-start = (bf16[912,256]{1,0:T(8,128)(2,1)}, bf16[912,256]{1,0:T(8,128)(2,1)S(1)}, u32[]{:S(2)}, u32[]{:S(2)}) collective-permute-start(bf16[912,256]{1,0:T(8,128)(2,1)} %get-tuple-element.52.refs_0_), channel_id=1, source_target_pairs={{0,1},{1,2},{2,3},{3,0},{4,5},{5,6},{6,7},{7,4},{8,9},{9,10},{10,1... | collective-permute-start | bytes 1400840 | tf_op jit(solution)/shard_map/ppermute | solution.py:727
  63.5 33.9 %collective-permute-start.1 = (bf16[912,256]{1,0:T(8,128)(2,1)}, bf16[912,256]{1,0:T(8,128)(2,1)S(1)}, u32[]{:S(2)}, u32[]{:S(2)}) collective-permute-start(bf16[912,256]{1,0:T(8,128)(2,1)} %get-tuple-element.52.refs_0_), channel_id=1, source_target_pairs={{0,2},{1,3},{2,0},{3,1},{4,6},{5,7},{6,4},{7,5},{8,10},{9,11},{10,... | collective-permute-start | bytes 1400840 | tf_op jit(solution)/shard_map/ppermute | solution.py:727
  65.5 31.9 %collective-permute-start.2 = (bf16[912,256]{1,0:T(8,128)(2,1)}, bf16[912,256]{1,0:T(8,128)(2,1)S(1)}, u32[]{:S(2)}, u32[]{:S(2)}) collective-permute-start(bf16[912,256]{1,0:T(8,128)(2,1)} %get-tuple-element.52.refs_0_), channel_id=1, source_target_pairs={{0,3},{1,0},{2,1},{3,2},{4,7},{5,4},{6,5},{7,6},{8,11},{9,8},{10,9... | collective-permute-start | bytes 1400840 | tf_op jit(solution)/shard_map/ppermute | solution.py:727
  67.3 48.9 %copy-start.13 = (f32[3,512]{1,0:T(4,128)S(1)}, f32[3,512]{1,0:T(4,128)}, u32[]{:S(2)}) copy-start(f32[3,512]{1,0:T(4,128)} %get-tuple-element.56) | copy-start | bytes 18436
  79.2 37.0 %copy-start.19 = (bf16[912,256]{1,0:T(8,128)(2,1)}, bf16[912,256]{1,0:T(8,128)(2,1)S(1)}, u32[]{:S(2)}) copy-start(bf16[912,256]{1,0:T(8,128)(2,1)S(1)} %collective-permute-done.refs_1_) | copy-start | bytes 1400836
  97.4 18.8 %copy-start.20 = (bf16[912,256]{1,0:T(8,128)(2,1)}, bf16[912,256]{1,0:T(8,128)(2,1)S(1)}, u32[]{:S(2)}) copy-start(bf16[912,256]{1,0:T(8,128)(2,1)S(1)} %collective-permute-done.1.refs_2_) | copy-start | bytes 1400836
  97.4 18.8 %copy-start.21 = (bf16[912,256]{1,0:T(8,128)(2,1)}, bf16[912,256]{1,0:T(8,128)(2,1)S(1)}, u32[]{:S(2)}) copy-start(bf16[912,256]{1,0:T(8,128)(2,1)S(1)} %collective-permute-done.2.refs_3_) | copy-start | bytes 1400836
  97.4 30.1 %collective-permute-start.3 = (bf16[912,128]{1,0:T(8,128)(2,1)}, bf16[912,128]{1,0:T(8,128)(2,1)S(1)}, u32[]{:S(2)}, u32[]{:S(2)}) collective-permute-start(bf16[912,128]{1,0:T(8,128)(2,1)} %get-tuple-element.53.refs_0_), channel_id=1, source_target_pairs={{0,1},{1,2},{2,3},{3,0},{4,5},{5,6},{6,7},{7,4},{8,9},{9,10},{10,1... | collective-permute-start | bytes 700424 | tf_op jit(solution)/shard_map/ppermute | solution.py:727
  113.6 27.6 %collective-permute-start.4 = (bf16[912,128]{1,0:T(8,128)(2,1)}, bf16[912,128]{1,0:T(8,128)(2,1)S(1)}, u32[]{:S(2)}, u32[]{:S(2)}) collective-permute-start(bf16[912,128]{1,0:T(8,128)(2,1)} %get-tuple-element.53.refs_0_), channel_id=1, source_target_pairs={{0,2},{1,3},{2,0},{3,1},{4,6},{5,7},{6,4},{7,5},{8,10},{9,11},{10,... | collective-permute-start | bytes 700424 | tf_op jit(solution)/shard_map/ppermute | solution.py:727
  113.6 27.6 %collective-permute-start.5 = (bf16[912,128]{1,0:T(8,128)(2,1)}, bf16[912,128]{1,0:T(8,128)(2,1)S(1)}, u32[]{:S(2)}, u32[]{:S(2)}) collective-permute-start(bf16[912,128]{1,0:T(8,128)(2,1)} %get-tuple-element.53.refs_0_), channel_id=1, source_target_pairs={{0,3},{1,0},{2,1},{3,2},{4,7},{5,4},{6,5},{7,6},{8,11},{9,8},{10,9... | collective-permute-start | bytes 700424 | tf_op jit(solution)/shard_map/ppermute | solution.py:727
  125.5 15.7 %copy-start.12 = (f32[3,512]{1,0:T(4,128)}, f32[3,512]{1,0:T(4,128)S(1)}, u32[]{:S(2)}) copy-start(f32[3,512]{1,0:T(4,128)S(1)} %reduce_sum.9.refs_4_) | copy-start | bytes 18436
  125.5 19.4 %collective-permute-start.10 = (f32[3,512]{1,0:T(4,128)S(1)}, f32[3,512]{1,0:T(4,128)S(1)}, u32[]{:S(2)}, u32[]{:S(2)}) collective-permute-start(f32[3,512]{1,0:T(4,128)S(1)} %reduce_sum.9.refs_4_), channel_id=1, source_target_pairs={{0,2},{1,3},{2,0},{3,1},{4,6},{5,7},{6,4},{7,5},{8,10},{9,11},{10,... | collective-permute-start | bytes 18440 | tf_op jit(solution)/shard_map/ppermute | solution.py:727
  126.0 20.6 %collective-permute-start.11 = (f32[3,512]{1,0:T(4,128)S(1)}, f32[3,512]{1,0:T(4,128)S(1)}, u32[]{:S(2)}, u32[]{:S(2)}) collective-permute-start(f32[3,512]{1,0:T(4,128)S(1)} %reduce_sum.9.refs_4_), channel_id=1, source_target_pairs={{0,3},{1,0},{2,1},{3,2},{4,7},{5,4},{6,5},{7,6},{8,11},{9,8},{10,9... | collective-permute-start | bytes 18440 | tf_op jit(solution)/shard_map/ppermute | solution.py:727
  127.5 13.7 %copy-start.22 = (bf16[912,128]{1,0:T(8,128)(2,1)}, bf16[912,128]{1,0:T(8,128)(2,1)S(1)}, u32[]{:S(2)}) copy-start(bf16[912,128]{1,0:T(8,128)(2,1)S(1)} %collective-permute-done.3.refs_1_) | copy-start | bytes 700420
  127.5 19.1 %collective-permute-start.9 = (f32[3,512]{1,0:T(4,128)S(1)}, f32[3,512]{1,0:T(4,128)S(1)}, u32[]{:S(2)}, u32[]{:S(2)}) collective-permute-start(f32[3,512]{1,0:T(4,128)S(1)} %reduce_sum.9.refs_4_), channel_id=1, source_target_pairs={{0,1},{1,2},{2,3},{3,0},{4,5},{5,6},{6,7},{7,4},{8,9},{9,10},{10,1... | collective-permute-start | bytes 18440 | tf_op jit(solution)/shard_map/ppermute | solution.py:727
  138.6 2.6 copy-start.3
  141.2 44.5 %copy-start.23 = (bf16[912,128]{1,0:T(8,128)(2,1)}, bf16[912,128]{1,0:T(8,128)(2,1)S(1)}, u32[]{:S(2)}) copy-start(bf16[912,128]{1,0:T(8,128)(2,1)S(1)} %collective-permute-done.4.refs_2_) | copy-start | bytes 700420
  141.2 44.5 %copy-start.24 = (bf16[912,128]{1,0:T(8,128)(2,1)}, bf16[912,128]{1,0:T(8,128)(2,1)S(1)}, u32[]{:S(2)}) copy-start(bf16[912,128]{1,0:T(8,128)(2,1)S(1)} %collective-permute-done.5.refs_3_) | copy-start | bytes 700420
  141.3 59.3 %collective-permute-start.6 = (bf16[912,256]{1,0:T(8,128)(2,1)S(1)}, bf16[912,256]{1,0:T(8,128)(2,1)S(1)}, u32[]{:S(2)}, u32[]{:S(2)}) collective-permute-start(bf16[912,256]{1,0:T(8,128)(2,1)S(1)} %copy-done.3), channel_id=1, source_target_pairs={{0,1},{1,2},{2,3},{3,0},{4,5},{5,6},{6,7},{7,4},{8,9},{9,10},{10,1... | collective-permute-start | bytes 1400840 | tf_op jit(solution)/shard_map/ppermute | solution.py:727
  143.8 56.7 %collective-permute-start.7 = (bf16[912,256]{1,0:T(8,128)(2,1)S(1)}, bf16[912,256]{1,0:T(8,128)(2,1)S(1)}, u32[]{:S(2)}, u32[]{:S(2)}) collective-permute-start(bf16[912,256]{1,0:T(8,128)(2,1)S(1)} %copy-done.3), channel_id=1, source_target_pairs={{0,2},{1,3},{2,0},{3,1},{4,6},{5,7},{6,4},{7,5},{8,10},{9,11},{10,... | collective-permute-start | bytes 1400840 | tf_op jit(solution)/shard_map/ppermute | solution.py:727
  144.9 1.7 copy-start.25
  144.9 55.7 %collective-permute-start.8 = (bf16[912,256]{1,0:T(8,128)(2,1)S(1)}, bf16[912,256]{1,0:T(8,128)(2,1)S(1)}, u32[]{:S(2)}, u32[]{:S(2)}) collective-permute-start(bf16[912,256]{1,0:T(8,128)(2,1)S(1)} %copy-done.3), channel_id=1, source_target_pairs={{0,3},{1,0},{2,1},{3,2},{4,7},{5,4},{6,5},{7,6},{8,11},{9,8},{10,9... | collective-permute-start | bytes 1400840 | tf_op jit(solution)/shard_map/ppermute | solution.py:727
  146.6 0.6 copy-start.26
  146.6 0.6 copy-start.27
  185.7 4.1 copy-start.14
  200.6 0.8 copy-start.4
  200.6 0.9 copy-start.5
  200.6 1.1 copy-start.6
  399.4 67.7 %reduce-scatter.7.cloned.1.call-start = ((), (), s32[]{:S(2)}) async-start(), calls=%async_computation.7 | async-start | bytes 331776 | tf_op jit(solution)/shard_map/reduce_scatter | solution.py:736
  400.2 105.7 %reduce-scatter.11.cloned.1.call-start = ((), (), s32[]{:S(2)}) async-start(), calls=%async_computation.11 | async-start | bytes 884736 | tf_op jit(solution)/shard_map/reduce_scatter | solution.py:736
  405.8 138.6 %reduce-scatter.9.cloned.1.call-start = ((), (), s32[]{:S(2)}) async-start(), calls=%async_computation.9 | async-start | bytes 884736 | tf_op jit(solution)/shard_map/reduce_scatter | solution.py:736
  421.1 125.7 %copy-start.9 = (f32[2,896]{1,0:T(2,128)S(1)}, f32[2,896]{1,0:T(2,128)}, u32[]{:S(2)}) copy-start(f32[2,896]{1,0:T(2,128)} %get-tuple-element.79.total_ref) | copy-start | bytes 21508
  421.1 125.7 %copy-start.16 = (f32[2,256]{1,0:T(2,128)S(1)}, f32[2,256]{1,0:T(2,128)}, u32[]{:S(2)}) copy-start(f32[2,256]{1,0:T(2,128)} %get-tuple-element.91) | copy-start | bytes 6148
  421.2 125.8 %copy-start.8 = (f32[2,896]{1,0:T(2,128)S(1)}, f32[2,896]{1,0:T(2,128)}, u32[]{:S(2)}) copy-start(f32[2,896]{1,0:T(2,128)} %get-tuple-element.74.total_ref) | copy-start | bytes 21508
  421.2 125.9 %copy-start.15 = (f32[2,256]{1,0:T(2,128)S(1)}, f32[2,256]{1,0:T(2,128)}, u32[]{:S(2)}) copy-start(f32[2,256]{1,0:T(2,128)} %get-tuple-element.92) | copy-start | bytes 6148
  421.2 180.1 %all-gather.21.cloned.1.call-start = ((), (), s32[]{:S(2)}) async-start(), calls=%async_computation.6 | async-start | bytes 1216512 | tf_op jit(solution)/shard_map/all_gather | solution.py:737
  431.2 225.9 %all-gather.23.cloned.1.call-start = ((), (), s32[]{:S(2)}) async-start(), calls=%async_computation.8 | async-start | bytes 1216512 | tf_op jit(solution)/shard_map/all_gather | solution.py:737
  467.1 250.7 %all-gather.27.cloned.1.call-start = ((), (), s32[]{:S(2)}) async-start(), calls=%async_computation.12 | async-start | bytes 3244032 | tf_op jit(solution)/shard_map/all_gather | solution.py:737
  505.9 272.6 %all-gather.25.cloned.1.call-start = ((), (), s32[]{:S(2)}) async-start(), calls=%async_computation.10 | async-start | bytes 3244032 | tf_op jit(solution)/shard_map/all_gather | solution.py:737
  545.6 3.3 copy-start.1
  545.6 3.3 copy-start.18
  (1 other events, 0.6 us)
Sparse Core Ops, SparseCore 0:
  399.6 31.5 reduce-scatter.4
  434.2 32.8 reduce-scatter.6
  470.8 34.9 reduce-scatter.10
  509.4 34.9 reduce-scatter.8
  547.2 54.0 all-gather.20
  604.0 52.9 all-gather.22
  659.9 57.8 all-gather.26
  720.7 57.7 all-gather.24

commit v2 on v1

--- a/solution.py
+++ b/solution.py
@@ -28,17 +28,26 @@
 VMEM_BYTES = 58 * 2**20
 
 
-def call(body, out_shape, scratch=(), scalars=0, flops=10**9):
+def call(body, out_shape, scratch=(), scalars=0, flops=10**9, out_space=pltpu.VMEM, aliases=None):
+    aliases = aliases or {}
+
     def run(*operands):
         specs = [
-            pl.BlockSpec(memory_space=pltpu.SMEM if number < scalars else pltpu.VMEM)
+            pl.BlockSpec(
+                memory_space=pl.ANY
+                if number in aliases
+                else pltpu.SMEM
+                if number < scalars
+                else pltpu.VMEM
+            )
             for number in range(len(operands))
         ]
         return pl.pallas_call(
             body,
             out_shape=out_shape,
             in_specs=specs,
-            out_specs=jax.tree.map(lambda _: pl.BlockSpec(memory_space=pltpu.VMEM), out_shape),
+            out_specs=jax.tree.map(lambda _: pl.BlockSpec(memory_space=out_space), out_shape),
+            input_output_aliases=aliases,
             scratch_shapes=list(scratch),
             compiler_params=pltpu.CompilerParams(vmem_limit_bytes=VMEM_BYTES),
             cost_estimate=pl.CostEstimate(
@@ -198,14 +207,11 @@
     rows = local * grid.frame_rows
     wide = 2 * grid.frame_rows
     count = count_ref[0]
-
-    @pl.loop(0, local // 2)
-    def _(pair):
-        at = rows_at(pair * wide, wide)
-        total = jnp.dot(x_ref[0, at, :], p_ref[0], preferred_element_type=F32)
-        for part in range(1, parts):
-            total = total + jnp.dot(x_ref[part, at, :], p_ref[part], preferred_element_type=F32)
-        u_ref[at, :] = total
+    for part in range(parts):
+        product = lax.dot_general(
+            x_ref[part], p_ref[part], (((0,), (0,)), ((), ())), preferred_element_type=F32
+        )
+        u_ref[...] = product if part == 0 else u_ref[...] + product
 
     def summed(pair, carry):
         values = u_ref[rows_at(pair * wide, wide), :]
@@ -320,7 +326,8 @@
 
 def first_output(grid, small, local, parts, length_ref, place_ref, *refs):
     directs, rest = (refs[:parts], refs[parts:])
-    q_ref, e_ref, moment_ref, sums_ref, gain_ref, shift_ref, pooled_ref, h_ref, outer_ref = rest
+    q_ref, e_ref, moment_ref, sums_ref, gain_ref, shift_ref, *rest = rest
+    pooled_ref, h_ref, slope_ref, outer_ref, pooled_slope_ref, pooled_product_ref = rest
     length = length_ref[0]
     valid, _ = row_geometry(grid.side, 128)
     wide_valid = jnp.concatenate([valid] * (OUTER // 128), axis=1)
@@ -341,7 +348,7 @@
 
         @pl.loop(0, local // 2)
         def _(pair):
-            acts = []
+            acts, slopes, products = ([], [], [])
             for number in range(2):
                 frame = source * local + 2 * pair + number
                 at = rows_at(frame * rows, rows)
@@ -349,12 +356,26 @@
                 values = jnp.concatenate([direct, e_ref[at, :], q_ref[at, :]], axis=1)
                 scaled = (values - center) * inverse
                 h_ref[at, :] = scaled.astype(BF16)
-                act = silu(gain_ref[...] * scaled + shift_ref[...])
-                acts.append((act * (wide_valid * frame_flag(frame, length))).astype(BF16))
-            coarse = source * (local // 2) + pair
-            pooled_ref[rows_at(coarse * small.frame_rows, small.frame_rows), :] = jnp.dot(
-                matrix, jnp.concatenate(acts, axis=0), preferred_element_type=F32
-            ).astype(BF16)
+                shifted = gain_ref[...] * scaled + shift_ref[...]
+                gate = sigmoid(shifted)
+                mask = wide_valid * frame_flag(frame, length)
+                gate_mask = gate * mask
+                act = shifted * gate_mask
+                slope = gate_mask + act * (1.0 - gate)
+                low_slope = slope.astype(BF16)
+                slope_ref[at, :] = low_slope
+                acts.append(act.astype(BF16))
+                slopes.append(low_slope)
+                products.append((slope * scaled).astype(BF16))
+            at = rows_at((source * (local // 2) + pair) * small.frame_rows, small.frame_rows)
+            for ref_out, pieces in (
+                (pooled_ref, acts),
+                (pooled_slope_ref, slopes),
+                (pooled_product_ref, products),
+            ):
+                ref_out[at, :] = jnp.dot(
+                    matrix, jnp.concatenate(pieces, axis=0), preferred_element_type=F32
+                ).astype(BF16)
 
 
 def second_pointwise(grid, length_ref, count_ref, x_ref, p_ref, q_ref, out_sums_ref, plane_ref, sums_ref, pool_sums_ref):
@@ -409,7 +430,7 @@
     write_sums(out_sums_ref, sums_ref, 0, SECOND)
 
 
-def second_output(grid, length_ref, q_ref, e_ref, moment_ref, sums_in_ref, gain_ref, shift_ref, cot_ref, act_ref, h_ref, outer_ref, out_sums_ref, sums_ref):
+def second_output(grid, length_ref, q_ref, e_ref, moment_ref, sums_in_ref, gain_ref, shift_ref, cot_ref, act_ref, h_ref, error_ref, outer_ref, out_sums_ref, sums_ref):
     length = length_ref[0]
     valid, _ = row_geometry(grid.side, 128)
     wide_valid = jnp.concatenate([valid] * (OUTER // 128), axis=1)
@@ -435,44 +456,27 @@
         act_ref[at, :] = (shifted * gate * mask).astype(BF16)
         slope = gate * (1.0 + shifted * (1.0 - gate))
         error = cot_ref[at, :].astype(F32) * slope * mask
+        error_ref[at, :] = error.astype(BF16)
         sums_ref[0:8] += partial_sum(error)
         sums_ref[8:16] += partial_sum(error * scaled)
 
     write_sums(out_sums_ref, sums_ref, 0, OUTER)
 
 
-def outer_gradient(grid, small, grad_ref, matrix, frame, lo, hi):
+def outer_error(grid, small, slope_ref, grad_ref, matrix, frame, lo, hi):
+    values = slope_ref[rows_at(frame * grid.frame_rows, grid.frame_rows), lo:hi].astype(F32)
     if small is None:
-        return grad_ref[rows_at(frame * grid.frame_rows, grid.frame_rows), lo:hi].astype(F32)
+        return values
     coarse = grad_ref[rows_at((frame // 2) * small.frame_rows, small.frame_rows), lo:hi]
-    return jnp.dot(matrix, coarse, preferred_element_type=F32)
+    return values * jnp.dot(matrix, coarse, preferred_element_type=F32)
 
 
 def spread_matrix(grid, small):
     return None if small is None else pool_matrix(small.side, True)[: grid.frame_rows]
 
 
-def first_outer_sums(grid, small, length_ref, h_ref, gain_ref, shift_ref, grad_ref, out_sums_ref, sums_ref):
-    length = length_ref[0]
-    valid, _ = row_geometry(grid.side, 128)
-    wide_valid = jnp.concatenate([valid] * (OUTER // 128), axis=1)
-    matrix = spread_matrix(grid, small)
-    sums_ref[...] = jnp.zeros_like(sums_ref)
-
-    @pl.loop(0, grid.frames)
-    def _(frame):
-        at = rows_at(frame * grid.frame_rows, grid.frame_rows)
-        scaled = h_ref[at, :].astype(F32)
-        slope = silu_slope(gain_ref[...] * scaled + shift_ref[...])
-        grad = outer_gradient(grid, small, grad_ref, matrix, frame, 0, OUTER)
-        error = grad * slope * (wide_valid * frame_flag(frame, length))
-        sums_ref[0:8] += partial_sum(error)
-        sums_ref[8:16] += partial_sum(error * scaled)
-
-    write_sums(out_sums_ref, sums_ref, 0, OUTER)
-
-
-def conv_back(grid, small, length_ref, h_ref, outer_ref, sums_in_ref, gain_ref, shift_ref, grad_ref, kernel_ref, reduced_ref, reduced_gain_ref, reduced_shift_ref, d_ref, r_ref, out_sums_ref, total_ref, acc_ref, sums_ref):
+def second_back(grid, small, length_ref, h_ref, outer_ref, sums_in_ref, gain_ref, slope_ref, *rest):
+    grad_ref, d_ref, total_ref = rest if small is not None else (None, *rest)
     length = length_ref[0]
     valid, _ = row_geometry(grid.side, 128)
     total = total_of(sums_in_ref)
@@ -481,8 +485,7 @@
     count = outer_ref[2:3, lo:hi]
     mean_r = total[0:1, lo:hi] / count
     mean_rh = total[1:2, lo:hi] / count
-    gain, shift = (gain_ref[:, lo:hi], shift_ref[:, lo:hi])
-    factor = gain * outer_ref[1:2, lo:hi]
+    factor = gain_ref[:, lo:hi] * outer_ref[1:2, lo:hi]
     wide_valid = jnp.concatenate([valid] * (SECOND // 128), axis=1)
     matrix = spread_matrix(grid, small)
     zero_rows(d_ref)
@@ -491,13 +494,16 @@
     def _(frame):
         at = rows_at(frame * grid.frame_rows, grid.frame_rows)
         scaled = h_ref[at, lo:hi].astype(F32)
-        grad = outer_gradient(grid, small, grad_ref, matrix, frame, lo, hi)
-        error = grad * silu_slope(gain * scaled + shift)
+        error = outer_error(grid, small, slope_ref, grad_ref, matrix, frame, lo, hi)
         back = factor * (error - mean_r - scaled * mean_rh)
         d_ref[rows_at(grid.lead + frame * grid.pitch, grid.frame_rows), :] = (
             back * (wide_valid * frame_flag(frame, length))
         ).astype(BF16)
 
+
+def conv_back(grid, length_ref, d_ref, kernel_ref, reduced_ref, reduced_gain_ref, reduced_shift_ref, r_ref, out_sums_ref, acc_ref, sums_ref):
+    length = length_ref[0]
+    valid, _ = row_geometry(grid.side, 128)
     group_rows = grid.group * grid.pitch
     sums_ref[...] = jnp.zeros_like(sums_ref)
     reduced_valid = jnp.concatenate([valid, valid], axis=1)
@@ -572,7 +578,14 @@
         out_ref[used:, :] = jnp.zeros((out_ref.shape[0] - used, 128), BF16)
 
 
-def point_back(grid, small, kept, length_ref, place_ref, h_ref, outer_ref, total_ref, gain_ref, shift_ref, grad_ref, reduced_ref, r_ref, moment_ref, sums_in_ref, reduced_gain_ref, x_ref, p_ref, dx_ref, dp_ref, reduced_total_ref, du_ref, plane_ref, acc_ref):
+def point_back(grid, small, kept, length_ref, place_ref, h_ref, outer_ref, total_ref, gain_ref, slope_ref, *rest):
+    first = small is not None
+    grad_ref, rest = (rest[0], rest[1:]) if first else (None, rest)
+    reduced_ref, r_ref, moment_ref, sums_in_ref, reduced_gain_ref, x_ref, p_ref, *rest = rest
+    pooled_refs, rest = ((), rest) if first else (rest[:2], rest[2:])
+    dx_ref, dp_ref, reduced_total_ref, *rest = rest
+    outer_sums_ref, rest = (None, rest) if first else (rest[0], rest[1:])
+    du_ref, plane_ref, acc_ref, *rest = rest
     length = length_ref[0]
     rows = grid.frame_rows
     valid, window = row_geometry(grid.side, 128)
@@ -590,12 +603,10 @@
     def section(frame, lo, hi, mask):
         at = rows_at(frame * rows, rows)
         scaled = h_ref[at, lo:hi].astype(F32)
-        gain, shift = (gain_ref[:, lo:hi], shift_ref[:, lo:hi])
-        grad = outer_gradient(grid, small, grad_ref, matrix, frame, lo, hi)
-        error = grad * silu_slope(gain * scaled + shift)
+        error = outer_error(grid, small, slope_ref, grad_ref, matrix, frame, lo, hi)
         size = outer_ref[2:3, lo:hi]
         inner = error - total_ref[0:1, lo:hi] / size - scaled * (total_ref[1:2, lo:hi] / size)
-        return (gain * outer_ref[1:2, lo:hi]) * inner * mask
+        return (gain_ref[:, lo:hi] * outer_ref[1:2, lo:hi]) * inner * mask
 
     @pl.loop(0, grid.frames)
     def _(frame):
@@ -612,6 +623,8 @@
 
     wide = 2 * rows
     acc_ref[...] = jnp.zeros_like(acc_ref)
+    if not first:
+        rest[0][...] = jnp.zeros_like(rest[0])
 
     @pl.loop(0, grid.frames // 2)
     def _(pair):
@@ -623,15 +636,23 @@
             + plane_ref[rows_at(start + 2 * rows, wide), :]
         ) * jnp.concatenate([valid, valid], axis=0)
         du = jnp.concatenate([du_ref[at, 0:SECOND], pool.astype(BF16)], axis=1)
-        dx_ref[at, :] = lax.dot_general(
+        dx = lax.dot_general(
             du, p_ref[...], (((1,), (1,)), ((), ())), preferred_element_type=F32
         ).astype(BF16)
+        dx_ref[at, :] = dx
+        if not first:
+            for number, ref in enumerate(pooled_refs):
+                rest[0][8 * number : 8 * number + 8] += partial_sum(
+                    dx.astype(F32) * ref[at, :].astype(F32)
+                )
         acc_ref[...] += lax.dot_general(
             x_ref[at, :], du, (((0,), (0,)), ((), ())), preferred_element_type=F32
         )
 
-    first = pl.multiple_of(place_ref[0] * kept, 16) if kept < acc_ref.shape[0] else 0
-    own = acc_ref[pl.ds(first, kept), :]
+    if not first:
+        write_sums(outer_sums_ref, rest[0], 0, OUTER)
+    start = pl.multiple_of(place_ref[0] * kept, 16) if kept < acc_ref.shape[0] else 0
+    own = acc_ref[pl.ds(start, kept), :]
     for tile in range(FIRST // 128):
         dp_ref[kept * tile : kept * (tile + 1), :] = own[:, 128 * tile : 128 * (tile + 1)].astype(
             BF16
@@ -641,51 +662,95 @@
         dp_ref[used:, :] = jnp.zeros((dp_ref.shape[0] - used, 128), BF16)
 
 
-def unpack_taps(first_ref, second_ref, mid_ref, small_ref):
+def write_taps(buffer_ref, parts, slots, mid_ref, small_ref):
     half = MID_IN // 2
-    for number, ref in enumerate((first_ref, second_ref)):
-        values = ref[0].astype(F32)
-        folded = values[2 * MID_IN : 2 * MID_IN + half]
-        mid_ref[number, 0, :, 0:128] = values[0:MID_IN]
-        mid_ref[number, 0, :, 128:256] = values[MID_IN : 2 * MID_IN]
-        mid_ref[number, 0, 0:half, 256:320] = folded[:, 0:64]
-        mid_ref[number, 0, half:MID_IN, 256:320] = pltpu.roll(folded, 64, 1)[:, 0:64]
-        small_ref[number, 0] = values[2 * MID_IN + half : TAP_ROWS]
-
-
-def unpack_point(parts, first_ref, second_ref, out_ref):
-    kept = CHANNELS // parts
-    for part in range(parts):
-        for tile in range(FIRST // 128):
-            values = first_ref[part, kept * tile : kept * (tile + 1), :].astype(F32)
-            at = slice(kept * part, kept * (part + 1))
-            place_columns(out_ref, 0, at, tile, values)
-    kept = OUTER // parts
-    for part in range(parts):
-        for tile in range(FIRST // 128):
-            start = kept * part
-            while start < kept * (part + 1):
-                stop = kept * (part + 1)
-                if start < SQUEEZED:
-                    stop, moved = (min(stop, SQUEEZED), 0)
-                elif start < FIRST:
-                    start = min(stop, FIRST)
-                    continue
-                else:
-                    moved = 64
-                source = kept * tile + start - kept * part
-                values = second_ref[part, source : source + stop - start, :].astype(F32)
-                place_columns(out_ref, 1, slice(start - moved, stop - moved), tile, values)
-                start = stop
-
-
-def place_columns(out_ref, block, at, tile, values):
-    if tile < 3:
-        out_ref[block, at, 128 * tile : 128 * (tile + 1)] = values
-    elif tile == 3:
-        out_ref[block, at, 384:448] = values[:, 0:64]
-    else:
-        out_ref[block, at, 448:576] = values
+
+    @pl.loop(0, TAPS)
+    def _(tap):
+        base = lax.rem(tap, slots) * TAP_ROWS
+        part = tap // slots
+
+        def piece(start, size):
+            return buffer_ref[part, rows_at(base + start, size), :].astype(F32)
+
+        folded = piece(2 * MID_IN, half)
+        mid_ref[tap, :, 0:128] = piece(0, MID_IN)
+        mid_ref[tap, :, 128:256] = piece(MID_IN, MID_IN)
+        mid_ref[tap, 0:half, 256:320] = folded[:, 0:64]
+        mid_ref[tap, half:MID_IN, 256:320] = pltpu.roll(folded, 64, 1)[:, 0:64]
+        small_ref[tap] = piece(2 * MID_IN + half, SMALL_IN)
+
+
+def write_point(read, parts, kept, point_ref, wide_ref):
+    for tile in range(FIRST // 128):
+        for part in range(parts):
+            start, stop = (kept * part, kept * (part + 1))
+            values = read(part, kept * tile, kept)
+            if kept * parts == CHANNELS:
+                wide_ref[start:stop, :] = values
+                continue
+            for lo, hi, moved in ((0, 576, 0), (640, OUTER, 64)):
+                lo, hi = (max(lo, start), min(hi, stop))
+                if lo < hi:
+                    wide_ref[lo - moved : hi - moved, :] = values[lo - start : hi - start]
+        turned = wide_ref[...].T
+        if tile < 3:
+            point_ref[128 * tile : 128 * (tile + 1), :] = turned
+        elif tile == 3:
+            point_ref[384:448, :] = turned[0:64]
+        else:
+            point_ref[448:576, :] = turned
+
+
+def copy_out(pairs, sem_ref):
+    copies = [
+        pltpu.make_async_copy(source, target, sem_ref.at[number])
+        for number, (source, target) in enumerate(pairs)
+    ]
+    for copy in copies:
+        copy.start()
+    for copy in copies:
+        copy.wait()
+
+
+def unpack_second(parts, slots, tap_rows, buffer_ref, mid_out, small_out, point_out, mid_ref, small_ref, point_ref, wide_ref, sem_ref):
+    def read(part, start, size):
+        return buffer_ref[part, tap_rows + start : tap_rows + start + size, :].astype(F32)
+
+    write_taps(buffer_ref, parts, slots, mid_ref, small_ref)
+    write_point(read, parts, OUTER // parts, point_ref, wide_ref)
+    copy_out(
+        [(mid_ref, mid_out.at[1]), (small_ref, small_out.at[1]), (point_ref, point_out.at[1])],
+        sem_ref,
+    )
+
+
+def reorder(parts, clips, share, place, clip, mine_ref, other_ref, buffer_ref):
+    for chip in range(clips // 2):
+        for step in range(parts):
+            source = (chip * parts + step) * share
+            part = lax.rem(place - step + parts, parts)
+            for swapped, ref in enumerate((mine_ref, other_ref)):
+                owner = clip ^ (2 * chip) ^ swapped
+                buffer_ref[part, rows_at(owner * share, share), :] = ref[
+                    source : source + share, :
+                ]
+
+
+def unpack_taps(parts, clips, slots, share, place_ref, clip_ref, mine_ref, other_ref, mid_in, small_in, mid_out, small_out, buffer_ref, mid_ref, small_ref, sem_ref):
+    reorder(parts, clips, share, place_ref[0], clip_ref[0], mine_ref, other_ref, buffer_ref)
+    write_taps(buffer_ref, parts, slots, mid_ref, small_ref)
+    copy_out([(mid_ref, mid_out.at[0]), (small_ref, small_out.at[0])], sem_ref)
+
+
+def unpack_point(parts, clips, share, place_ref, clip_ref, mine_ref, other_ref, point_in, point_out, buffer_ref, point_ref, wide_ref, sem_ref):
+    reorder(parts, clips, share, place_ref[0], clip_ref[0], mine_ref, other_ref, buffer_ref)
+
+    def read(part, start, size):
+        return buffer_ref[part, start : start + size, :].astype(F32)
+
+    write_point(read, parts, CHANNELS // parts, point_ref, wide_ref)
+    copy_out([(point_ref, point_out.at[0])], sem_ref)
 
 
 def outer_vector(values):
@@ -732,10 +797,21 @@
     return lax.optimization_barrier((values, earlier))[0]
 
 
-def summed_everywhere(packed):
-    share = lax.psum_scatter(packed, "dp", scatter_dimension=0, tiled=True)
-    whole = lax.all_gather(share, ("branch", "dp"), axis=0, tiled=True)
-    return whole.reshape(-1, packed.shape[0], 128)
+def shared_sum(packed, clips):
+    pieces = packed.reshape(clips, packed.shape[0] // clips, 128)
+    pieces = lax.all_to_all(pieces, "dp", 0, 0, tiled=True)
+    return jnp.sum(pieces.astype(F32), axis=0).astype(BF16)
+
+
+def gather_steps(share, parts, clips):
+    column = jnp.concatenate(spread_over(share, "branch", parts), axis=0)
+    columns = [column]
+    for chip in range(1, clips // 2):
+        perm = [(source, source ^ (2 * chip)) for source in range(clips)]
+        columns.append(lax.ppermute(column, "dp", perm))
+    mine = jnp.concatenate(columns, axis=0)
+    other = lax.ppermute(mine, "dp", [(source, source ^ 1) for source in range(clips)])
+    return (mine, other)
 
 
 def on_device(frames, lengths, cotangent, pointwise, conv_mid, conv_small, gains, shifts):
@@ -755,7 +831,11 @@
     own = jnp.pad(frames[0] * mask, ((0, 0), (0, 0), (0, PITCH - side), (0, 0)))
     own = own.reshape(grid.rows, own_channels)
     by_frames = lax.all_to_all(
-        own.reshape(parts, local * grid.frame_rows, own_channels), "branch", 0, 0, tiled=True
+        own.reshape(parts, local * grid.frame_rows, own_channels).transpose(0, 2, 1),
+        "branch",
+        0,
+        0,
+        tiled=True,
     )
 
     columns = [point_columns(pointwise[0]), point_columns(pointwise[1])]
@@ -792,8 +872,9 @@
     mids = spread_over(mid, "branch", parts)
     sums = jnp.sum(lax.all_gather(sums, "dp"), axis=0)
     all_sums = spread_over(sums, "branch", parts)
-    pools = spread_over(after(pool, mids), "branch", parts)
-    directs = spread_over(after(direct, pools), "branch", parts)
+    pool, direct = after((pool, direct), (mids, all_sums))
+    pools = spread_over(pool, "branch", parts)
+    directs = spread_over(direct, "branch", parts)
     group_rows = grid.group * grid.pitch
     h_reduced, taps, e, e_sums, moment = call(
         functools.partial(first_convolve, grid, local, parts),
@@ -818,12 +899,15 @@
         scalars=2,
     )(length, place_one, *pools)
     second_sums = lax.all_gather(jnp.concatenate([e_sums, pool_sums], axis=1), "dp")
-    pooled, h_outer, outer = call(
+    pooled, h_outer, slope, outer, pooled_slope, pooled_product = call(
         functools.partial(first_output, grid, small, local, parts),
         (
             shape((small.rows, OUTER), BF16),
             shape((grid.rows, OUTER), BF16),
+            shape((grid.rows, OUTER), BF16),
             shape((3, OUTER), F32),
+            shape((small.rows, OUTER), BF16),
+            shape((small.rows, OUTER), BF16),
         ),
         scalars=2,
     )(length, place_one, *directs, q_pool, e, moment, second_sums, outer_gain[0], outer_shift[0])
@@ -854,9 +938,10 @@
         scalars=1,
     )(half_length, q_small, sums_small, reduced_gain[1], reduced_shift[1], kernels[1])
     e_sums_small = lax.all_gather(e_sums_small, "dp")
-    act, h_outer_small, outer_small, outer_sums_small = call(
+    act, h_outer_small, error_small, outer_small, outer_sums_small = call(
         functools.partial(second_output, small),
         (
+            shape((small.rows, OUTER), BF16),
             shape((small.rows, OUTER), BF16),
             shape((small.rows, OUTER), BF16),
             shape((3, OUTER), F32),
@@ -870,52 +955,53 @@
     tap_rows = round_up(slots * TAP_ROWS, 16 * clips)
     first_tap = place_one * slots
 
-    def back(at, coarse, number, span, h_out, outer_moment, outer_sums, grad, h_red, taps_of, moment_of, x, point, kept):
+    def back(at, coarse, number, span, h_out, outer_moment, outer_sums, slopes, grad, h_red, taps_of, moment_of, x, point, kept, pooled_pair):
+        first = coarse is not None
         gathered = lax.all_gather(outer_sums, "dp")
         rows = at.group * at.pitch
-        d_low, r_low, sums_low, total = call(
-            functools.partial(conv_back, at, coarse),
-            (
-                shape((at.padded, SECOND), BF16),
-                shape((at.rows, REDUCED), BF16),
-                shape((2, REDUCED), F32),
-                shape((2, OUTER), F32),
-            ),
-            [pltpu.VMEM((rows, 3 * REDUCED), F32), pltpu.VMEM((16, REDUCED), F32)],
+        grads = (grad,) if first else ()
+        d_low, total = call(
+            functools.partial(second_back, at, coarse),
+            (shape((at.padded, SECOND), BF16), shape((2, OUTER), F32)),
             scalars=1,
-            flops=2 * 10**10 if coarse is not None else 10**9,
-        )(
-            span,
-            h_out,
-            outer_moment,
-            gathered,
-            outer_gain[number],
-            outer_shift[number],
-            grad,
-            kernels[number],
-            h_red,
-            reduced_gain[number],
-            reduced_shift[number],
-        )
+        )(span, h_out, outer_moment, gathered, outer_gain[number], slopes, *grads)
         packed_taps = call(
             functools.partial(kernel_grads, at, slots),
             shape((tap_rows, 128), BF16),
             [pltpu.VMEM((slots, REDUCED, SECOND), F32)],
             scalars=1,
         )(first_tap, taps_of, d_low)
+        r_low, sums_low = call(
+            functools.partial(conv_back, at),
+            (shape((at.rows, REDUCED), BF16), shape((2, REDUCED), F32)),
+            [pltpu.VMEM((rows, 3 * REDUCED), F32), pltpu.VMEM((16, REDUCED), F32)],
+            scalars=1,
+            flops=2 * 10**10 if first else 10**9,
+        )(
+            span,
+            after(d_low, packed_taps) if first else d_low,
+            kernels[number],
+            h_red,
+            reduced_gain[number],
+            reduced_shift[number],
+        )
         gathered = lax.all_gather(sums_low, "dp")
         point_rows = round_up(kept * (FIRST // 128), 16 * clips)
-        dx, packed_point, reduced_total = call(
+        extra_out = () if first else (shape((2, OUTER), F32),)
+        extra_scratch = [] if first else [pltpu.VMEM((16, OUTER), F32)]
+        dx, packed_point, reduced_total, *next_sums = call(
             functools.partial(point_back, at, coarse, kept),
             (
                 shape((at.rows, x.shape[1]), BF16),
                 shape((point_rows, 128), BF16),
                 shape((2, REDUCED), F32),
+                *extra_out,
             ),
             [
                 pltpu.VMEM((at.rows, SECOND), BF16),
                 pltpu.VMEM((at.rows + 2 * at.frame_rows, POOLED), F32),
                 pltpu.VMEM((x.shape[1], FIRST), F32),
+                *extra_scratch,
             ],
             scalars=2,
         )(
@@ -925,8 +1011,8 @@
             outer_moment,
             total,
             outer_gain[number],
-            outer_shift[number],
-            grad,
+            slopes,
+            *grads,
             h_red,
             r_low,
             moment_of,
@@ -934,46 +1020,86 @@
             reduced_gain[number],
             x,
             point,
+            *pooled_pair,
         )
         norms = [norm_vector(total[row], reduced_total[row]) for row in range(2)]
-        return (dx, packed_taps, packed_point, norms)
-
-    dx_small, taps_packed_small, point_packed_small, norms_small = back(
-        small, None, 1, half_length, h_outer_small, outer_small, outer_sums_small, cot,
+        return (dx, packed_taps, packed_point, norms, next_sums)
+
+    dx_small, taps_packed_small, point_packed_small, norms_small, (outer_sums,) = back(
+        small, None, 1, half_length, h_outer_small, outer_small, outer_sums_small, error_small, None,
         h_reduced_small, taps_small, moment_small, pooled, point_second, OUTER // parts,
-    )
-    outer_sums = call(
-        functools.partial(first_outer_sums, grid, small),
-        shape((2, OUTER), F32),
-        [pltpu.VMEM((16, OUTER), F32)],
-        scalars=1,
-    )(length, h_outer, outer_gain[0], outer_shift[0], dx_small)
-    dx, taps_packed, point_packed, norms = back(
-        grid, small, 0, length, h_outer, outer, outer_sums, dx_small,
-        h_reduced, taps, moment, own, point_own, own_channels,
-    )
-
-    taps_small_whole = summed_everywhere(taps_packed_small)
-    point_small_whole = summed_everywhere(point_packed_small)
-    taps_whole = summed_everywhere(taps_packed)
-    point_whole = summed_everywhere(point_packed)
-    block = pl.BlockSpec((1, TAP_ROWS, 128), lambda tap: (tap // slots, tap % slots, 0))
-    mid_grad, small_grad = pl.pallas_call(
-        unpack_taps,
-        grid=(TAPS,),
-        in_specs=[block, block],
-        out_specs=(
-            pl.BlockSpec((2, 1, MID_IN, MID_OUT), lambda tap: (0, tap, 0, 0)),
-            pl.BlockSpec((2, 1, SMALL_IN, SMALL_OUT), lambda tap: (0, tap, 0, 0)),
-        ),
-        out_shape=(
-            shape((2, TAPS, MID_IN, MID_OUT), F32),
-            shape((2, TAPS, SMALL_IN, SMALL_OUT), F32),
-        ),
-    )(taps_whole, taps_small_whole)
+        (pooled_slope, pooled_product),
+    )
+    share_small = shared_sum(
+        jnp.concatenate(
+            [
+                taps_packed_small.reshape(clips, -1, 128),
+                point_packed_small.reshape(clips, -1, 128),
+            ],
+            axis=1,
+        ).reshape(-1, 128),
+        clips,
+    )
+    whole_small = lax.all_gather(share_small, ("branch", "dp"), axis=0, tiled=True)
+    dx, taps_packed, point_packed, norms, _ = back(
+        grid, small, 0, length, h_outer, outer, outer_sums, slope, dx_small,
+        h_reduced, taps, moment, own, point_own, own_channels, (),
+    )
+    taps_mine, taps_other = gather_steps(shared_sum(taps_packed, clips), parts, clips)
+    point_mine, point_other = gather_steps(shared_sum(point_packed, clips), parts, clips)
+
+    outs = (
+        shape((2, TAPS, MID_IN, MID_OUT), F32),
+        shape((2, TAPS, SMALL_IN, SMALL_OUT), F32),
+        shape((2, SQUEEZED, CHANNELS), F32),
+    )
+    mid_scratch = pltpu.VMEM((TAPS, MID_IN, MID_OUT), F32)
+    small_scratch = pltpu.VMEM((TAPS, SMALL_IN, SMALL_OUT), F32)
+    point_scratch = [pltpu.VMEM((SQUEEZED, CHANNELS), F32), pltpu.VMEM((CHANNELS, 128), F32)]
+    small_rows = round_up((OUTER // parts) * (FIRST // 128), 16 * clips)
+    point_rows = point_packed.shape[0]
+    whole_small = whole_small.reshape(parts, clips, -1, 128)
+    tap_share = tap_rows // clips
+    whole_small = jnp.concatenate(
+        [
+            whole_small[:, :, :tap_share].reshape(parts, tap_rows, 128),
+            whole_small[:, :, tap_share:].reshape(parts, small_rows, 128),
+        ],
+        axis=1,
+    )
+    mid_grad, small_grad, point_grad = call(
+        functools.partial(unpack_second, parts, slots, tap_rows),
+        outs,
+        [mid_scratch, small_scratch, *point_scratch, pltpu.SemaphoreType.DMA((3,))],
+        out_space=pl.ANY,
+    )(whole_small)
+    clip_one = lax.axis_index("dp").astype(jnp.int32).reshape(1)
+    mid_grad, small_grad = call(
+        functools.partial(unpack_taps, parts, clips, slots, tap_share),
+        outs[:2],
+        [
+            pltpu.VMEM((parts, tap_rows, 128), BF16),
+            mid_scratch,
+            small_scratch,
+            pltpu.SemaphoreType.DMA((2,)),
+        ],
+        scalars=2,
+        out_space=pl.ANY,
+        aliases={4: 0, 5: 1},
+    )(place_one, clip_one, taps_mine, taps_other, mid_grad, small_grad)
     point_grad = call(
-        functools.partial(unpack_point, parts), shape((2, CHANNELS, SQUEEZED), F32)
-    )(point_whole, point_small_whole)
+        functools.partial(unpack_point, parts, clips, point_rows // clips),
+        outs[2],
+        [
+            pltpu.VMEM((parts, point_rows, 128), BF16),
+            *point_scratch,
+            pltpu.SemaphoreType.DMA((1,)),
+        ],
+        scalars=2,
+        out_space=pl.ANY,
+        aliases={4: 0},
+    )(place_one, clip_one, point_mine, point_other, point_grad)
+    point_grad = point_grad.swapaxes(1, 2)
     act = act.reshape(1, small.frames, small.side, PITCH, OUTER)[:, :, :, : small.side]
     act = jnp.concatenate([act[..., :576], act[..., 640:]], axis=-1)
     input_grad = dx.reshape(1, grid.frames, side, PITCH, own_channels)[:, :, :, :side]

time: 813 us -> 534 us (0.66)
  waiting for transfers between devices: 383 us -> 68.8 us
  starting transfers between devices: 35.9 us -> 55.4 us
  blocking collectives: 78.5 us -> 96.7 us
    all_gather x4 -> x1, waiting for transfers between devices: 218 us -> 0.01 us  [on_device(): lax.all_gather(share_small, ('branch', 'dp'), axis=0, tiled=True)]
    reduce_scatter x4 -> x0, waiting for transfers between devices: 123 us -> none  [summed_everywhere(): share = lax.psum_scatter(packed, 'dp', scatter_dimension=0, tiled=True)]
    ppermute x0 -> x8, waiting for transfers between devices: none -> 20.4 us  [the longest x6 20.4 us: gather_steps(): columns.append(lax.ppermute(column, 'dp', perm))]
    pallas_call x1 -> x0, Pallas kernels: 18.3 us -> none  [on_device(): pl.pallas_call(unpack_taps, grid=(TAPS,), in_specs=[block, block], out_sp...]
    all_to_all x0 -> x1, blocking collectives: none -> 18.3 us  [shared_sum(): pieces = lax.all_to_all(pieces, 'dp', 0, 0, tiled=True)]
    pallas_call x15 -> x18, Pallas kernels: 211 us -> 225 us  [run(): pl.pallas_call(body, out_shape=out_shape, in_specs=specs, out_specs=jax.t...]
    ppermute x0 -> x8, starting transfers between devices: none -> 8.73 us  [the longest x6 8.62 us: gather_steps(): columns.append(lax.ppermute(column, 'dp', perm))]
    all_to_all x1 -> x3, waiting for transfers between devices: 15.5 us -> 22.4 us  [the longest x2 11.4 us: shared_sum(): pieces = lax.all_to_all(pieces, 'dp', 0, 0, tiled=True)]
  transfers between devices with their start and end apart: 21 -> 30, of which waited for: 11 -> 11; matrix products, arithmetic and copies ran while one was open for 6% -> 10% of each run, Pallas kernels for 8% -> 26%
where the time goes in v2:
time: 534 us; the launch traced here: 525 us
  Pallas kernels  225 us (42%)
  blocking collectives  96.7 us (18%)
  waiting for transfers between devices  68.8 us (13%)
  starting transfers between devices  55.4 us (10%)
  local copies, waits for them, and re-layouts  37.9 us (7%)
  other arithmetic  24.6 us (5%)
  between operations  15.8 us (3%)
    pallas_call x18, Pallas kernels, run(): pl.pallas_call(body, out_shape=out_shape, in_specs=specs, out_specs=jax.t...  225 us
    ppermute x18, starting transfers between devices, spread_over(): received.append(lax.ppermute(values, axis, perm))  33.1 us
    ppermute x18, waiting for transfers between devices, spread_over(): received.append(lax.ppermute(values, axis, perm))  25.9 us
    ppermute x6, waiting for transfers between devices, gather_steps(): columns.append(lax.ppermute(column, 'dp', perm))  20.4 us
    all_gather x2, blocking collectives, back(): gathered = lax.all_gather(sums_low, 'dp')  19.5 us
    all_gather x2, blocking collectives, back(): gathered = lax.all_gather(outer_sums, 'dp')  19.3 us
    all_to_all x1, blocking collectives, shared_sum(): pieces = lax.all_to_all(pieces, 'dp', 0, 0, tiled=True)  18.3 us
    all_to_all x2, waiting for transfers between devices, shared_sum(): pieces = lax.all_to_all(pieces, 'dp', 0, 0, tiled=True)  11.4 us
  transfers between devices with their start and end apart: 30, of which 11 were waited for; matrix products, arithmetic and copies ran while one was open for 10% of the time, Pallas kernels for 26%

profile of v2, /device:TPU:0, one launch (start us, length us, event | category | flops | bytes accessed | tf_op | source)
XLA Modules:
  0.0 524.6 jit_solution(6662459052814180380)
XLA Ops:
  12.8 6.5 %all-to-all-start = ((bf16[4,208,896]{2,1,0:T(8,128)(2,1)}), bf16[4,208,896]{2,1,0:T(8,128)(2,1)}, u32[]{:S(2)}, u32[]{:S(2)}) async-start(bf16[4,208,896]{2,1,0:T(8,128)(2,1)} %bitcast.5), calls=%async_computation | async-start | bytes 2981888 | tf_op jit(solution)/shard_map/all_to_all | solution.py:833
  32.2 3.6 slice_bitcast_fusion
  35.8 3.9 pad_add_fusion
  39.8 3.8 pad_add_fusion.1
  43.6 11.0 %all-to-all-done.x_ref = bf16[4,208,896]{2,1,0:T(8,128)(2,1)} async-done(((bf16[4,208,896]{2,1,0:T(8,128)(2,1)}), bf16[4,208,896]{2,1,0:T(8,128)(2,1)}, u32[]{:S(2)}, u32[]{:S(2)}) %all-to-all-start) | async-done | bytes 1490976 | tf_op jit(solution)/shard_map/all_to_all | solution.py:833
  54.6 4.8 shard_map.135
  61.5 9.4 %all-gather.8 = f32[8,3,512]{2,1,0:T(4,128)S(1)} all-gather(f32[1,3,512]{2,1,0:T(4,128)} %bitcast.136), channel_id=2, replica_groups=mesh['dp'=8,'branch'=4] {'dp'}, dimensions={0}, use_global_device_ids=true | all-gather | bytes 55296 | tf_op jit(solution)/shard_map/all_gather | solution.py:873
  71.0 3.2 collective-permute-start.5
  75.5 14.7 %collective-permute-done.5.refs_7_ = f32[3,512]{1,0:T(4,128)S(1)} collective-permute-done((f32[3,512]{1,0:T(4,128)S(1)}, f32[3,512]{1,0:T(4,128)S(1)}, u32[]{:S(2)}, u32[]{:S(2)}) %collective-permute-start.5) | collective-permute-done | bytes 6176 | tf_op jit(solution)/shard_map/ppermute | solution.py:792
  90.2 10.1 %collective-permute-start.3 = (f32[3,512]{1,0:T(4,128)S(1)}, f32[3,512]{1,0:T(4,128)S(1)}, u32[]{:S(2)}, u32[]{:S(2)}) collective-permute-start(f32[3,512]{1,0:T(4,128)S(1)} %reduce_sum.45.refs_4_), channel_id=1, source_target_pairs={{0,1},{1,2},{2,3},{3,0},{4,5},{5,6},{6,7},{7,4},{8,9},{9,10},{10,1... | collective-permute-start | bytes 18440 | tf_op jit(solution)/shard_map/ppermute | solution.py:792
  110.4 3.3 collective-permute-start.8
  113.7 5.0 collective-permute-done.11.refs_3_
  118.7 7.2 %collective-permute-start.6 = (bf16[912,256]{1,0:T(8,128)(2,1)S(1)}, bf16[912,256]{1,0:T(8,128)(2,1)S(1)}, u32[]{:S(2)}, u32[]{:S(2)}) collective-permute-start(bf16[912,256]{1,0:T(8,128)(2,1)S(1)} %copy-done.9), channel_id=1, source_target_pairs={{0,1},{1,2},{2,3},{3,0},{4,5},{5,6},{6,7},{7,4},{8,9},{9,10},{10,1... | collective-permute-start | bytes 1400840 | tf_op jit(solution)/shard_map/ppermute | solution.py:792
  125.9 38.5 %shard_map.137 = (bf16[3584,256]{1,0:T(8,128)(2,1)}, bf16[4352,768]{1,0:T(8,128)(2,1)}, f32[3584,512]{1,0:T(8,128)}, f32[2,512]{1,0:T(2,128)}, f32[3,512]{1,0:T(4,128)}) custom-call(s32[1]{0:T(128)} %copy.66.length_ref, s32[1]{0:T(128)} %bitcast.place_ref, bf16[912,256]{1,0:T(8,128)(2,1)} %get-tuple-element.61.refs_0_, ...), custom_call_target="tpu_custom_call" | custom-call | flops 20000000000 | bytes 16777216 | tf_op jit(solution)/shard_map/pallas_call | solution.py:45
  165.8 4.1 shard_map.136
  170.6 10.1 %all-gather.9.refs_7_ = f32[8,2,640]{2,1,0:T(2,128)} all-gather(f32[1,2,640]{2,1,0:T(2,128)S(1)} %maximum_bitcast_fusion), channel_id=3, replica_groups=mesh['dp'=8,'branch'=4] {'dp'}, dimensions={0}, use_global_device_ids=true | all-gather | bytes 46080 | tf_op jit(solution)/shard_map/all_gather | solution.py:901
  181.7 20.5 %shard_map.138 = (bf16[896,896]{1,0:T(8,128)(2,1)}, bf16[3584,896]{1,0:T(8,128)(2,1)}, bf16[3584,896]{1,0:T(8,128)(2,1)}, f32[3,896]{1,0:T(4,128)}, bf16[896,896]{1,0:T(8,128)(2,1)}, /*index=5*/bf16[896,896]{1,0:T(8,128)(2,1)}) custom-call(s32[1]{0:T(128)} %copy.66.length_ref, s32[1]{0:T(128)} %bitcast.place_ref, ...), custom_call_target="tpu_custom_call" | custom-call | flops 1000000000 | bytes 16777216 | tf_op jit(solution)/shard_map/pallas_call | solution.py:45
  202.2 5.5 %shard_map.139 = (f32[896,640]{1,0:T(8,128)}, f32[3,640]{1,0:T(4,128)}) custom-call(s32[1]{0:T(128)S(6)} %select_n.8.length_ref, f32[1]{0:T(128)S(6)} %mul.31.count_ref, bf16[896,896]{1,0:T(8,128)(2,1)} %get-tuple-element.70.x_ref.rest_5_, bf16[896,640]{1,0:T(8,128)(2,1)} %pad_maximum_fusion.1.p_ref.rest_6_), custom_call_target="tpu_custom_call" | custom-call | flops 1000000000 | bytes 16777216 | tf_op jit(solution)/shard_map/pallas_call | solution.py:45
  207.7 10.2 %all-gather.10.sums_in_ref = f32[8,3,640]{2,1,0:T(4,128)} all-gather(f32[1,3,640]{2,1,0:T(4,128)} %bitcast.133), channel_id=4, replica_groups=mesh['dp'=8,'branch'=4] {'dp'}, dimensions={0}, use_global_device_ids=true | all-gather | bytes 69120 | tf_op jit(solution)/shard_map/all_gather | solution.py:926
  217.9 13.5 %shard_map.140 = (bf16[896,256]{1,0:T(8,128)(2,1)}, bf16[1312,768]{1,0:T(8,128)(2,1)}, f32[896,512]{1,0:T(8,128)}, f32[2,512]{1,0:T(2,128)}, f32[3,640]{1,0:T(4,128)}) custom-call(s32[1]{0:T(128)S(6)} %select_n.8.length_ref, f32[896,640]{1,0:T(8,128)} %get-tuple-element.71.q_ref, f32[8,3,640]{2,1,0:T(4,128)} %all-gather.10.sums_in_ref, f32[1,256]{1,0:T(1,128)} %bitcast.130, ...), custom_call_target="tpu_custom_call" | custom-call | flops 1000000000 | bytes 16777216 | tf_op jit(solution)/shard_map/pallas_call | solution.py:45
  231.4 10.0 %all-gather.11.sums_in_ref = f32[8,2,512]{2,1,0:T(2,128)} all-gather(f32[1,2,512]{2,1,0:T(2,128)} %bitcast.142), channel_id=5, replica_groups=mesh['dp'=8,'branch'=4] {'dp'}, dimensions={0}, use_global_device_ids=true | all-gather | bytes 36864 | tf_op jit(solution)/shard_map/all_gather | solution.py:940
  241.4 7.3 %shard_map.141 = (bf16[896,896]{1,0:T(8,128)(2,1)}, bf16[896,896]{1,0:T(8,128)(2,1)}, bf16[896,896]{1,0:T(8,128)(2,1)}, f32[3,896]{1,0:T(4,128)}, f32[2,896]{1,0:T(2,128)}) custom-call(s32[1]{0:T(128)S(6)} %select_n.8.length_ref, f32[896,640]{1,0:T(8,128)} %get-tuple-element.71.q_ref, f32[896,512]{1,0:T(8,128)} %get-tuple-element.73.e_ref, ...), custom_call_target="tpu_custom_call" | custom-call | flops 1000000000 | bytes 16777216 | tf_op jit(solution)/shard_map/pallas_call | solution.py:45
  248.7 9.9 %all-gather.12.sums_in_ref = f32[8,2,896]{2,1,0:T(2,128)} all-gather(f32[1,2,896]{2,1,0:T(2,128)} %bitcast.138), channel_id=6, replica_groups=mesh['dp'=8,'branch'=4] {'dp'}, dimensions={0}, use_global_device_ids=true | all-gather | bytes 64512 | tf_op jit(solution)/shard_map/all_gather | solution.py:960
  258.6 3.8 shard_map.142
  262.4 12.3 %shard_map.143 = (bf16[896,256]{1,0:T(8,128)(2,1)}, f32[2,256]{1,0:T(2,128)}) custom-call(s32[1]{0:T(128)S(6)} %select_n.8.length_ref, bf16[1312,512]{1,0:T(8,128)(2,1)} %get-tuple-element.85.d_ref, bf16[9,768,512]{2,1,0:T(8,128)(2,1)} %bitcast.102, bf16[896,256]{1,0:T(8,128)(2,1)} %get-tuple-element.84.reduced_ref.rest_0_, f32[1,256]{1,0:T(1,128)} %bitcast.131, ...), custom_call_target="tpu_custom_call" | custom-call | flops 1000000000 | bytes 16777216 | tf_op jit(solution)/shard_map/pallas_call | solution.py:45
  274.7 9.6 %all-gather.13.rest_3_ = f32[8,2,256]{2,1,0:T(2,128)} all-gather(f32[1,2,256]{2,1,0:T(2,128)} %bitcast.160), channel_id=7, replica_groups=mesh['dp'=8,'branch'=4] {'dp'}, dimensions={0}, use_global_device_ids=true | all-gather | bytes 18432 | tf_op jit(solution)/shard_map/all_gather | solution.py:988
  284.3 5.5 %shard_map.149 = bf16[3072,128]{1,0:T(8,128)(2,1)} custom-call(s32[1]{0:T(128)S(6)} %mul.36.first_ref, bf16[1312,768]{1,0:T(8,128)(2,1)} %get-tuple-element.102.taps_ref, bf16[1312,512]{1,0:T(8,128)(2,1)} %get-tuple-element.85.d_ref), custom_call_target="tpu_custom_call" | custom-call | flops 1000000000 | bytes 16777216 | tf_op jit(solution)/shard_map/pallas_call | solution.py:45
  289.8 10.0 %shard_map.144 = (bf16[896,896]{1,0:T(8,128)(2,1)}, bf16[1152,128]{1,0:T(8,128)(2,1)}, f32[2,256]{1,0:T(2,128)}, f32[2,896]{1,0:T(2,128)}) custom-call(s32[1]{0:T(128)S(6)} %select_n.8.length_ref, s32[1]{0:T(128)} %bitcast.place_ref, bf16[896,896]{1,0:T(8,128)(2,1)} %get-tuple-element.79.h_ref, f32[3,896]{1,0:T(4,128)} %get-tuple-element.80.outer_ref, ...), custom_call_target="tpu_custom_call" | custom-call | flops 1000000000 | bytes 16777216 | tf_op jit(solution)/shard_map/pallas_call | solution.py:45
  300.9 18.3 %all_to_all.20 = bf16[8,528,128]{2,1,0:T(8,128)(2,1)S(1)} all-to-all(bf16[8,528,128]{2,1,0:T(8,128)(2,1)S(1)} %pad_maximum_fusion.2), channel_id=1, replica_groups=mesh['dp'=8,'branch'=4] {'dp'}, dimensions={0} | all-to-all | bytes 2162688 | tf_op jit(solution)/shard_map/all_to_all | solution.py:802
  321.8 9.4 %all-gather.14.sums_in_ref = f32[8,2,896]{2,1,0:T(2,128)} all-gather(f32[1,2,896]{2,1,0:T(2,128)S(1)} %bitcast.137), channel_id=8, replica_groups=mesh['dp'=8,'branch'=4] {'dp'}, dimensions={0}, use_global_device_ids=true | all-gather | bytes 64512 | tf_op jit(solution)/shard_map/all_gather | solution.py:960
  331.2 11.7 %shard_map.145 = (bf16[4352,512]{1,0:T(8,128)(2,1)}, f32[2,896]{1,0:T(2,128)}) custom-call(s32[1]{0:T(128)} %copy.66.length_ref, bf16[3584,896]{1,0:T(8,128)(2,1)} %get-tuple-element.77.h_ref, f32[3,896]{1,0:T(4,128)} %get-tuple-element.78.outer_ref, f32[8,2,896]{2,1,0:T(2,128)} %all-gather.14.sums_in_ref, f32[1,896]{1,0:T(1,128)} %reshape.147.refs_8_.gain_ref, ...), custom_call_target="tpu_custom_call" | custom-call | flops 1000000000 | bytes 16777216 | tf_op jit(solution)/shard_map/pallas_call | solution.py:45
  342.9 14.9 %shard_map.146 = bf16[3072,128]{1,0:T(8,128)(2,1)} custom-call(s32[1]{0:T(128)S(6)} %mul.36.first_ref, bf16[4352,768]{1,0:T(8,128)(2,1)} %get-tuple-element.96.taps_ref, bf16[4352,512]{1,0:T(8,128)(2,1)} %get-tuple-element.97.d_ref), custom_call_target="tpu_custom_call" | custom-call | flops 1000000000 | bytes 16777216 | tf_op jit(solution)/shard_map/pallas_call | solution.py:45
  357.8 37.2 %shard_map.147 = (bf16[3584,256]{1,0:T(8,128)(2,1)}, f32[2,256]{1,0:T(2,128)}) custom-call(s32[1]{0:T(128)} %copy.66.length_ref, bf16[4352,512]{1,0:T(8,128)(2,1)} %get-tuple-element.97.d_ref, bf16[9,768,512]{2,1,0:T(8,128)(2,1)} %bitcast.107, bf16[3584,256]{1,0:T(8,128)(2,1)} %get-tuple-element.94.reduced_ref.rest_1_, f32[1,256]{1,0:T(1,128)} %bitcast.140, ...), custom_call_target="tpu_custom_call" | custom-call | flops 20000000000 | bytes 16777216 | tf_op jit(solution)/shard_map/pallas_call | solution.py:45
  395.0 9.8 %all-gather.15.rest_4_ = f32[8,2,256]{2,1,0:T(2,128)} all-gather(f32[1,2,256]{2,1,0:T(2,128)} %bitcast.159), channel_id=9, replica_groups=mesh['dp'=8,'branch'=4] {'dp'}, dimensions={0}, use_global_device_ids=true | all-gather | bytes 18432 | tf_op jit(solution)/shard_map/all_gather | solution.py:988
  404.8 17.5 %shard_map.148 = (bf16[3584,208]{1,0:T(8,128)(2,1)}, bf16[1152,128]{1,0:T(8,128)(2,1)}, f32[2,256]{1,0:T(2,128)}) custom-call(s32[1]{0:T(128)} %copy.66.length_ref, s32[1]{0:T(128)} %bitcast.place_ref, bf16[3584,896]{1,0:T(8,128)(2,1)} %get-tuple-element.77.h_ref, f32[3,896]{1,0:T(4,128)} %get-tuple-element.78.outer_ref, ...), custom_call_target="tpu_custom_call" | custom-call | flops 1000000000 | bytes 16777216 | tf_op jit(solution)/shard_map/pallas_call | solution.py:45
  422.3 3.6 all-to-all-start.1
  426.8 6.4 %all-to-all-done.1 = bf16[8,144,128]{2,1,0:T(8,128)(2,1)S(1)} async-done(((bf16[8,144,128]{2,1,0:T(8,128)(2,1)}), bf16[8,144,128]{2,1,0:T(8,128)(2,1)S(1)}, u32[]{:S(2)}, u32[]{:S(2)}) %all-to-all-start.1) | async-done | bytes 294944 | tf_op jit(solution)/shard_map/all_to_all | solution.py:802
  433.1 3.5 all-to-all-start.3
  444.2 5.0 all-to-all-done.3
  452.0 3.5 collective-permute-done.21
  455.9 2.6 collective-permute-done.20
  458.5 2.9 collective-permute-start.22
  462.1 7.6 %collective-permute-done.22 = bf16[1536,128]{1,0:T(8,128)(2,1)S(1)} collective-permute-done((bf16[1536,128]{1,0:T(8,128)(2,1)S(1)}, bf16[1536,128]{1,0:T(8,128)(2,1)S(1)}, u32[]{:S(2)}, u32[]{:S(2)}) %collective-permute-start.22) | collective-permute-done | bytes 393248 | tf_op jit(solution)/shard_map/ppermute | solution.py:811
  471.4 8.5 %collective-permute-done.24 = bf16[1536,128]{1,0:T(8,128)(2,1)S(1)} collective-permute-done((bf16[1536,128]{1,0:T(8,128)(2,1)S(1)}, bf16[1536,128]{1,0:T(8,128)(2,1)S(1)}, u32[]{:S(2)}, u32[]{:S(2)}) %collective-permute-start.24) | collective-permute-done | bytes 393248 | tf_op jit(solution)/shard_map/ppermute | solution.py:811
  485.5 3.8 collective-permute-done.15
  497.7 8.1 %shard_map.150 = (f32[2,27,160,320]{3,2,1,0:T(8,128)}, f32[2,27,32,128]{3,2,1,0:T(8,128)}, f32[2,576,832]{2,1,0:T(8,128)}) custom-call(bf16[4,4224,128]{2,1,0:T(8,128)(2,1)} %pad_maximum_fusion.buffer_ref), custom_call_target="tpu_custom_call" | custom-call | flops 1000000000 | bytes 16777216 | tf_op jit(solution)/shard_map/pallas_call | solution.py:45
  505.8 3.0 shard_map.151
  510.0 7.2 %shard_map.152 = (f32[2,27,160,320]{3,2,1,0:T(8,128)}, f32[2,27,32,128]{3,2,1,0:T(8,128)}) custom-call(s32[1]{0:T(128)} %bitcast.place_ref, s32[1]{0:T(128)} %bitcast.48.clip_ref, bf16[6144,128]{1,0:T(8,128)(2,1)} %copy-done.5, bf16[6144,128]{1,0:T(8,128)(2,1)} %copy-done.6, ...), custom_call_target="tpu_custom_call", output_to_operand_aliasing={{0}: (4, {}), {1}: (5, {})} | custom-call | flops 1000000000 | bytes 16777216 | tf_op jit(solution)/shard_map/pallas_call | solution.py:45
  (194 shorter events, 66.9 us)
Async XLA Ops:
  12.8 6.6 %copy-start.16 = (f32[2,1024]{1,0:T(2,128)S(1)}, f32[2,1024]{1,0:T(2,128)}, u32[]{:S(2)}) copy-start(f32[2,1024]{1,0:T(2,128)} %param.14) | copy-start | bytes 24580
  12.8 6.6 %copy-start.8 = (bf16[1,8,7,7,832]{4,1,3,2,0:T(8,128)(2,1)S(1)}, bf16[1,8,7,7,832]{4,1,3,2,0:T(8,128)(2,1)}, u32[]{:S(2)}) copy-start(bf16[1,8,7,7,832]{4,1,3,2,0:T(8,128)(2,1)} %param.10) | copy-start | bytes 1956868
  12.8 41.8 %all-to-all-start = ((bf16[4,208,896]{2,1,0:T(8,128)(2,1)}), bf16[4,208,896]{2,1,0:T(8,128)(2,1)}, u32[]{:S(2)}, u32[]{:S(2)}) async-start(bf16[4,208,896]{2,1,0:T(8,128)(2,1)} %bitcast.5), calls=%async_computation | async-start | bytes 2981888 | tf_op jit(solution)/shard_map/all_to_all | solution.py:833
  19.3 472.5 %all-gather.18.cloned.1.call-start = ((), (), s32[]{:S(2)}) async-start(), calls=%async_computation.4 | async-start | bytes 4460544 | tf_op jit(solution)/shard_map/all_gather | solution.py:1043
  59.4 46.2 %copy-start.2 = (bf16[8,7,7,896]{3,0,2,1:T(8,128)(2,1)S(1)}, bf16[8,7,7,896]{3,0,2,1:T(8,128)(2,1)}, u32[]{:S(2)}) copy-start(bf16[8,7,7,896]{3,0,2,1:T(8,128)(2,1)} %pad_maximum_fusion.5) | copy-start | bytes 2107396
  59.4 47.6 %collective-permute-start.2 = (bf16[912,256]{1,0:T(8,128)(2,1)}, bf16[912,256]{1,0:T(8,128)(2,1)S(1)}, u32[]{:S(2)}, u32[]{:S(2)}) collective-permute-start(bf16[912,256]{1,0:T(8,128)(2,1)} %get-tuple-element.61.refs_0_), channel_id=1, source_target_pairs={{0,3},{1,0},{2,1},{3,2},{4,7},{5,4},{6,5},{7,6},{8,11},{9,8},{10,9... | collective-permute-start | bytes 1400840 | tf_op jit(solution)/shard_map/ppermute | solution.py:792
  60.8 46.2 %collective-permute-start.1 = (bf16[912,256]{1,0:T(8,128)(2,1)}, bf16[912,256]{1,0:T(8,128)(2,1)}, u32[]{:S(2)}, u32[]{:S(2)}) collective-permute-start(bf16[912,256]{1,0:T(8,128)(2,1)} %get-tuple-element.61.refs_0_), channel_id=1, source_target_pairs={{0,2},{1,3},{2,0},{3,1},{4,6},{5,7},{6,4},{7,5},{8,10},{9,11},{10,... | collective-permute-start | bytes 1400840 | tf_op jit(solution)/shard_map/ppermute | solution.py:792
  60.8 46.2 %collective-permute-start = (bf16[912,256]{1,0:T(8,128)(2,1)}, bf16[912,256]{1,0:T(8,128)(2,1)}, u32[]{:S(2)}, u32[]{:S(2)}) collective-permute-start(bf16[912,256]{1,0:T(8,128)(2,1)} %get-tuple-element.61.refs_0_), channel_id=1, source_target_pairs={{0,1},{1,2},{2,3},{3,0},{4,5},{5,6},{6,7},{7,4},{8,9},{9,10},{10,1... | collective-permute-start | bytes 1400840 | tf_op jit(solution)/shard_map/ppermute | solution.py:792
  70.9 34.7 %copy-start.18 = (f32[3,512]{1,0:T(4,128)}, f32[3,512]{1,0:T(4,128)S(1)}, u32[]{:S(2)}) copy-start(f32[3,512]{1,0:T(4,128)S(1)} %reduce_sum.45.refs_4_) | copy-start | bytes 18436
  71.0 19.2 %collective-permute-start.5 = (f32[3,512]{1,0:T(4,128)S(1)}, f32[3,512]{1,0:T(4,128)S(1)}, u32[]{:S(2)}, u32[]{:S(2)}) collective-permute-start(f32[3,512]{1,0:T(4,128)S(1)} %reduce_sum.45.refs_4_), channel_id=1, source_target_pairs={{0,3},{1,0},{2,1},{3,2},{4,7},{5,4},{6,5},{7,6},{8,11},{9,8},{10,9... | collective-permute-start | bytes 18440 | tf_op jit(solution)/shard_map/ppermute | solution.py:792
  74.3 32.7 %collective-permute-start.4 = (f32[3,512]{1,0:T(4,128)S(1)}, f32[3,512]{1,0:T(4,128)S(1)}, u32[]{:S(2)}, u32[]{:S(2)}) collective-permute-start(f32[3,512]{1,0:T(4,128)S(1)} %reduce_sum.45.refs_4_), channel_id=1, source_target_pairs={{0,2},{1,3},{2,0},{3,1},{4,6},{5,7},{6,4},{7,5},{8,10},{9,11},{10,... | collective-permute-start | bytes 18440 | tf_op jit(solution)/shard_map/ppermute | solution.py:792
  90.2 15.4 %copy-start.27 = (f32[3,512]{1,0:T(4,128)}, f32[3,512]{1,0:T(4,128)S(1)}, u32[]{:S(2)}) copy-start(f32[3,512]{1,0:T(4,128)S(1)} %collective-permute-done.5.refs_7_) | copy-start | bytes 18436
  90.2 16.8 %collective-permute-start.3 = (f32[3,512]{1,0:T(4,128)S(1)}, f32[3,512]{1,0:T(4,128)S(1)}, u32[]{:S(2)}, u32[]{:S(2)}) collective-permute-start(f32[3,512]{1,0:T(4,128)S(1)} %reduce_sum.45.refs_4_), channel_id=1, source_target_pairs={{0,1},{1,2},{2,3},{3,0},{4,5},{5,6},{6,7},{7,4},{8,9},{9,10},{10,1... | collective-permute-start | bytes 18440 | tf_op jit(solution)/shard_map/ppermute | solution.py:792
  107.0 18.9 %copy-start.28 = (f32[3,512]{1,0:T(4,128)}, f32[3,512]{1,0:T(4,128)S(1)}, u32[]{:S(2)}) copy-start(f32[3,512]{1,0:T(4,128)S(1)} %collective-permute-done.4.refs_6_) | copy-start | bytes 18436
  107.0 18.9 %copy-start.29 = (f32[3,512]{1,0:T(4,128)}, f32[3,512]{1,0:T(4,128)S(1)}, u32[]{:S(2)}) copy-start(f32[3,512]{1,0:T(4,128)S(1)} %collective-permute-done.3.refs_5_) | copy-start | bytes 18436
  107.0 18.9 %copy-start.22 = (bf16[912,256]{1,0:T(8,128)(2,1)}, bf16[912,256]{1,0:T(8,128)(2,1)S(1)}, u32[]{:S(2)}) copy-start(bf16[912,256]{1,0:T(8,128)(2,1)S(1)} %collective-permute-done.2.refs_3_) | copy-start | bytes 1400836
  107.1 11.7 %collective-permute-start.11 = (bf16[912,128]{1,0:T(8,128)(2,1)S(1)}, bf16[912,128]{1,0:T(8,128)(2,1)S(1)}, u32[]{:S(2)}, u32[]{:S(2)}) collective-permute-start(bf16[912,128]{1,0:T(8,128)(2,1)S(1)} %copy-done.23), channel_id=1, source_target_pairs={{0,3},{1,0},{2,1},{3,2},{4,7},{5,4},{6,5},{7,6},{8,11},{9,8},{10,9... | collective-permute-start | bytes 700424 | tf_op jit(solution)/shard_map/ppermute | solution.py:792
  108.4 56.0 %collective-permute-start.10 = (bf16[912,128]{1,0:T(8,128)(2,1)S(1)}, bf16[912,128]{1,0:T(8,128)(2,1)S(1)}, u32[]{:S(2)}, u32[]{:S(2)}) collective-permute-start(bf16[912,128]{1,0:T(8,128)(2,1)S(1)} %copy-done.23), channel_id=1, source_target_pairs={{0,2},{1,3},{2,0},{3,1},{4,6},{5,7},{6,4},{7,5},{8,10},{9,11},{10,... | collective-permute-start | bytes 700424 | tf_op jit(solution)/shard_map/ppermute | solution.py:792
  109.9 54.6 %collective-permute-start.9 = (bf16[912,128]{1,0:T(8,128)(2,1)S(1)}, bf16[912,128]{1,0:T(8,128)(2,1)S(1)}, u32[]{:S(2)}, u32[]{:S(2)}) collective-permute-start(bf16[912,128]{1,0:T(8,128)(2,1)S(1)} %copy-done.23), channel_id=1, source_target_pairs={{0,1},{1,2},{2,3},{3,0},{4,5},{5,6},{6,7},{7,4},{8,9},{9,10},{10,1... | collective-permute-start | bytes 700424 | tf_op jit(solution)/shard_map/ppermute | solution.py:792
  110.4 70.2 %collective-permute-start.8 = (bf16[912,256]{1,0:T(8,128)(2,1)S(1)}, bf16[912,256]{1,0:T(8,128)(2,1)S(1)}, u32[]{:S(2)}, u32[]{:S(2)}) collective-permute-start(bf16[912,256]{1,0:T(8,128)(2,1)S(1)} %copy-done.9), channel_id=1, source_target_pairs={{0,3},{1,0},{2,1},{3,2},{4,7},{5,4},{6,5},{7,6},{8,11},{9,8},{10,9... | collective-permute-start | bytes 1400840 | tf_op jit(solution)/shard_map/ppermute | solution.py:792
  113.7 67.0 %collective-permute-start.7 = (bf16[912,256]{1,0:T(8,128)(2,1)S(1)}, bf16[912,256]{1,0:T(8,128)(2,1)S(1)}, u32[]{:S(2)}, u32[]{:S(2)}) collective-permute-start(bf16[912,256]{1,0:T(8,128)(2,1)S(1)} %copy-done.9), channel_id=1, source_target_pairs={{0,2},{1,3},{2,0},{3,1},{4,6},{5,7},{6,4},{7,5},{8,10},{9,11},{10,... | collective-permute-start | bytes 1400840 | tf_op jit(solution)/shard_map/ppermute | solution.py:792
  118.7 45.7 %copy-start.24 = (bf16[912,128]{1,0:T(8,128)(2,1)}, bf16[912,128]{1,0:T(8,128)(2,1)S(1)}, u32[]{:S(2)}) copy-start(bf16[912,128]{1,0:T(8,128)(2,1)S(1)} %collective-permute-done.11.refs_3_) | copy-start | bytes 700420
  118.7 61.9 %collective-permute-start.6 = (bf16[912,256]{1,0:T(8,128)(2,1)S(1)}, bf16[912,256]{1,0:T(8,128)(2,1)S(1)}, u32[]{:S(2)}, u32[]{:S(2)}) collective-permute-start(bf16[912,256]{1,0:T(8,128)(2,1)S(1)} %copy-done.9), channel_id=1, source_target_pairs={{0,1},{1,2},{2,3},{3,0},{4,5},{5,6},{6,7},{7,4},{8,9},{9,10},{10,1... | collective-permute-start | bytes 1400840 | tf_op jit(solution)/shard_map/ppermute | solution.py:792
  164.4 5.5 %copy-start.20 = (f32[2,512]{1,0:T(2,128)S(1)}, f32[2,512]{1,0:T(2,128)}, u32[]{:S(2)}) copy-start(f32[2,512]{1,0:T(2,128)} %get-tuple-element.68) | copy-start | bytes 12292
  289.8 10.0 %copy-start.1 = (bf16[3072,128]{1,0:T(8,128)(2,1)S(1)}, bf16[3072,128]{1,0:T(8,128)(2,1)}, u32[]{:S(2)}) copy-start(bf16[3072,128]{1,0:T(8,128)(2,1)} %shard_map.149) | copy-start | bytes 2359300
  300.9 20.9 %copy-start.19 = (f32[2,896]{1,0:T(2,128)S(1)}, f32[2,896]{1,0:T(2,128)}, u32[]{:S(2)}) copy-start(f32[2,896]{1,0:T(2,128)} %get-tuple-element.90) | copy-start | bytes 21508
  404.8 21.1 %copy-start.14 = (f32[2,896]{1,0:T(2,128)S(1)}, f32[2,896]{1,0:T(2,128)}, u32[]{:S(2)}) copy-start(f32[2,896]{1,0:T(2,128)} %get-tuple-element.83.total_ref) | copy-start | bytes 21508
  404.8 21.1 %copy-start.15 = (f32[2,896]{1,0:T(2,128)S(1)}, f32[2,896]{1,0:T(2,128)}, u32[]{:S(2)}) copy-start(f32[2,896]{1,0:T(2,128)} %get-tuple-element.93.total_ref) | copy-start | bytes 21508
  404.8 21.2 %copy-start.21 = (f32[2,256]{1,0:T(2,128)S(1)}, f32[2,256]{1,0:T(2,128)}, u32[]{:S(2)}) copy-start(f32[2,256]{1,0:T(2,128)} %get-tuple-element.110) | copy-start | bytes 6148
  422.3 14.4 %copy-start.13 = (bf16[896,896]{1,0:T(8,128)(2,1)S(1)}, bf16[896,896]{1,0:T(8,128)(2,1)}, u32[]{:S(2)}) copy-start(bf16[896,896]{1,0:T(8,128)(2,1)} %get-tuple-element.76) | copy-start | bytes 4816900
  422.3 10.8 %all-to-all-start.1 = ((bf16[8,144,128]{2,1,0:T(8,128)(2,1)}), bf16[8,144,128]{2,1,0:T(8,128)(2,1)S(1)}, u32[]{:S(2)}, u32[]{:S(2)}) async-start(bf16[8,144,128]{2,1,0:T(8,128)(2,1)} %bitcast.124), calls=%async_computation.1 | async-start | bytes 589824 | tf_op jit(solution)/shard_map/all_to_all | solution.py:802
  433.1 16.1 %all-to-all-start.3 = ((bf16[8,384,128]{2,1,0:T(8,128)(2,1)}), bf16[8,384,128]{2,1,0:T(8,128)(2,1)S(1)}, u32[]{:S(2)}, u32[]{:S(2)}) async-start(bf16[8,384,128]{2,1,0:T(8,128)(2,1)} %bitcast.56), calls=%async_computation.3 | async-start | bytes 1572864 | tf_op jit(solution)/shard_map/all_to_all | solution.py:802
  436.8 3.7 copy-start.4
  442.6 37.5 %collective-permute-start.14 = (bf16[144,128]{1,0:T(8,128)(2,1)S(1)}, bf16[144,128]{1,0:T(8,128)(2,1)S(1)}, u32[]{:S(2)}, u32[]{:S(2)}) collective-permute-start(bf16[144,128]{1,0:T(8,128)(2,1)S(1)} %reduce_sum.46), channel_id=1, source_target_pairs={{0,3},{1,0},{2,1},{3,2},{4,7},{5,4},{6,5},{7,6},{8,11},{9,8},{10,9... | collective-permute-start | bytes 110600 | tf_op jit(solution)/shard_map/ppermute | solution.py:792
  442.6 37.4 %collective-permute-start.13 = (bf16[144,128]{1,0:T(8,128)(2,1)S(1)}, bf16[144,128]{1,0:T(8,128)(2,1)S(1)}, u32[]{:S(2)}, u32[]{:S(2)}) collective-permute-start(bf16[144,128]{1,0:T(8,128)(2,1)S(1)} %reduce_sum.46), channel_id=1, source_target_pairs={{0,2},{1,3},{2,0},{3,1},{4,6},{5,7},{6,4},{7,5},{8,10},{9,11},{10,... | collective-permute-start | bytes 110600 | tf_op jit(solution)/shard_map/ppermute | solution.py:792
  449.3 6.2 %collective-permute-start.21 = (bf16[384,128]{1,0:T(8,128)(2,1)S(1)}, bf16[384,128]{1,0:T(8,128)(2,1)S(1)}, u32[]{:S(2)}, u32[]{:S(2)}) collective-permute-start(bf16[384,128]{1,0:T(8,128)(2,1)S(1)} %reduce_sum.48), channel_id=1, source_target_pairs={{0,3},{1,0},{2,1},{3,2},{4,7},{5,4},{6,5},{7,6},{8,11},{9,8},{10,9... | collective-permute-start | bytes 294920 | tf_op jit(solution)/shard_map/ppermute | solution.py:792
  449.4 9.1 %collective-permute-start.20 = (bf16[384,128]{1,0:T(8,128)(2,1)S(1)}, bf16[384,128]{1,0:T(8,128)(2,1)S(1)}, u32[]{:S(2)}, u32[]{:S(2)}) collective-permute-start(bf16[384,128]{1,0:T(8,128)(2,1)S(1)} %reduce_sum.48), channel_id=1, source_target_pairs={{0,2},{1,3},{2,0},{3,1},{4,6},{5,7},{6,4},{7,5},{8,10},{9,11},{10,... | collective-permute-start | bytes 294920 | tf_op jit(solution)/shard_map/ppermute | solution.py:792
  451.0 7.5 %collective-permute-start.19 = (bf16[384,128]{1,0:T(8,128)(2,1)S(1)}, bf16[384,128]{1,0:T(8,128)(2,1)S(1)}, u32[]{:S(2)}, u32[]{:S(2)}) collective-permute-start(bf16[384,128]{1,0:T(8,128)(2,1)S(1)} %reduce_sum.48), channel_id=1, source_target_pairs={{0,1},{1,2},{2,3},{3,0},{4,5},{5,6},{6,7},{7,4},{8,9},{9,10},{10,1... | collective-permute-start | bytes 294920 | tf_op jit(solution)/shard_map/ppermute | solution.py:792
  455.5 24.5 %collective-permute-start.12 = (bf16[144,128]{1,0:T(8,128)(2,1)S(1)}, bf16[144,128]{1,0:T(8,128)(2,1)S(1)}, u32[]{:S(2)}, u32[]{:S(2)}) collective-permute-start(bf16[144,128]{1,0:T(8,128)(2,1)S(1)} %reduce_sum.46), channel_id=1, source_target_pairs={{0,1},{1,2},{2,3},{3,0},{4,5},{5,6},{6,7},{7,4},{8,9},{9,10},{10,1... | collective-permute-start | bytes 110600 | tf_op jit(solution)/shard_map/ppermute | solution.py:792
  458.5 11.2 %collective-permute-start.22 = (bf16[1536,128]{1,0:T(8,128)(2,1)S(1)}, bf16[1536,128]{1,0:T(8,128)(2,1)S(1)}, u32[]{:S(2)}, u32[]{:S(2)}) collective-permute-start(bf16[1536,128]{1,0:T(8,128)(2,1)S(1)} %pad_maximum_fusion.7), channel_id=1, source_target_pairs={{0,8},{4,12},{8,0},{12,4},{16,24},{20,28},{24,16},{28,20},{1,9},{5... | collective-permute-start | bytes 1179656 | tf_op jit(solution)/shard_map/ppermute | solution.py:811
  461.4 9.9 %collective-permute-start.23 = (bf16[1536,128]{1,0:T(8,128)(2,1)S(1)}, bf16[1536,128]{1,0:T(8,128)(2,1)S(1)}, u32[]{:S(2)}, u32[]{:S(2)}) collective-permute-start(bf16[1536,128]{1,0:T(8,128)(2,1)S(1)} %pad_maximum_fusion.7), channel_id=1, source_target_pairs={{0,16},{4,20},{8,24},{12,28},{16,0},{20,4},{24,8},{28,12},{1,17},{... | collective-permute-start | bytes 1179656 | tf_op jit(solution)/shard_map/ppermute | solution.py:811
  469.7 10.2 %collective-permute-start.24 = (bf16[1536,128]{1,0:T(8,128)(2,1)S(1)}, bf16[1536,128]{1,0:T(8,128)(2,1)S(1)}, u32[]{:S(2)}, u32[]{:S(2)}) collective-permute-start(bf16[1536,128]{1,0:T(8,128)(2,1)S(1)} %pad_maximum_fusion.7), channel_id=1, source_target_pairs={{0,24},{4,28},{8,16},{12,20},{16,8},{20,12},{24,0},{28,4},{1,25},{... | collective-permute-start | bytes 1179656 | tf_op jit(solution)/shard_map/ppermute | solution.py:811
  479.9 13.2 %copy-start.5 = (bf16[6144,128]{1,0:T(8,128)(2,1)}, bf16[6144,128]{1,0:T(8,128)(2,1)S(1)}, u32[]{:S(2)}) copy-start(bf16[6144,128]{1,0:T(8,128)(2,1)S(1)} %constant_dynamic-update-slice_fusion.7.mine_ref) | copy-start | bytes 4718596
  480.0 28.9 %collective-permute-start.25 = (bf16[6144,128]{1,0:T(8,128)(2,1)S(1)}, bf16[6144,128]{1,0:T(8,128)(2,1)S(1)}, u32[]{:S(2)}, u32[]{:S(2)}) collective-permute-start(bf16[6144,128]{1,0:T(8,128)(2,1)S(1)} %constant_dynamic-update-slice_fusion.7.mine_ref), channel_id=1, source_target_pairs={{0,4},{4,0},{8,12},{12,8},{16,20},{20,16},{24,28},{28,24},{1,5},{5... | collective-permute-start | bytes 4718600 | tf_op jit(solution)/shard_map/ppermute | solution.py:813
  480.1 11.0 %collective-permute-start.17 = (bf16[576,128]{1,0:T(8,128)(2,1)S(1)}, bf16[576,128]{1,0:T(8,128)(2,1)S(1)}, u32[]{:S(2)}, u32[]{:S(2)}) collective-permute-start(bf16[576,128]{1,0:T(8,128)(2,1)S(1)} %pad_maximum_fusion.8), channel_id=1, source_target_pairs={{0,24},{4,28},{8,16},{12,20},{16,8},{20,12},{24,0},{28,4},{1,25},{... | collective-permute-start | bytes 442376 | tf_op jit(solution)/shard_map/ppermute | solution.py:811
  481.4 9.1 %collective-permute-start.16 = (bf16[576,128]{1,0:T(8,128)(2,1)S(1)}, bf16[576,128]{1,0:T(8,128)(2,1)S(1)}, u32[]{:S(2)}, u32[]{:S(2)}) collective-permute-start(bf16[576,128]{1,0:T(8,128)(2,1)S(1)} %pad_maximum_fusion.8), channel_id=1, source_target_pairs={{0,16},{4,20},{8,24},{12,28},{16,0},{20,4},{24,8},{28,12},{1,17},{... | collective-permute-start | bytes 442376 | tf_op jit(solution)/shard_map/ppermute | solution.py:811
  483.1 6.2 %collective-permute-start.15 = (bf16[576,128]{1,0:T(8,128)(2,1)S(1)}, bf16[576,128]{1,0:T(8,128)(2,1)S(1)}, u32[]{:S(2)}, u32[]{:S(2)}) collective-permute-start(bf16[576,128]{1,0:T(8,128)(2,1)S(1)} %pad_maximum_fusion.8), channel_id=1, source_target_pairs={{0,8},{4,12},{8,0},{12,4},{16,24},{20,28},{24,16},{28,20},{1,9},{5... | collective-permute-start | bytes 442376 | tf_op jit(solution)/shard_map/ppermute | solution.py:811
  491.8 14.0 %collective-permute-start.18 = (bf16[2304,128]{1,0:T(8,128)(2,1)}, bf16[2304,128]{1,0:T(8,128)(2,1)}, u32[]{:S(2)}, u32[]{:S(2)}) collective-permute-start(bf16[2304,128]{1,0:T(8,128)(2,1)} %constant_dynamic-update-slice_fusion.mine_ref), channel_id=1, source_target_pairs={{0,4},{4,0},{8,12},{12,8},{16,20},{20,16},{24,28},{28,24},{1,5},{5... | collective-permute-start | bytes 1769480 | tf_op jit(solution)/shard_map/ppermute | solution.py:813
  (12 other events, 20.0 us)
Sparse Core Ops, SparseCore 0:
  320.2 58.8 all-gather.17

commit v3 on v2

v3 whole, which is shorter than its diff:
```python
import functools

import jax
import jax.numpy as jnp
from jax import lax
from jax.experimental import pallas as pl
from jax.experimental.pallas import tpu as pltpu
from jax.sharding import PartitionSpec as P

DIRECT = 256
MID_IN = 160
MID_OUT = 320
SMALL_IN = 32
SMALL_OUT = 128
TAPS = 27
CHANNELS = 832
SQUEEZED = 576
PITCH = 16
REDUCED = 256
POOLED = 128
FIRST = 640
SECOND = 512
OUTER = 896
TAP_ROWS = 432
EPSILON = 1e-05
F32 = jnp.float32
BF16 = jnp.bfloat16
VMEM_BYTES = 58 * 2**20


def call(body, out_shape, scratch=(), scalars=0, flops=10**9, out_space=pltpu.VMEM, aliases=None, far=(), far_out=()):
    aliases = aliases or {}

    def run(*operands):
        specs = [
            pl.BlockSpec(
                memory_space=pl.ANY
                if number in aliases or number in far
                else pltpu.SMEM
                if number < scalars
                else pltpu.VMEM
            )
            for number in range(len(operands))
        ]
        if isinstance(out_shape, tuple):
            out_specs = tuple(
                pl.BlockSpec(memory_space=pl.ANY if number in far_out else out_space)
                for number in range(len(out_shape))
            )
        else:
            out_specs = pl.BlockSpec(memory_space=out_space)
        return pl.pallas_call(
            body,
            out_shape=out_shape,
            in_specs=specs,
            out_specs=out_specs,
            input_output_aliases=aliases,
            scratch_shapes=list(scratch),
            compiler_params=pltpu.CompilerParams(vmem_limit_bytes=VMEM_BYTES),
            cost_estimate=pl.CostEstimate(
                flops=flops, bytes_accessed=16 * 2**20, transcendentals=0
            ),
        )(*operands)

    return run


def shape(dims, dtype):
    return jax.ShapeDtypeStruct(tuple(dims), dtype)


def rows_at(start, size):
    return pl.ds(pl.multiple_of(start, 16), size)


def frames_of(rows, width=128):
    return lax.broadcasted_iota(jnp.int32, (rows, width), 0) & (PITCH - 1)


def frame_mask(rows, length, width=128):
    mask = jnp.where(frames_of(rows) < length, 1.0, 0.0)
    return jnp.concatenate([mask] * (width // 128), axis=1) if width > 128 else mask


def earlier(values):
    return jnp.where(frames_of(*values.shape) > 0, pltpu.roll(values, 1, 0), 0.0)


def later(values):
    rows = values.shape[0]
    return jnp.where(frames_of(*values.shape) < PITCH - 1, pltpu.roll(values, rows - 1, 0), 0.0)


def plane_box(values):
    across = values + earlier(values) + later(values)
    edge = jnp.zeros((PITCH, values.shape[1]), values.dtype)
    return (
        across
        + jnp.concatenate([across[PITCH:], edge], axis=0)
        + jnp.concatenate([edge, across[:-PITCH]], axis=0)
    )


def box_window(side, length):
    frame = frames_of(side * PITCH)
    place = lax.broadcasted_iota(jnp.int32, (side * PITCH, 128), 0) >> 4

    def one(condition):
        return jnp.where(condition, 1.0, 0.0)

    count = one(frame < length) + one(frame + 1 < length) + one((frame > 0) & (frame - 1 < length))
    return count * (3.0 - one(place == 0) - one(place == side - 1))


def box_scale(line, side, window):
    lines = 3.0 - jnp.where(line == 0, 1.0, 0.0) - jnp.where(line == side - 1, 1.0, 0.0)
    return 1.0 / jnp.maximum(window * lines, 1.0)


def sigmoid(value):
    return 0.5 * jnp.tanh(0.5 * value) + 0.5


def silu(value):
    return value * sigmoid(value)


def silu_slope(value):
    gate = sigmoid(value)
    return gate * (1.0 + value * (1.0 - gate))


def partial_sum(values):
    rows, width = values.shape
    return jnp.sum(values.reshape(rows // 8, 8, width), axis=0)


def moments(total, square, count):
    center = total / count
    return (center, lax.rsqrt(square / count - center * center + EPSILON))


def total_of(gathered):
    total = gathered[0]
    for number in range(1, gathered.shape[0]):
        total = total + gathered[number]
    return total


def pool_matrix(side, transposed):
    line = 2 * side * PITCH
    few, many = (side * PITCH, 2 * line)
    dims = (many, few) if transposed else (few, many)
    coarse = lax.broadcasted_iota(jnp.int32, dims, 1 if transposed else 0)
    fine = lax.broadcasted_iota(jnp.int32, dims, 0 if transposed else 1)
    fine = jnp.where(fine >= line, fine - line, fine)
    same = (fine >> 5 == coarse >> 4) & ((fine & (PITCH - 1)) >> 1 == coarse & (PITCH - 1))
    return jnp.where(same, 0.125, 0.0).astype(BF16)


class Grid:
    def __init__(self, side):
        self.side = side
        self.line_rows = side * PITCH
        self.rows = side * self.line_rows
        self.pitch = (side + 1) * PITCH
        self.lead = self.pitch + PITCH
        self.padded = (side + 2) * self.pitch + 2 * PITCH
        self.group = 2 if side % 2 == 0 else side


def zero_rows(ref):
    rows = ref.shape[0]
    step = 16
    while rows % (step * 2) == 0 and step < 256:
        step = step * 2

    @pl.loop(0, rows // step)
    def _(number):
        ref[rows_at(number * step, step), :] = jnp.zeros((step, ref.shape[1]), ref.dtype)


def store_taps(mid_ref, small_ref, at, act):
    before, after_ = (earlier(act), later(act))
    mid_ref[at, 0:128] = before[:, :128].astype(BF16)
    mid_ref[at, 128:256] = act[:, :128].astype(BF16)
    mid_ref[at, 256:384] = after_[:, :128].astype(BF16)
    before, act, after_ = (before[:, 128:], act[:, 128:], after_[:, 128:])
    lane = lax.broadcasted_iota(jnp.int32, act.shape, 1)
    mid_ref[at, 384:512] = jnp.where(
        lane < 32, before, jnp.where(lane < 64, pltpu.roll(act, 32, 1), pltpu.roll(after_, 64, 1))
    ).astype(BF16)
    small_ref[at, :] = jnp.where(
        lane < 32, pltpu.roll(before, 96, 1), jnp.where(lane < 64, act, pltpu.roll(after_, 32, 1))
    ).astype(BF16)


def tap_start(grid, base, tap, sign):
    return base + sign * ((tap // 3 - 1) * grid.pitch + (tap % 3 - 1) * PITCH)


def convolve(grid, taps, kernels, rest_ref, acc_ref, stage_ref, e_ref, stage_sem, sums_ref, length):
    mid_ref, small_ref = taps
    main_ref, last_ref, small_kernel_ref = kernels
    group_rows = grid.group * grid.pitch
    stage_rows = grid.group * grid.line_rows
    groups = grid.side // grid.group
    sums_ref[...] = jnp.zeros_like(sums_ref)
    mask = frame_mask(grid.line_rows, length, SECOND)
    edge = jnp.zeros((grid.pitch, 256), F32)
    rest_ref[PITCH : grid.lead, :] = edge
    end = grid.lead + grid.side * grid.pitch
    rest_ref[end : end + grid.pitch, :] = edge

    @pl.loop(0, groups)
    def _(group):
        base = grid.lead + group * group_rows
        total = None
        for place in range(3):
            part = jnp.dot(
                mid_ref[rows_at(base + (place - 1) * PITCH, group_rows), :],
                last_ref[place],
                preferred_element_type=F32,
            )
            total = part if total is None else total + part
        rest_ref[rows_at(base, group_rows), :] = total

    lane = lax.broadcasted_iota(jnp.int32, (grid.line_rows, 128), 1)

    def staged(group, slot):
        return pltpu.make_async_copy(
            stage_ref.at[slot],
            e_ref.at[rows_at(group * stage_rows, stage_rows), :],
            stage_sem.at[slot],
        )

    @pl.loop(0, groups)
    def _(group):
        base = grid.lead + group * group_rows
        slot = lax.rem(group, 2)
        for tap in range(9):
            part = jnp.dot(
                mid_ref[rows_at(tap_start(grid, base, tap, 1), group_rows), :],
                main_ref[tap],
                preferred_element_type=F32,
            )
            acc_ref[:, 0:256] = part if tap == 0 else acc_ref[:, 0:256] + part
        near = [small_ref[rows_at(tap_start(grid, base, tap, 1), group_rows), :] for tap in range(9)]
        acc_ref[:, 256:384] = jnp.dot(
            jnp.concatenate(near, axis=1), small_kernel_ref[...], preferred_element_type=F32
        )

        @pl.when(group >= 2)
        def _():
            staged(group - 2, slot).wait()

        for number in range(grid.group):
            rows = grid.line_rows
            start = base + number * grid.pitch
            last = (
                rest_ref[rows_at(start - grid.pitch, rows), 0:128]
                + pltpu.roll(rest_ref[rows_at(start, rows), 0:128], 64, 1)
                + rest_ref[rows_at(start + grid.pitch, rows), 128:256]
            )
            lines = slice(number * grid.pitch, number * grid.pitch + rows)
            values = jnp.concatenate(
                [acc_ref[lines, 0:256], jnp.where(lane < 64, last, 0.0), acc_ref[lines, 256:384]],
                axis=1,
            )
            stage_ref[slot, number * rows : (number + 1) * rows, :] = values
            masked = values * mask
            sums_ref[0:8] += partial_sum(masked)
            sums_ref[8:16] += partial_sum(masked * values)
        staged(group, slot).start()

    for group in range(max(groups - 2, 0), groups):
        staged(group, group % 2).wait()


def conv_scratch(grid):
    group_rows = grid.group * grid.pitch
    return [
        pltpu.VMEM((9, 512, 256), BF16),
        pltpu.VMEM((3, 512, 256), BF16),
        pltpu.VMEM((1152, 128), BF16),
        pltpu.VMEM((grid.padded, 512), BF16),
        pltpu.VMEM((grid.padded, 128), BF16),
        pltpu.VMEM((grid.rows, REDUCED), BF16),
        pltpu.VMEM((grid.padded, 256), F32),
        pltpu.VMEM((group_rows, 384), F32),
        pltpu.VMEM((2, grid.group * grid.line_rows, SECOND), F32),
        pltpu.VMEM((16, SECOND), F32),
        pltpu.SemaphoreType.DMA((3,)),
        pltpu.SemaphoreType.DMA((3,)),
        pltpu.SemaphoreType.DMA((2,)),
    ]


def conv_outputs(grid, width):
    return (
        shape((grid.rows, REDUCED), BF16),
        shape((grid.padded, 512), BF16),
        shape((grid.padded, 128), BF16),
        shape((grid.rows, SECOND), F32),
        shape((2, SECOND), F32),
        shape((3, width), F32),
    )


def copies(sources, targets, sem_ref):
    return [
        pltpu.make_async_copy(source, target, sem_ref.at[number])
        for number, (source, target) in enumerate(zip(sources, targets))
    ]


def run_convolution(grid, length, far_kernels, outputs, scratch, fill):
    h_out, mid_out, small_out, e_out, sums_out = outputs
    kernels, (mid_ref, small_ref, h_ref), rest = (scratch[:3], scratch[3:6], scratch[6:])
    rest_ref, acc_ref, stage_ref, sums_ref, in_sem, out_sem, stage_sem = rest
    arriving = copies(far_kernels, kernels, in_sem)
    for copy in arriving:
        copy.start()
    zero_rows(mid_ref)
    zero_rows(small_ref)
    fill(h_ref, mid_ref, small_ref)
    leaving = copies((mid_ref, small_ref, h_ref), (mid_out, small_out, h_out), out_sem)
    for copy in leaving:
        copy.start()
    for copy in arriving:
        copy.wait()
    convolve(
        grid, (mid_ref, small_ref), kernels, rest_ref, acc_ref, stage_ref, e_out, stage_sem, sums_ref, length
    )
    write_sums(sums_out, sums_ref, 0, SECOND)
    for copy in leaving:
        copy.wait()


def write_sums(out_ref, sums_ref, lo, hi):
    for number in range(2):
        out_ref[number : number + 1, lo:hi] = jnp.sum(
            sums_ref[8 * number : 8 * number + 8], axis=0, keepdims=True
        )


def first_pointwise(parts, length_ref, count_ref, x_ref, p_ref, mid_ref, rest_ref, u_ref):
    rows = u_ref.shape[0]
    step = 112 if rows % 112 == 0 else PITCH
    length, count = (length_ref[0], count_ref[0])
    for part in range(parts):
        product = lax.dot_general(
            x_ref[part], p_ref[part], (((0,), (1,)), ((), ())), preferred_element_type=F32
        )
        u_ref[...] = product if part == 0 else u_ref[...] + product
    mask = frame_mask(step, length, FIRST)

    def summed(number, carry):
        return carry + partial_sum(u_ref[rows_at(number * step, step), :] * mask)

    total = lax.fori_loop(0, rows // step, summed, jnp.zeros((8, FIRST), F32))
    total = jnp.sum(total, axis=0, keepdims=True)
    offset = (total / jnp.full((1, FIRST), jnp.maximum(count, 1.0), F32)).astype(BF16)
    wide_offset = offset.astype(F32)
    tail = jnp.broadcast_to(wide_offset, (PITCH, FIRST)).astype(BF16)
    places = ((rest_ref, 0, 0, DIRECT), (mid_ref, 0, DIRECT, SECOND), (rest_ref, DIRECT, SECOND, FIRST))
    for ref, at, lo, hi in places:
        ref[rows : rows + PITCH, at : at + hi - lo] = tail[:, lo:hi]

    @pl.loop(0, rows // step)
    def _(number):
        here = rows_at(number * step, step)
        values = u_ref[here, :] * mask - wide_offset
        for ref, at, lo, hi in places:
            ref[here, at : at + hi - lo] = values[:, lo:hi].astype(BF16)


def each_chunk(local_rows, parts, place, refs, visit):
    step = 112 if local_rows % 112 == 0 else PITCH
    for number, ref in enumerate(refs):
        source = lax.rem(place - number + parts, parts)
        offset = ref[local_rows : local_rows + PITCH, :].astype(F32)[0:1]

        @pl.loop(0, local_rows // step)
        def _(chunk):
            at = rows_at(chunk * step, step)
            visit(source * local_rows + chunk * step, step, ref[at, :].astype(F32) + offset)


def first_sums(local_rows, parts, place_ref, count_ref, *refs):
    mids, (out_sums_ref, sums_ref) = (refs[:parts], refs[parts:])
    sums_ref[...] = jnp.zeros_like(sums_ref)

    def visit(row, size, values):
        sums_ref[0:8] += partial_sum(values)
        sums_ref[8:16] += partial_sum(values * values)

    each_chunk(local_rows, parts, place_ref[0], mids, visit)
    write_sums(out_sums_ref, sums_ref, 0, REDUCED)
    out_sums_ref[2:3, :] = jnp.full((1, REDUCED), count_ref[0], F32)


def reduced_moments(sums_in_ref, moment_ref, lo, hi):
    total = total_of(sums_in_ref)
    count = total[2:3]
    center, inverse = moments(total[0:1], total[1:2], count)
    moment_ref[0:1, :] = center
    moment_ref[1:2, :] = inverse
    moment_ref[2:3, :] = count
    return (center[:, lo:hi], inverse[:, lo:hi])


def first_convolve(grid, block, local_rows, parts, length_ref, place_ref, *refs):
    mids, (sums_in_ref, gain_ref, shift_ref), refs = (refs[:parts], refs[parts : parts + 3], refs[parts + 3 :])
    far_kernels, outputs, moment_ref, scratch = (refs[:3], refs[3:8], refs[8], refs[9:])
    length = length_ref[0]
    center, inverse = reduced_moments(sums_in_ref, moment_ref, 0, REDUCED)
    gain, shift = (gain_ref[block : block + 1], shift_ref[block : block + 1])

    def fill(h_ref, mid_ref, small_ref):
        def visit(row, size, values):
            @pl.when(row < grid.rows)
            def _():
                scaled = (values - center) * inverse
                h_ref[rows_at(row, size), :] = scaled.astype(BF16)
                act = silu(gain * scaled + shift) * frame_mask(size, length, REDUCED)
                line = row // grid.line_rows
                at = grid.lead + line * grid.pitch + row - line * grid.line_rows
                store_taps(mid_ref, small_ref, rows_at(at, size), act)

        each_chunk(local_rows, parts, place_ref[0], mids, visit)

    run_convolution(grid, length, far_kernels, outputs, scratch, fill)


def pool_planes(grid, plane_ref, q_ref, lo, sums_ref, length, window):
    rows = grid.line_rows
    mask = frame_mask(rows, length)
    sums_ref[...] = jnp.zeros_like(sums_ref)

    @pl.loop(0, grid.side)
    def _(line):
        start = line * rows
        values = (
            plane_ref[rows_at(start, rows), :]
            + plane_ref[rows_at(start + rows, rows), :]
            + plane_ref[rows_at(start + 2 * rows, rows), :]
        ) * box_scale(line, grid.side, window)
        q_ref[rows_at(start, rows), lo : lo + POOLED] = values
        masked = values * mask
        sums_ref[0:8] += partial_sum(masked)
        sums_ref[8:16] += partial_sum(masked * values)


def clear_edges(grid, plane_ref):
    rows = grid.line_rows
    plane_ref[0:rows] = jnp.zeros((rows, POOLED), F32)
    plane_ref[grid.rows + rows : grid.rows + 2 * rows] = jnp.zeros((rows, POOLED), F32)


def first_pool(grid, local_rows, parts, length_ref, place_ref, *refs):
    rests, refs = (refs[:parts], refs[parts:])
    q_ref, out_sums_ref, all_ref, plane_ref, sums_ref, pool_sums_ref = refs
    length = length_ref[0]
    rows = grid.line_rows
    clear_edges(grid, plane_ref)
    sums_ref[...] = jnp.zeros_like(sums_ref)

    def visit(row, size, values):
        at = rows_at(row, size)
        all_ref[at, :] = values
        sums_ref[0:8] += partial_sum(values[:, :DIRECT])
        sums_ref[8:16] += partial_sum(values[:, :DIRECT] * values[:, :DIRECT])

    each_chunk(local_rows, parts, place_ref[0], rests, visit)

    @pl.loop(0, grid.side)
    def _(line):
        at = rows_at(line * rows, rows)
        q_ref[at, 0:DIRECT] = all_ref[at, 0:DIRECT]
        plane_ref[rows_at((line + 1) * rows, rows), :] = plane_box(all_ref[at, DIRECT:])

    pool_planes(grid, plane_ref, q_ref, DIRECT, pool_sums_ref, length, box_window(grid.side, length))
    write_sums(out_sums_ref, sums_ref, 0, DIRECT)
    write_sums(out_sums_ref, pool_sums_ref, DIRECT, DIRECT + POOLED)


def outer_moments(center, inverse, count, outer_ref):
    outer_ref[0:1, :] = center
    outer_ref[1:2, :] = inverse
    outer_ref[2:3, :] = jnp.concatenate([count[:, 0:128]] * (OUTER // 128), axis=1)


def first_output(grid, small, block, length_ref, q_far, e_far, moment_ref, e_sums_ref, rest_sums_ref, gain_ref, shift_ref, *refs):
    pooled_ref, h_far, slope_far, outer_ref, pooled_slope_ref, pooled_product_ref, *refs = refs
    q_ref, e_ref, h_ref, slope_ref, q_sem, e_sem, h_sem, slope_sem = refs
    rows = grid.line_rows
    wide = 2 * rows
    pairs = grid.side // 2

    def arriving(pair, slot):
        at = rows_at(pair * wide, wide)
        return [
            pltpu.make_async_copy(q_far.at[at, :], q_ref.at[slot], q_sem.at[slot]),
            pltpu.make_async_copy(e_far.at[at, :], e_ref.at[slot], e_sem.at[slot]),
        ]

    def leaving(pair, slot):
        at = rows_at(pair * wide, wide)
        return [
            pltpu.make_async_copy(h_ref.at[slot], h_far.at[at, :], h_sem.at[slot]),
            pltpu.make_async_copy(slope_ref.at[slot], slope_far.at[at, :], slope_sem.at[slot]),
        ]

    for copy in arriving(0, 0):
        copy.start()
    mask = frame_mask(rows, length_ref[0], OUTER)
    e_total, rest_total = (total_of(e_sums_ref), total_of(rest_sums_ref))
    total = jnp.concatenate(
        [rest_total[0:2, :DIRECT], e_total[0:2], rest_total[0:2, DIRECT:]], axis=1
    )
    count = jnp.concatenate([moment_ref[2:3, 0:128]] * (OUTER // 128), axis=1)
    center, inverse = moments(total[0:1], total[1:2], count)
    outer_moments(center, inverse, count, outer_ref)
    matrix = pool_matrix(small.side, False)
    gain, shift = (gain_ref[block : block + 1], shift_ref[block : block + 1])

    @pl.loop(0, pairs)
    def _(pair):
        slot = lax.rem(pair, 2)

        @pl.when(pair + 1 < pairs)
        def _():
            for copy in arriving(pair + 1, 1 - slot):
                copy.start()

        for copy in arriving(pair, slot):
            copy.wait()

        @pl.when(pair >= 2)
        def _():
            for copy in leaving(pair - 2, slot):
                copy.wait()

        acts, slopes, products = ([], [], [])
        for number in range(2):
            lines = slice(number * rows, (number + 1) * rows)
            values = jnp.concatenate(
                [q_ref[slot, lines, :DIRECT], e_ref[slot, lines, :], q_ref[slot, lines, DIRECT:]],
                axis=1,
            )
            scaled = (values - center) * inverse
            h_ref[slot, lines, :] = scaled.astype(BF16)
            shifted = gain * scaled + shift
            gate = sigmoid(shifted)
            gate_mask = gate * mask
            act = shifted * gate_mask
            slope = gate_mask + act * (1.0 - gate)
            low_slope = slope.astype(BF16)
            slope_ref[slot, lines, :] = low_slope
            acts.append(act.astype(BF16))
            slopes.append(low_slope)
            products.append((slope * scaled).astype(BF16))
        for copy in leaving(pair, slot):
            copy.start()
        at = rows_at(pair * small.line_rows, small.line_rows)
        for ref, pieces in (
            (pooled_ref, acts),
            (pooled_slope_ref, slopes),
            (pooled_product_ref, products),
        ):
            ref[at, :] = jnp.dot(
                matrix, jnp.concatenate(pieces, axis=0), preferred_element_type=F32
            ).astype(BF16)

    for pair in range(max(pairs - 2, 0), pairs):
        for copy in leaving(pair, pair % 2):
            copy.wait()


def second_pointwise(grid, length_ref, count_ref, x_ref, p_ref, q_ref, out_sums_ref, plane_ref, sums_ref, pool_sums_ref):
    length = length_ref[0]
    rows = grid.line_rows
    sums_ref[...] = jnp.zeros_like(sums_ref)
    clear_edges(grid, plane_ref)
    q_ref[...] = lax.dot_general(
        x_ref[...], p_ref[...], (((1,), (1,)), ((), ())), preferred_element_type=F32
    )

    @pl.loop(0, grid.side)
    def _(line):
        values = q_ref[rows_at(line * rows, rows), :]
        sums_ref[0:8] += partial_sum(values[:, :SECOND])
        sums_ref[8:16] += partial_sum(values[:, :SECOND] * values[:, :SECOND])
        plane_ref[rows_at((line + 1) * rows, rows), :] = plane_box(values[:, SECOND:])

    pool_planes(grid, plane_ref, q_ref, SECOND, pool_sums_ref, length, box_window(grid.side, length))
    write_sums(out_sums_ref, sums_ref, 0, SECOND)
    write_sums(out_sums_ref, pool_sums_ref, SECOND, FIRST)
    out_sums_ref[2:3, :] = jnp.full((1, FIRST), count_ref[0], F32)


def second_convolve(grid, block, length_ref, q_ref, sums_in_ref, gain_ref, shift_ref, *refs):
    far_kernels, outputs, moment_ref, scratch = (refs[:3], refs[3:8], refs[8], refs[9:])
    length = length_ref[0]
    center, inverse = reduced_moments(sums_in_ref, moment_ref, DIRECT, SECOND)
    gain, shift = (gain_ref[block : block + 1], shift_ref[block : block + 1])
    mask = frame_mask(grid.line_rows, length, REDUCED)

    def fill(h_ref, mid_ref, small_ref):
        @pl.loop(0, grid.side)
        def _(line):
            at = rows_at(line * grid.line_rows, grid.line_rows)
            scaled = (q_ref[at, DIRECT:SECOND] - center) * inverse
            h_ref[at, :] = scaled.astype(BF16)
            act = silu(gain * scaled + shift) * mask
            store_taps(
                mid_ref, small_ref, rows_at(grid.lead + line * grid.pitch, grid.line_rows), act
            )

    run_convolution(grid, length, far_kernels, outputs, scratch, fill)


def second_output(grid, block, length_ref, q_ref, e_ref, moment_ref, sums_in_ref, gain_ref, shift_ref, cot_ref, act_ref, h_ref, error_ref, outer_ref, out_sums_ref, sums_ref):
    rows = grid.line_rows
    side, frames = (grid.side, cot_ref.shape[1])
    mask = frame_mask(rows, length_ref[0], OUTER)
    total = total_of(sums_in_ref)
    count = moment_ref[2:3, 0:SECOND]
    center, inverse = moments(total[0:1], total[1:2], count)
    center = jnp.concatenate([moment_ref[0:1, :DIRECT], center, moment_ref[0:1, SECOND:]], axis=1)
    inverse = jnp.concatenate([moment_ref[1:2, :DIRECT], inverse, moment_ref[1:2, SECOND:]], axis=1)
    outer_moments(center, inverse, count, outer_ref)
    sums_ref[...] = jnp.zeros_like(sums_ref)
    gain, shift = (gain_ref[block : block + 1], shift_ref[block : block + 1])
    gap = jnp.zeros((rows, 64), F32)
    unused = jnp.zeros((side, PITCH - frames, CHANNELS), F32)

    @pl.loop(0, side)
    def _(line):
        at = rows_at(line * rows, rows)
        places = pl.ds(line * side, side)
        values = jnp.concatenate([q_ref[at, :DIRECT], e_ref[at, :], q_ref[at, SECOND:]], axis=1)
        scaled = (values - center) * inverse
        h_ref[at, :] = scaled.astype(BF16)
        shifted = gain * scaled + shift
        gate = sigmoid(shifted)
        act = (shifted * gate * mask).reshape(side, PITCH, OUTER)[:, :frames].astype(BF16)
        act_ref[places, :, 0:576] = act[:, :, 0:576]
        act_ref[places, :, 576:CHANNELS] = act[:, :, 640:OUTER]
        slope = gate * (1.0 + shifted * (1.0 - gate))
        grad = jnp.concatenate([cot_ref[places].astype(F32), unused], axis=1)
        grad = grad.reshape(rows, CHANNELS)
        grad = jnp.concatenate([grad[:, :576], gap, grad[:, 576:]], axis=1)
        error = grad * slope * mask
        error_ref[at, :] = error.astype(BF16)
        sums_ref[0:8] += partial_sum(error)
        sums_ref[8:16] += partial_sum(error * scaled)

    write_sums(out_sums_ref, sums_ref, 0, OUTER)


def spread_matrix(grid, small):
    return None if small is None else pool_matrix(small.side, True)[: grid.line_rows]


def outer_error(slopes, small, grad_ref, matrix, line, lo, hi):
    values = slopes.astype(F32)
    if small is None:
        return values
    coarse = grad_ref[rows_at((line // 2) * small.line_rows, small.line_rows), lo:hi]
    return values * jnp.dot(matrix, coarse, preferred_element_type=F32)


class Lines:
    def __init__(self, grid, sources, buffers, sem_ref):
        self.step = 2 if grid.side % 2 == 0 else 1
        self.size = self.step * grid.line_rows
        self.steps = grid.side // self.step
        self.sources, self.buffers, self.sem = (sources, buffers, sem_ref)

    def copies(self, step, slot):
        at = rows_at(step * self.size, self.size)
        return [
            pltpu.make_async_copy(
                ref.at[at, pl.ds(lo, hi - lo)],
                buffer.at[slot, :, pl.ds(place, hi - lo)],
                self.sem.at[number, slot],
            )
            for number, ((ref, lo, hi), (buffer, place)) in enumerate(
                zip(self.sources, self.buffers)
            )
        ]

    def first(self):
        for copy in self.copies(0, 0):
            copy.start()

    def run(self, visit):
        @pl.loop(0, self.steps)
        def _(step):
            slot = lax.rem(step, 2)

            @pl.when(step + 1 < self.steps)
            def _():
                for copy in self.copies(step + 1, 1 - slot):
                    copy.start()

            for copy in self.copies(step, slot):
                copy.wait()
            visit(step, slot)

    @staticmethod
    def rows(grid):
        return (2 if grid.side % 2 == 0 else 1) * grid.line_rows


def second_back(grid, small, block, slots, length_ref, first_ref, h_far, outer_ref, sums_in_ref, gain_ref, slope_far, *refs):
    grad_ref, refs = (refs[0], refs[1:]) if small is not None else (None, refs)
    mid_far, few_far, d_far, total_ref, out_ref, *refs = refs
    d_ref, h_ref, slope_ref, mid_ref, few_ref, mid_acc_ref, small_acc_ref, turned_ref, sem_ref, in_sem, out_sem = refs
    lo, hi = (DIRECT, DIRECT + SECOND)
    lines = Lines(grid, ((h_far, lo, hi), (slope_far, lo, hi)), ((h_ref, 0), (slope_ref, 0)), sem_ref)
    lines.first()
    arriving = copies((mid_far, few_far), (mid_ref, few_ref), in_sem)
    for copy in arriving:
        copy.start()
    total = total_of(sums_in_ref)
    total_ref[...] = total
    count = outer_ref[2:3, lo:hi]
    mean_r = total[0:1, lo:hi] / count
    mean_rh = total[1:2, lo:hi] / count
    factor = gain_ref[block : block + 1, lo:hi] * outer_ref[1:2, lo:hi]
    mask = frame_mask(grid.line_rows, length_ref[0], SECOND)
    matrix = spread_matrix(grid, small)
    zero_rows(d_ref)
    rows = grid.line_rows

    def visit(step, slot):
        for number in range(lines.step):
            line = step * lines.step + number
            here = slice(number * rows, (number + 1) * rows)
            scaled = h_ref[slot, here, :].astype(F32)
            error = outer_error(slope_ref[slot, here, :], small, grad_ref, matrix, line, lo, hi)
            back = factor * (error - mean_r - scaled * mean_rh) * mask
            d_ref[rows_at(grid.lead + line * grid.pitch, rows), :] = back.astype(BF16)

    lines.run(visit)
    leaving = pltpu.make_async_copy(d_ref, d_far, out_sem.at[0])
    leaving.start()
    for copy in arriving:
        copy.wait()
    kernel_grads(grid, slots, first_ref, mid_ref, few_ref, d_ref, out_ref, mid_acc_ref, small_acc_ref, turned_ref)
    leaving.wait()


def second_back_scratch(grid, slots):
    rows = Lines.rows(grid)
    return [
        pltpu.VMEM((grid.padded, SECOND), BF16),
        pltpu.VMEM((2, rows, SECOND), BF16),
        pltpu.VMEM((2, rows, SECOND), BF16),
        pltpu.VMEM((grid.padded, 512), BF16),
        pltpu.VMEM((grid.padded, 128), BF16),
        pltpu.VMEM((slots, 384, 256), F32),
        pltpu.VMEM((slots, 128, 128), F32),
        pltpu.VMEM((MID_IN + 128, 128), F32),
        pltpu.SemaphoreType.DMA((2, 2)),
        pltpu.SemaphoreType.DMA((2,)),
        pltpu.SemaphoreType.DMA((1,)),
    ]


def conv_back(grid, block, length_ref, d_ref, reduced_ref, reduced_gain_ref, reduced_shift_ref, *refs):
    far_kernels, (r_ref, out_sums_ref), refs = (refs[:3], refs[3:5], refs[5:])
    kernels, (last_ref, acc_ref, sums_ref, in_sem) = (refs[:3], refs[3:])
    main_ref, rest_ref, small_ref = kernels
    arriving = copies(far_kernels, kernels, in_sem)
    for copy in arriving:
        copy.start()
    rows = grid.line_rows
    group_rows = grid.group * grid.pitch
    sums_ref[...] = jnp.zeros_like(sums_ref)
    mask = frame_mask(rows, length_ref[0], REDUCED)
    gain, shift = (reduced_gain_ref[block : block + 1], reduced_shift_ref[block : block + 1])
    turned = (((1,), (1,)), ((), ()))
    lane = lax.broadcasted_iota(jnp.int32, (rows, 128), 1)
    wide_lane = lax.broadcasted_iota(jnp.int32, (grid.pitch, 128), 1)

    @pl.loop(0, grid.side)
    def _(line):
        place = grid.lead + line * grid.pitch
        here = d_ref[rows_at(place, grid.pitch), 256:384].astype(F32)
        further = d_ref[rows_at(place + grid.pitch, grid.pitch), 256:384].astype(F32)
        at = rows_at(place, grid.pitch)
        last_ref[at, 0:128] = jnp.where(wide_lane < 64, further, pltpu.roll(here, 64, 1)).astype(
            BF16
        )
        last_ref[at, 128:256] = d_ref[rows_at(place - grid.pitch, grid.pitch), 256:384]

    last_ref[grid.lead - PITCH : grid.lead, :] = jnp.zeros((PITCH, 256), BF16)
    end = grid.lead + grid.side * grid.pitch
    last_ref[end : end + PITCH, :] = jnp.zeros((PITCH, 256), BF16)
    for copy in arriving:
        copy.wait()

    @pl.loop(0, grid.side // grid.group)
    def _(group):
        base = grid.lead + group * group_rows
        for tap in range(9):
            part = lax.dot_general(
                d_ref[rows_at(tap_start(grid, base, tap, -1), group_rows), 0:256],
                main_ref[tap],
                turned,
                preferred_element_type=F32,
            )
            acc_ref[:, 0:512] = part if tap == 0 else acc_ref[:, 0:512] + part
        for place in range(3):
            acc_ref[:, 0:512] += lax.dot_general(
                last_ref[rows_at(base - (place - 1) * PITCH, group_rows), :],
                rest_ref[place],
                turned,
                preferred_element_type=F32,
            )
        near = [
            d_ref[rows_at(tap_start(grid, base, tap, -1), group_rows), 384:512] for tap in range(9)
        ]
        acc_ref[:, 512:640] = jnp.dot(
            jnp.concatenate(near, axis=1), small_ref[...], preferred_element_type=F32
        )
        for number in range(grid.group):
            line = group * grid.group + number
            lines = slice(number * grid.pitch, number * grid.pitch + rows)
            rest, small = (acc_ref[lines, 384:512], acc_ref[lines, 512:640])
            one = jnp.where(lane < 32, rest, pltpu.roll(small, 32, 1))
            two = jnp.where(lane < 32, pltpu.roll(rest, 96, 1), small)
            three = jnp.where(lane < 32, pltpu.roll(rest, 64, 1), pltpu.roll(small, 96, 1))
            wide = later(acc_ref[lines, 0:128]) + acc_ref[lines, 128:256]
            wide = wide + earlier(acc_ref[lines, 256:384])
            narrow = jnp.where(lane < 64, later(one) + two + earlier(three), 0.0)
            back = jnp.concatenate([wide, narrow], axis=1)
            at = rows_at(line * rows, rows)
            scaled = reduced_ref[at, :].astype(F32)
            error = back * silu_slope(gain * scaled + shift) * mask
            r_ref[at, :] = error.astype(BF16)
            sums_ref[0:8] += partial_sum(error)
            sums_ref[8:16] += partial_sum(error * scaled)

    write_sums(out_sums_ref, sums_ref, 0, REDUCED)


def kernel_grads(grid, slots, first_ref, mid_ref, small_ref, d_ref, out_ref, mid_acc_ref, small_acc_ref, turned_ref):
    group_rows = grid.group * grid.pitch
    mid_acc_ref[...] = jnp.zeros_like(mid_acc_ref)
    small_acc_ref[...] = jnp.zeros_like(small_acc_ref)

    def neighbour(slot):
        return jnp.minimum(first_ref[0] + slot, TAPS - 1) // 9

    @pl.loop(0, grid.side // grid.group)
    def _(group):
        base = grid.lead + group * group_rows
        left = d_ref[rows_at(base, group_rows), :].T
        for slot in range(slots):
            tap = lax.rem(jnp.minimum(first_ref[0] + slot, TAPS - 1), 9)
            at = rows_at(
                base + (tap // 3 - 1) * grid.pitch + (lax.rem(tap, 3) - 1) * PITCH, group_rows
            )
            lanes = pl.ds(pl.multiple_of(neighbour(slot) * 128, 128), 128)
            right = jnp.concatenate([mid_ref[at, lanes], mid_ref[at, 384:512]], axis=1)
            mid_acc_ref[slot] += jnp.dot(left[0:384], right, preferred_element_type=F32)
            small_acc_ref[slot] += jnp.dot(
                left[384:512], small_ref[at, :], preferred_element_type=F32
            )

    half = MID_IN // 2
    for slot in range(slots):
        base = slot * TAP_ROWS
        rest = pl.ds(pl.multiple_of(neighbour(slot) * 32, 32), 32)
        for tile in range(3):
            lines = slice(128 * tile, 128 * (tile + 1))
            turned_ref[0:128, :] = mid_acc_ref[slot, lines, 0:128].T
            turned_ref[MID_IN : MID_IN + 128, :] = mid_acc_ref[slot, lines, 128:256].T
            turned_ref[128:MID_IN, :] = turned_ref[
                pl.ds(pl.multiple_of(MID_IN + neighbour(slot) * 32, 32), 32), :
            ]
            if tile < 2:
                out_ref[base + MID_IN * tile : base + MID_IN * (tile + 1), :] = turned_ref[
                    0:MID_IN, :
                ].astype(BF16)
            else:
                folded = turned_ref[0:half, :] + pltpu.roll(turned_ref[half:MID_IN, :], 64, 1)
                out_ref[base + 2 * MID_IN : base + 2 * MID_IN + half, :] = folded.astype(BF16)
        turned_ref[0:128, :] = small_acc_ref[slot].T
        base = base + 2 * MID_IN + half
        out_ref[base : base + SMALL_IN, :] = turned_ref[rest, :].astype(BF16)
    used = slots * TAP_ROWS
    if out_ref.shape[0] > used:
        out_ref[used:, :] = jnp.zeros((out_ref.shape[0] - used, 128), BF16)


def point_back(grid, small, block, kept, length_ref, place_ref, h_far, outer_ref, total_ref, gain_ref, slope_far, *refs):
    first = small is not None
    grad_ref, refs = (refs[0], refs[1:]) if first else (None, refs)
    reduced_far, r_far, moment_ref, sums_in_ref, reduced_gain_ref, x_far, p_far, *refs = refs
    pooled_refs, refs = ((), refs) if first else (refs[:2], refs[2:])
    dx_ref, dp_ref, reduced_total_ref, *refs = refs
    outer_sums_ref, refs = (None, refs) if first else (refs[0], refs[1:])
    h_ref, slope_ref, reduced_ref, r_ref, x_ref, p_ref, du_ref, plane_ref, acc_ref, sem_ref, in_sem, *refs = refs
    rows = grid.line_rows
    pool = OUTER - POOLED
    lines = Lines(
        grid,
        (
            (h_far, 0, DIRECT),
            (h_far, pool, OUTER),
            (slope_far, 0, DIRECT),
            (slope_far, pool, OUTER),
            (reduced_far, 0, REDUCED),
            (r_far, 0, REDUCED),
        ),
        ((h_ref, 0), (h_ref, DIRECT), (slope_ref, 0), (slope_ref, DIRECT), (reduced_ref, 0), (r_ref, 0)),
        sem_ref,
    )
    lines.first()
    arriving = copies((x_far, p_far.at[place_ref[0]] if first else p_far), (x_ref, p_ref), in_sem)
    for copy in arriving:
        copy.start()
    length = length_ref[0]
    matrix = spread_matrix(grid, small)
    total = total_of(sums_in_ref)
    reduced_total_ref[...] = total
    count = outer_ref[2:3, 0:REDUCED]
    mid_r, mid_rh = (total[0:1] / count, total[1:2] / count)
    mid_factor = reduced_gain_ref[block : block + 1] * moment_ref[1:2]
    mask = frame_mask(rows, length, REDUCED)
    window = box_window(grid.side, length)
    clear_edges(grid, plane_ref)

    def constants(lo, hi):
        size = outer_ref[2:3, lo:hi]
        return (
            total_ref[0:1, lo:hi] / size,
            total_ref[1:2, lo:hi] / size,
            gain_ref[block : block + 1, lo:hi] * outer_ref[1:2, lo:hi],
        )

    direct_constants, pool_constants = (constants(0, DIRECT), constants(pool, OUTER))

    def visit(step, slot):
        for number in range(lines.step):
            line = step * lines.step + number
            here = slice(number * rows, (number + 1) * rows)
            at = rows_at(line * rows, rows)

            def section(lo, hi, kept_lo, kept_hi, constant):
                scaled = h_ref[slot, here, kept_lo:kept_hi].astype(F32)
                error = outer_error(
                    slope_ref[slot, here, kept_lo:kept_hi], small, grad_ref, matrix, line, lo, hi
                )
                inner = error - constant[0] - scaled * constant[1]
                return constant[2] * inner * mask[:, : hi - lo]

            du_ref[at, 0:DIRECT] = section(0, DIRECT, 0, DIRECT, direct_constants).astype(BF16)
            scaled = reduced_ref[slot, here, :].astype(F32)
            inner = r_ref[slot, here, :].astype(F32) - mid_r - scaled * mid_rh
            du_ref[at, DIRECT:SECOND] = (mid_factor * inner * mask).astype(BF16)
            pooled = section(pool, OUTER, DIRECT, DIRECT + POOLED, pool_constants)
            plane_ref[rows_at((line + 1) * rows, rows), :] = plane_box(
                pooled * box_scale(line, grid.side, window)
            )

    lines.run(visit)
    for copy in arriving:
        copy.wait()
    acc_ref[...] = jnp.zeros_like(acc_ref)
    if not first:
        refs[0][...] = jnp.zeros_like(refs[0])
    wide = lines.size
    pool_mask = frame_mask(wide, length)

    @pl.loop(0, lines.steps)
    def _(step):
        start = step * wide
        at = rows_at(start, wide)
        pooled = (
            plane_ref[at, :]
            + plane_ref[rows_at(start + rows, wide), :]
            + plane_ref[rows_at(start + 2 * rows, wide), :]
        ) * pool_mask
        du = jnp.concatenate([du_ref[at, 0:SECOND], pooled.astype(BF16)], axis=1)
        dx = jnp.dot(du, p_ref[...], preferred_element_type=F32).astype(BF16)
        dx_ref[at, :] = dx
        if not first:
            for number, ref in enumerate(pooled_refs):
                refs[0][8 * number : 8 * number + 8] += partial_sum(
                    dx.astype(F32) * ref[at, :].astype(F32)
                )
        acc_ref[...] += lax.dot_general(
            x_ref[at, :], du, (((0,), (0,)), ((), ())), preferred_element_type=F32
        )

    if not first:
        write_sums(outer_sums_ref, refs[0], 0, OUTER)
    start = pl.multiple_of(place_ref[0] * kept, 16) if kept < acc_ref.shape[0] else 0
    own = acc_ref[pl.ds(start, kept), :]
    for tile in range(FIRST // 128):
        dp_ref[kept * tile : kept * (tile + 1), :] = own[:, 128 * tile : 128 * (tile + 1)].astype(
            BF16
        )
    used = (FIRST // 128) * kept
    if dp_ref.shape[0] > used:
        dp_ref[used:, :] = jnp.zeros((dp_ref.shape[0] - used, 128), BF16)


def write_taps(buffer_ref, parts, slots, mid_ref, small_ref):
    half = MID_IN // 2

    @pl.loop(0, TAPS)
    def _(tap):
        base = lax.rem(tap, slots) * TAP_ROWS
        part = tap // slots

        def piece(start, size):
            return buffer_ref[part, rows_at(base + start, size), :].astype(F32)

        folded = piece(2 * MID_IN, half)
        mid_ref[tap, :, 0:128] = piece(0, MID_IN)
        mid_ref[tap, :, 128:256] = piece(MID_IN, MID_IN)
        mid_ref[tap, 0:half, 256:320] = folded[:, 0:64]
        mid_ref[tap, half:MID_IN, 256:320] = pltpu.roll(folded, 64, 1)[:, 0:64]
        small_ref[tap] = piece(2 * MID_IN + half, SMALL_IN)


def write_point(read, parts, kept, point_ref, wide_ref):
    for tile in range(FIRST // 128):
        for part in range(parts):
            start, stop = (kept * part, kept * (part + 1))
            values = read(part, kept * tile, kept)
            if kept * parts == CHANNELS:
                wide_ref[start:stop, :] = values
                continue
            for lo, hi, moved in ((0, 576, 0), (640, OUTER, 64)):
                lo, hi = (max(lo, start), min(hi, stop))
                if lo < hi:
                    wide_ref[lo - moved : hi - moved, :] = values[lo - start : hi - start]
        turned = wide_ref[...].T
        if tile < 3:
            point_ref[128 * tile : 128 * (tile + 1), :] = turned
        elif tile == 3:
            point_ref[384:448, :] = turned[0:64]
        else:
            point_ref[448:576, :] = turned


def copy_out(pairs, sem_ref):
    copies = [
        pltpu.make_async_copy(source, target, sem_ref.at[number])
        for number, (source, target) in enumerate(pairs)
    ]
    for copy in copies:
        copy.start()
    for copy in copies:
        copy.wait()


def unpack_second(parts, clips, slots, share, shares_ref, mid_out, small_out, point_out, taps_ref, rows_ref, mid_ref, small_ref, point_ref, wide_ref, sem_ref):
    size = shares_ref.shape[1] - share
    for part in range(parts):
        for clip in range(clips):
            taps_ref[part, share * clip : share * (clip + 1), :] = shares_ref[
                part * clips + clip, 0:share, :
            ]
            rows_ref[part, size * clip : size * (clip + 1), :] = shares_ref[
                part * clips + clip, share : share + size, :
            ]

    def read(part, start, size):
        return rows_ref[part, start : start + size, :].astype(F32)

    write_taps(taps_ref, parts, slots, mid_ref, small_ref)
    write_point(read, parts, OUTER // parts, point_ref, wide_ref)
    copy_out(
        [(mid_ref, mid_out.at[1]), (small_ref, small_out.at[1]), (point_ref, point_out.at[1])],
        sem_ref,
    )


def reorder(parts, clips, share, place, clip, mine_ref, other_ref, buffer_ref):
    for chip in range(clips // 2):
        for step in range(parts):
            source = (chip * parts + step) * share
            part = lax.rem(place - step + parts, parts)
            for swapped, ref in enumerate((mine_ref, other_ref)):
                owner = clip ^ (2 * chip) ^ swapped
                buffer_ref[part, rows_at(owner * share, share), :] = ref[
                    source : source + share, :
                ]


def unpack_taps(parts, clips, slots, share, place_ref, clip_ref, mine_ref, other_ref, *refs):
    totals, refs = (refs[:4], refs[4:])
    mid_in, small_in, mid_out, small_out, gain_out, shift_out, buffer_ref, mid_ref, small_ref, sem_ref = refs
    for block in range(2):
        outer_ref, reduced_ref = totals[2 * block : 2 * block + 2]
        for row, out in enumerate((shift_out, gain_out)):
            at, line = (slice(block, block + 1), slice(row, row + 1))
            out[at, 0:256] = outer_ref[line, 0:256]
            out[at, 256:448] = reduced_ref[line, 0:192]
            out[at, 448:576] = outer_ref[line, 768:896]
            out[at, 576:896] = outer_ref[line, 256:576]
            out[at, 896:1024] = outer_ref[line, 640:768]
    reorder(parts, clips, share, place_ref[0], clip_ref[0], mine_ref, other_ref, buffer_ref)
    write_taps(buffer_ref, parts, slots, mid_ref, small_ref)
    copy_out([(mid_ref, mid_out.at[0]), (small_ref, small_out.at[0])], sem_ref)


def unpack_point(parts, clips, share, place_ref, clip_ref, mine_ref, other_ref, point_in, point_out, buffer_ref, point_ref, wide_ref, sem_ref):
    reorder(parts, clips, share, place_ref[0], clip_ref[0], mine_ref, other_ref, buffer_ref)

    def read(part, start, size):
        return buffer_ref[part, start : start + size, :].astype(F32)

    write_point(read, parts, CHANNELS // parts, point_ref, wide_ref)
    copy_out([(point_ref, point_out.at[0])], sem_ref)


def prepare(parts, mid_in, small_in, point_in, gain_in, shift_in, *refs):
    kernels, (point_ref, second_ref, *vectors) = (refs[:8], refs[8:14])
    for block in range(2):
        main_ref, last_ref, few_ref, back_ref = kernels[4 * block : 4 * block + 4]

        @pl.loop(0, 9)
        def _(tap):
            for number in range(3):
                source = 9 * number + tap
                main_ref[tap, 128 * number : 128 * (number + 1), :] = mid_in[block, source, 0:128, 0:256]
                main_ref[tap, 384 + 32 * number : 416 + 32 * number, :] = mid_in[
                    block, source, 128:MID_IN, 0:256
                ]
            main_ref[tap, 480:512, :] = jnp.zeros((32, 256), BF16)
            small = jnp.concatenate(
                [small_in[block, 9 * number + tap] for number in range(3)]
                + [jnp.zeros((32, 128), BF16)],
                axis=0,
            )
            at = pl.ds(pl.multiple_of(tap * 128, 128), 128)
            few_ref[at, :] = small
            back_ref[at, :] = small.astype(F32).T.astype(BF16)

        @pl.loop(0, 3)
        def _(place):
            for number in range(3):
                for rows, start, size in (
                    (slice(0, 128), 128 * number, 128),
                    (slice(128, MID_IN), 384 + 32 * number, 32),
                ):
                    pieces = [
                        mid_in[block, 9 * number + 3 * line + place, rows, 256:MID_OUT].astype(F32)
                        for line in range(3)
                    ]
                    pieces.append(jnp.zeros((size, 64), F32))
                    last_ref[place, start : start + size, :] = jnp.concatenate(
                        pieces, axis=1
                    ).astype(BF16)
            last_ref[place, 480:512, :] = jnp.zeros((32, 256), BF16)

    own = point_ref.shape[2]
    for lo, hi, at in ((0, 448, 0), (448, SQUEEZED, SECOND)):
        values = point_in[0, lo:hi, :].astype(F32)
        for part in range(parts):
            point_ref[part, at : at + hi - lo, :] = values[:, own * part : own * (part + 1)].astype(
                BF16
            )
        values = point_in[1, lo:hi, :].astype(F32)
        gap = jnp.zeros((hi - lo, 64), F32)
        second_ref[at : at + hi - lo, :] = jnp.concatenate(
            [values[:, :576], gap, values[:, 576:]], axis=1
        ).astype(BF16)
    for part in range(parts):
        point_ref[part, 448:SECOND, :] = jnp.zeros((64, own), BF16)
    second_ref[448:SECOND, :] = jnp.zeros((64, OUTER), BF16)
    for source, outer, reduced in ((gain_in, vectors[0], vectors[1]), (shift_in, vectors[2], vectors[3])):
        outer[:, 0:256] = source[:, 0:256]
        outer[:, 256:576] = source[:, 576:896]
        outer[:, 576:640] = jnp.zeros((2, 64), F32)
        outer[:, 640:768] = source[:, 896:1024]
        outer[:, 768:896] = source[:, 448:576]
        reduced[:, 0:192] = source[:, 256:448]
        reduced[:, 192:256] = jnp.zeros((2, 64), F32)


def round_up(value, unit):
    return -(-value // unit) * unit


def spread_over(values, axis, size):
    received = [values]
    for step in range(1, size):
        perm = [(source, (source + step) % size) for source in range(size)]
        received.append(lax.ppermute(values, axis, perm))
    return received


def after(values, earlier):
    return lax.optimization_barrier((values, earlier))[0]


def shared_sum(packed, clips):
    pieces = packed.reshape(clips, packed.shape[0] // clips, 128)
    pieces = lax.all_to_all(pieces, "dp", 0, 0, tiled=True)
    return jnp.sum(pieces.astype(F32), axis=0).astype(BF16)


def gather_steps(share, parts, clips):
    column = jnp.concatenate(spread_over(share, "branch", parts), axis=0)
    columns = [column]
    for chip in range(1, clips // 2):
        perm = [(source, source ^ (2 * chip)) for source in range(clips)]
        columns.append(lax.ppermute(column, "dp", perm))
    mine = jnp.concatenate(columns, axis=0)
    other = lax.ppermute(mine, "dp", [(source, source ^ 1) for source in range(clips)])
    return (mine, other)


def on_device(frames, lengths, cotangent, pointwise, conv_mid, conv_small, gains, shifts):
    parts = lax.axis_size("branch")
    clips = lax.axis_size("dp")
    place = lax.axis_index("branch").astype(jnp.int32)
    side = frames.shape[2]
    grid, small = (Grid(side), Grid(side // 2))
    cells = side * side
    own_channels = frames.shape[-1]
    length = lengths.astype(jnp.int32)
    half_length = length // 2
    place_one = place.reshape(1)

    own = frames[0].transpose(1, 2, 0, 3).reshape(grid.rows, own_channels)
    local = -(-cells // parts)
    local_rows = local * PITCH
    split = own
    if parts * local_rows > grid.rows:
        split = jnp.pad(own, ((0, parts * local_rows - grid.rows), (0, 0)))
    by_places = lax.all_to_all(
        split.reshape(parts, local_rows, own_channels).transpose(0, 2, 1), "branch", 0, 0, tiled=True
    )
    kernel_shapes = (
        shape((9, 512, 256), BF16),
        shape((3, 512, 256), BF16),
        shape((1152, 128), BF16),
        shape((1152, 128), BF16),
    )
    prepared = call(
        functools.partial(prepare, parts),
        (
            *kernel_shapes,
            *kernel_shapes,
            shape((parts, FIRST, own_channels), BF16),
            shape((FIRST, OUTER), BF16),
            shape((2, OUTER), F32),
            shape((2, REDUCED), F32),
            shape((2, OUTER), F32),
            shape((2, REDUCED), F32),
        ),
    )(conv_mid, conv_small, pointwise.swapaxes(1, 2), gains, shifts)
    kernels = (prepared[0:4], prepared[4:8])
    point_first, point_second, outer_gain, reduced_gain, outer_shift, reduced_shift = prepared[8:]

    local_cells = jnp.clip(cells - place * local, 0, local)
    local_count = (length * local_cells).astype(F32)
    mid, rest = call(
        functools.partial(first_pointwise, parts),
        (
            shape((local_rows + PITCH, REDUCED), BF16),
            shape((local_rows + PITCH, DIRECT + POOLED), BF16),
        ),
        [pltpu.VMEM((local_rows, FIRST), F32)],
        scalars=2,
    )(length, local_count, by_places, point_first)
    mids = spread_over(mid, "branch", parts)
    rests = spread_over(after(rest, mids), "branch", parts)
    count = length.astype(F32) * float(cells)
    sums = call(
        functools.partial(first_sums, local_rows, parts),
        shape((3, REDUCED), F32),
        [pltpu.VMEM((16, REDUCED), F32)],
        scalars=2,
    )(place_one, count, *mids)
    sums = lax.all_gather(sums, "dp")
    h_reduced, taps_mid, taps_few, e, e_sums, moment = call(
        functools.partial(first_convolve, grid, 0, local_rows, parts),
        conv_outputs(grid, REDUCED),
        conv_scratch(grid),
        scalars=2,
        flops=2 * 10**10,
        far=range(5 + parts, 8 + parts),
        far_out=range(4),
    )(length, place_one, *mids, sums, reduced_gain, reduced_shift, *kernels[0][:3])
    q_rest, rest_sums = call(
        functools.partial(first_pool, grid, local_rows, parts),
        (shape((grid.rows, DIRECT + POOLED), F32), shape((2, DIRECT + POOLED), F32)),
        [
            pltpu.VMEM((parts * local_rows, DIRECT + POOLED), F32),
            pltpu.VMEM((grid.rows + 2 * grid.line_rows, POOLED), F32),
            pltpu.VMEM((16, DIRECT), F32),
            pltpu.VMEM((16, POOLED), F32),
        ],
        scalars=2,
    )(length, place_one, *rests)
    second_sums = lax.all_gather(jnp.concatenate([e_sums, rest_sums], axis=1), "dp")
    pair = 2 * grid.line_rows
    pooled, h_outer, slope, outer, pooled_slope, pooled_product = call(
        functools.partial(first_output, grid, small, 0),
        (
            shape((small.rows, OUTER), BF16),
            shape((grid.rows, OUTER), BF16),
            shape((grid.rows, OUTER), BF16),
            shape((3, OUTER), F32),
            shape((small.rows, OUTER), BF16),
            shape((small.rows, OUTER), BF16),
        ),
        [
            pltpu.VMEM((2, pair, DIRECT + POOLED), F32),
            pltpu.VMEM((2, pair, SECOND), F32),
            pltpu.VMEM((2, pair, OUTER), BF16),
            pltpu.VMEM((2, pair, OUTER), BF16),
            *[pltpu.SemaphoreType.DMA((2,))] * 4,
        ],
        scalars=1,
        far=(1, 2),
        far_out=(1, 2),
    )(length, q_rest, e, moment, second_sums[:, :, :SECOND], second_sums[:, :, SECOND:], outer_gain, outer_shift)

    small_count = half_length.astype(F32) * float(small.side * small.side)
    q_small, sums_small = call(
        functools.partial(second_pointwise, small),
        (shape((small.rows, FIRST), F32), shape((3, FIRST), F32)),
        [
            pltpu.VMEM((small.rows + 2 * small.line_rows, POOLED), F32),
            pltpu.VMEM((16, SECOND), F32),
            pltpu.VMEM((16, POOLED), F32),
        ],
        scalars=2,
    )(half_length, small_count, pooled, point_second)
    sums_small = lax.all_gather(sums_small, "dp")
    h_reduced_small, taps_mid_small, taps_few_small, e_small, e_sums_small, moment_small = call(
        functools.partial(second_convolve, small, 1),
        conv_outputs(small, FIRST),
        conv_scratch(small),
        scalars=1,
        far=range(5, 8),
        far_out=range(4),
    )(half_length, q_small, sums_small, reduced_gain, reduced_shift, *kernels[1][:3])
    e_sums_small = lax.all_gather(e_sums_small, "dp")
    cot = cotangent[0].transpose(1, 2, 0, 3).reshape(small.side**2, cotangent.shape[1], CHANNELS)
    act, h_outer_small, error_small, outer_small, outer_sums_small = call(
        functools.partial(second_output, small, 1),
        (
            shape(cot.shape, BF16),
            shape((small.rows, OUTER), BF16),
            shape((small.rows, OUTER), BF16),
            shape((3, OUTER), F32),
            shape((2, OUTER), F32),
        ),
        [pltpu.VMEM((16, OUTER), F32)],
        scalars=1,
    )(half_length, q_small, e_small, moment_small, e_sums_small, outer_gain, outer_shift, cot)

    slots = -(-TAPS // parts)
    tap_rows = round_up(slots * TAP_ROWS, 16 * clips)
    first_tap = place_one * slots

    def back(at, coarse, block, span, h_out, outer_moment, outer_sums, slopes, grads, h_red, taps, moment_of, x, point, kept, pooled_pair):
        first = coarse is not None
        gathered = lax.all_gather(outer_sums, "dp")
        d_low, total, packed_taps = call(
            functools.partial(second_back, at, coarse, block, slots),
            (
                shape((at.padded, SECOND), BF16),
                shape((2, OUTER), F32),
                shape((tap_rows, 128), BF16),
            ),
            second_back_scratch(at, slots),
            scalars=2,
            far=(2, 6, 7 + len(grads), 8 + len(grads)),
            far_out=(0,),
        )(span, first_tap, h_out, outer_moment, gathered, outer_gain, slopes, *grads, *taps)
        r_low, sums_low = call(
            functools.partial(conv_back, at, block),
            (shape((at.rows, REDUCED), BF16), shape((2, REDUCED), F32)),
            [
                pltpu.VMEM((9, 512, 256), BF16),
                pltpu.VMEM((3, 512, 256), BF16),
                pltpu.VMEM((1152, 128), BF16),
                pltpu.VMEM((at.padded, 256), BF16),
                pltpu.VMEM((at.group * at.pitch, FIRST), F32),
                pltpu.VMEM((16, REDUCED), F32),
                pltpu.SemaphoreType.DMA((3,)),
            ],
            scalars=1,
            flops=2 * 10**10 if first else 10**9,
            far=(5, 6, 7),
        )(span, d_low, h_red, reduced_gain, reduced_shift, *kernels[block][:2], kernels[block][3])
        gathered = lax.all_gather(sums_low, "dp")
        point_rows = round_up(kept * (FIRST // 128), 16 * clips)
        step = Lines.rows(at)
        wide = x.shape[1]
        moment_of = moment_of if first else moment_of[:, DIRECT:SECOND]
        dx, packed_point, reduced_total, *next_sums = call(
            functools.partial(point_back, at, coarse, block, kept),
            (
                shape((at.rows, wide), BF16),
                shape((point_rows, 128), BF16),
                shape((2, REDUCED), F32),
                *(() if first else (shape((2, OUTER), F32),)),
            ),
            [
                pltpu.VMEM((2, step, DIRECT + POOLED), BF16),
                pltpu.VMEM((2, step, DIRECT + POOLED), BF16),
                pltpu.VMEM((2, step, REDUCED), BF16),
                pltpu.VMEM((2, step, REDUCED), BF16),
                pltpu.VMEM((at.rows, wide), BF16),
                pltpu.VMEM((FIRST, wide), BF16),
                pltpu.VMEM((at.rows, SECOND), BF16),
                pltpu.VMEM((at.rows + 2 * at.line_rows, POOLED), F32),
                pltpu.VMEM((wide, FIRST), F32),
                pltpu.SemaphoreType.DMA((6, 2)),
                pltpu.SemaphoreType.DMA((2,)),
                *([] if first else [pltpu.VMEM((16, OUTER), F32)]),
            ],
            scalars=2,
            far=(2, 6, 7 + len(grads), 8 + len(grads), 12 + len(grads), 13 + len(grads)),
        )(
            span,
            place_one,
            h_out,
            outer_moment,
            total,
            outer_gain,
            slopes,
            *grads,
            h_red,
            r_low,
            moment_of,
            gathered,
            reduced_gain,
            x,
            point,
            *pooled_pair,
        )
        return (dx, packed_taps, packed_point, (total, reduced_total), next_sums)

    dx_small, taps_packed_small, point_packed_small, totals_small, (outer_sums,) = back(
        small, None, 1, half_length, h_outer_small, outer_small, outer_sums_small, error_small, (),
        h_reduced_small, (taps_mid_small, taps_few_small), moment_small, pooled, point_second,
        OUTER // parts, (pooled_slope, pooled_product),
    )
    share_small = shared_sum(
        jnp.concatenate(
            [
                taps_packed_small.reshape(clips, -1, 128),
                point_packed_small.reshape(clips, -1, 128),
            ],
            axis=1,
        ).reshape(-1, 128),
        clips,
    )
    whole_small = lax.all_gather(share_small, ("branch", "dp"), axis=0, tiled=True)
    dx, taps_packed, point_packed, totals, _ = back(
        grid, small, 0, length, h_outer, outer, outer_sums, slope, (dx_small,),
        h_reduced, (taps_mid, taps_few), moment, own, point_first, own_channels, (),
    )
    taps_mine, taps_other = gather_steps(shared_sum(taps_packed, clips), parts, clips)
    point_mine, point_other = gather_steps(shared_sum(point_packed, clips), parts, clips)

    outs = (
        shape((2, TAPS, MID_IN, MID_OUT), F32),
        shape((2, TAPS, SMALL_IN, SMALL_OUT), F32),
        shape((2, SQUEEZED, CHANNELS), F32),
    )
    mid_scratch = pltpu.VMEM((TAPS, MID_IN, MID_OUT), F32)
    small_scratch = pltpu.VMEM((TAPS, SMALL_IN, SMALL_OUT), F32)
    point_scratch = [pltpu.VMEM((SQUEEZED, CHANNELS), F32), pltpu.VMEM((CHANNELS, 128), F32)]
    point_rows = point_packed.shape[0]
    tap_share = tap_rows // clips
    mid_grad, small_grad, point_grad = call(
        functools.partial(unpack_second, parts, clips, slots, tap_share),
        outs,
        [
            pltpu.VMEM((parts, tap_rows, 128), BF16),
            pltpu.VMEM((parts, point_packed_small.shape[0], 128), BF16),
            mid_scratch,
            small_scratch,
            *point_scratch,
            pltpu.SemaphoreType.DMA((3,)),
        ],
        out_space=pl.ANY,
    )(whole_small.reshape(parts * clips, -1, 128))
    clip_one = lax.axis_index("dp").astype(jnp.int32).reshape(1)
    norms = shape((2, 1024), F32)
    mid_grad, small_grad, gain_grad, shift_grad = call(
        functools.partial(unpack_taps, parts, clips, slots, tap_share),
        (*outs[:2], norms, norms),
        [
            pltpu.VMEM((parts, tap_rows, 128), BF16),
            mid_scratch,
            small_scratch,
            pltpu.SemaphoreType.DMA((2,)),
        ],
        scalars=2,
        far_out=(0, 1),
        aliases={8: 0, 9: 1},
    )(place_one, clip_one, taps_mine, taps_other, *totals, *totals_small, mid_grad, small_grad)
    point_grad = call(
        functools.partial(unpack_point, parts, clips, point_rows // clips),
        outs[2],
        [
            pltpu.VMEM((parts, point_rows, 128), BF16),
            *point_scratch,
            pltpu.SemaphoreType.DMA((1,)),
        ],
        scalars=2,
        out_space=pl.ANY,
        aliases={4: 0},
    )(place_one, clip_one, point_mine, point_other, point_grad)
    act = act.reshape(small.side, small.side, cotangent.shape[1], CHANNELS).transpose(2, 0, 1, 3)
    input_grad = dx.reshape(side, side, PITCH, own_channels).transpose(2, 0, 1, 3)
    return (
        act[None],
        input_grad[None],
        point_grad.swapaxes(1, 2),
        mid_grad,
        small_grad,
        gain_grad,
        shift_grad,
    )


def solution(mesh):
    split = P("dp", None, None, None, "branch")
    whole = P("dp", None, None, None, None)
    return jax.shard_map(
        on_device,
        mesh=mesh,
        in_specs=(split, P("dp"), whole, P(), P(), P(), P(), P()),
        out_specs=(whole, split, P(), P(), P(), P(), P()),
        check_vma=False,
    )
```

time: 534 us -> 460 us (0.86)
  Pallas kernels: 225 us -> 189 us
  local copies, waits for them, and re-layouts: 37.9 us -> 14 us
  other arithmetic: 24.6 us -> 2.74 us
  starting transfers between devices: 55.4 us -> 66.6 us
    pallas_call x18, Pallas kernels: 225 us -> 189 us  [run(): pl.pallas_call(body, out_shape=out_shape, in_specs=specs, out_specs=out_s...]
    all_to_all x1, waiting for transfers between devices: 11 us -> 24.3 us  [on_device(): lax.all_to_all(split.reshape(parts, local_rows, own_channels).transpose(0...]
    concatenate x5 -> x0, other arithmetic: 9.79 us -> none  [the longest x1 2.37 us: point_columns(): return jnp.concatenate([point[:, :448], gap, point[:, 448:]], axis=1)]
    ppermute x18 -> x12, starting transfers between devices: 33.1 us -> 42.9 us  [spread_over(): received.append(lax.ppermute(values, axis, perm))]
    all_to_all x2, waiting for transfers between devices: 11.4 us -> 3.22 us  [shared_sum(): pieces = lax.all_to_all(pieces, 'dp', 0, 0, tiled=True)]
    add x2 -> x0, other arithmetic: 7.72 us -> none  [wide_kernels(): return (mid + small).reshape(9, 3 * REDUCED, SECOND)]
    slice x29 -> x3, local copies, waits for them, and re-layouts: 9.95 us -> 2.5 us  [the longest x1 1.27 us: back(): moment_of = moment_of if first else moment_of[:, DIRECT:SECOND]]
    unnamed x78 -> x36, local copies, waits for them, and re-layouts: 11.2 us -> 8.19 us
  transfers between devices with their start and end apart: 30 -> 24, of which waited for: 11 -> 10; matrix products, arithmetic and copies ran while one was open for 10% -> 1% of each run, Pallas kernels for 26% -> 23%
where the time goes in v3:
time: 460 us; the launch traced here: 454 us
  Pallas kernels  189 us (41%)
  blocking collectives  97.2 us (21%)
  waiting for transfers between devices  70 us (15%)
  starting transfers between devices  66.6 us (14%)
  between operations  15 us (3%)
  local copies, waits for them, and re-layouts  14 us (3%)
    pallas_call x18, Pallas kernels, run(): pl.pallas_call(body, out_shape=out_shape, in_specs=specs, out_specs=out_s...  189 us
    ppermute x12, starting transfers between devices, spread_over(): received.append(lax.ppermute(values, axis, perm))  42.9 us
    ppermute x12, waiting for transfers between devices, spread_over(): received.append(lax.ppermute(values, axis, perm))  26.4 us
    all_to_all x1, waiting for transfers between devices, on_device(): lax.all_to_all(split.reshape(parts, local_rows, own_channels).transpose(0...  24.3 us
    all_gather x2, blocking collectives, back(): gathered = lax.all_gather(sums_low, 'dp')  20.6 us
    all_gather x2, blocking collectives, back(): gathered = lax.all_gather(outer_sums, 'dp')  19.1 us
    all_to_all x1, blocking collectives, shared_sum(): pieces = lax.all_to_all(pieces, 'dp', 0, 0, tiled=True)  18.3 us
    ppermute x6, waiting for transfers between devices, gather_steps(): columns.append(lax.ppermute(column, 'dp', perm))  16.1 us
  transfers between devices with their start and end apart: 24, of which 10 were waited for; matrix products, arithmetic and copies ran while one was open for 1% of the time, Pallas kernels for 23%

profile of v3, /device:TPU:0, one launch (start us, length us, event | category | flops | bytes accessed | tf_op | source)
XLA Modules:
  0.0 454.1 jit_solution(7677085016501244973)
XLA Ops:
  7.2 2.6 copy.19
  9.8 6.3 %all-to-all-start = ((bf16[4,208,784]{2,1,0:T(8,128)(2,1)}), bf16[4,208,784]{2,1,0:T(8,128)(2,1)S(1)}, u32[]{:S(2)}, u32[]{:S(2)}) async-start(bf16[4,208,784]{2,1,0:T(8,128)(2,1)} %bitcast.5), calls=%async_computation | async-start | bytes 2981888 | tf_op jit(solution)/shard_map/all_to_all | solution.py:1244
  16.8 10.3 %shard_map.135 = (bf16[9,512,256]{2,1,0:T(8,128)(2,1)}, bf16[3,512,256]{2,1,0:T(8,128)(2,1)}, bf16[1152,128]{1,0:T(8,128)(2,1)}, bf16[1152,128]{1,0:T(8,128)(2,1...) custom-call(bf16[2,27,160,320]{3,2,1,0:T(8,128)(2,1)} %mid_in.1, ...), custom_call_target="tpu_custom_call" | custom-call | flops 1000000000 | bytes 16777216 | tf_op jit(solution)/shard_map/pallas_call | solution.py:52
  27.0 24.3 %all-to-all-done.x_ref = bf16[4,208,784]{2,1,0:T(8,128)(2,1)S(1)} async-done(((bf16[4,208,784]{2,1,0:T(8,128)(2,1)}), bf16[4,208,784]{2,1,0:T(8,128)(2,1)S(1)}, u32[]{:S(2)}, u32[]{:S(2)}) %all-to-all-start) | async-done | bytes 1304608 | tf_op jit(solution)/shard_map/all_to_all | solution.py:1244
  52.4 4.6 %shard_map.136 = (bf16[800,256]{1,0:T(8,128)(2,1)}, bf16[800,384]{1,0:T(8,128)(2,1)}) custom-call(s32[1]{0:T(128)S(6)} %copy.35.length_ref, f32[1]{0:T(128)S(6)} %convert_element_type.7.count_ref, bf16[4,208,784]{2,1,0:T(8,128)(2,1)} %copy-done.2, bf16[4,640,208]{2,1,0:T(8,128)(2,1)} %get-tuple-element.75.p_ref.refs_7_), custom_call_target="tpu_custom_call" | custom-call | flops 1000000000 | bytes 16777216 | tf_op jit(solution)/shard_map/pallas_call | solution.py:52
  57.0 2.0 collective-permute-start.1
  59.1 1.8 collective-permute-start.2
  60.9 10.7 %collective-permute-done.refs_1_ = bf16[800,256]{1,0:T(8,128)(2,1)S(1)} collective-permute-done((bf16[800,256]{1,0:T(8,128)(2,1)}, bf16[800,256]{1,0:T(8,128)(2,1)S(1)}, u32[]{:S(2)}, u32[]{:S(2)}) %collective-permute-start) | collective-permute-done | bytes 409632 | tf_op jit(solution)/shard_map/ppermute | solution.py:1201
  71.5 15.7 %collective-permute-done.1.refs_2_ = bf16[800,256]{1,0:T(8,128)(2,1)S(1)} collective-permute-done((bf16[800,256]{1,0:T(8,128)(2,1)}, bf16[800,256]{1,0:T(8,128)(2,1)S(1)}, u32[]{:S(2)}, u32[]{:S(2)}) %collective-permute-start.1) | collective-permute-done | bytes 409632 | tf_op jit(solution)/shard_map/ppermute | solution.py:1201
  87.2 29.0 %collective-permute-start.3 = (bf16[800,384]{1,0:T(8,128)(2,1)}, bf16[800,384]{1,0:T(8,128)(2,1)S(1)}, u32[]{:S(2)}, u32[]{:S(2)}) collective-permute-start(bf16[800,384]{1,0:T(8,128)(2,1)} %get-tuple-element.78.refs_0_), channel_id=1, source_target_pairs={{0,1},{1,2},{2,3},{3,0},{4,5},{5,6},{6,7},{7,4},{8,9},{9,10},{10,1... | collective-permute-start | bytes 1843208 | tf_op jit(solution)/shard_map/ppermute | solution.py:1201
  116.2 2.4 collective-permute-start.5
  118.6 2.7 shard_map.138
  121.3 10.8 %all-gather.8.refs_4_ = f32[8,3,256]{2,1,0:T(4,128)} all-gather(f32[1,3,256]{2,1,0:T(4,128)} %bitcast.56), channel_id=2, replica_groups=mesh['dp'=8,'branch'=4] {'dp'}, dimensions={0}, use_global_device_ids=true | all-gather | bytes 27648 | tf_op jit(solution)/shard_map/all_gather | solution.py:1289
  132.1 25.9 %shard_map.139 = (bf16[3136,256]{1,0:T(8,128)(2,1)}, bf16[3872,512]{1,0:T(8,128)(2,1)}, bf16[3872,128]{1,0:T(8,128)(2,1)}, f32[3136,512]{1,0:T(8,128)}, f32[2,512]{1,0:T(2,128)}, /*index=5*/f32[3,256]{1,0:T(4,128)}) custom-call(s32[1]{0:T(128)S(6)} %copy.35.length_ref, s32[1]{0:T(128)} %bitcast.place_ref, bf16[800,256]{1,0:T(8,128)(2,1)} %get-tuple-element.77.refs_0_, ...), custom_call_target="tpu_custom_call" | custom-call | flops 20000000000 | bytes 16777216 | tf_op jit(solution)/shard_map/pallas_call | solution.py:52
  159.9 6.2 %shard_map.137 = (f32[3136,384]{1,0:T(8,128)}, f32[2,384]{1,0:T(2,128)}) custom-call(s32[1]{0:T(128)S(6)} %copy.35.length_ref, s32[1]{0:T(128)} %bitcast.place_ref, bf16[800,384]{1,0:T(8,128)(2,1)} %get-tuple-element.78.refs_0_, bf16[800,384]{1,0:T(8,128)(2,1)} %copy-done.6, bf16[800,384]{1,0:T(8,128)(2,1)} %copy-done.7, bf16[800,384]{1,0:T(8,128)(2,1)} %copy-done.8), custom_call_target="tpu_custom_call" | custom-call | flops 1000000000 | bytes 16777216 | tf_op jit(solution)/shard_map/pallas_call | solution.py:52
  166.8 8.4 %all-gather.9 = f32[8,2,896]{2,1,0:T(2,128)S(1)} all-gather(f32[1,2,896]{2,1,0:T(2,128)S(1)} %maximum_bitcast_fusion), channel_id=3, replica_groups=mesh['dp'=8,'branch'=4] {'dp'}, dimensions={0}, use_global_device_ids=true | all-gather | bytes 64512 | tf_op jit(solution)/shard_map/all_gather | solution.py:1310
  176.4 14.2 %shard_map.140 = (bf16[784,896]{1,0:T(8,128)(2,1)}, bf16[3136,896]{1,0:T(8,128)(2,1)}, bf16[3136,896]{1,0:T(8,128)(2,1)}, f32[3,896]{1,0:T(4,128)}, bf16[784,896]{1,0:T(8,128)(2,1)}, /*index=5*/bf16[784,896]{1,0:T(8,128)(2,1)}) custom-call(s32[1]{0:T(128)S(6)} %copy.35.length_ref, f32[3136,384]{1,0:T(8,128)} %get-tuple-element.79.q_far, ...), custom_call_target="tpu_custom_call" | custom-call | flops 1000000000 | bytes 16777216 | tf_op jit(solution)/shard_map/pallas_call | solution.py:52
  190.7 5.0 %shard_map.141 = (f32[784,640]{1,0:T(8,128)}, f32[3,640]{1,0:T(4,128)}) custom-call(s32[1]{0:T(128)S(6)} %select_n.5.length_ref, f32[1]{0:T(128)S(6)} %mul.18.count_ref, bf16[784,896]{1,0:T(8,128)(2,1)} %get-tuple-element.91.x_ref.refs_5_, bf16[640,896]{1,0:T(8,128)(2,1)} %get-tuple-element.92.p_ref.refs_6_), custom_call_target="tpu_custom_call" | custom-call | flops 1000000000 | bytes 16777216 | tf_op jit(solution)/shard_map/pallas_call | solution.py:52
  195.7 10.1 %all-gather.10.sums_in_ref = f32[8,3,640]{2,1,0:T(4,128)} all-gather(f32[1,3,640]{2,1,0:T(4,128)} %bitcast.52), channel_id=4, replica_groups=mesh['dp'=8,'branch'=4] {'dp'}, dimensions={0}, use_global_device_ids=true | all-gather | bytes 69120 | tf_op jit(solution)/shard_map/all_gather | solution.py:1345
  205.8 8.9 %shard_map.142 = (bf16[784,256]{1,0:T(8,128)(2,1)}, bf16[1184,512]{1,0:T(8,128)(2,1)}, bf16[1184,128]{1,0:T(8,128)(2,1)}, f32[784,512]{1,0:T(8,128)}, f32[2,512]{1,0:T(2,128)}, /*index=5*/f32[3,640]{1,0:T(4,128)}) custom-call(s32[1]{0:T(128)S(6)} %select_n.5.length_ref, f32[784,640]{1,0:T(8,128)} %get-tuple-element.93.q_ref, ...), custom_call_target="tpu_custom_call" | custom-call | flops 1000000000 | bytes 16777216 | tf_op jit(solution)/shard_map/pallas_call | solution.py:52
  214.8 9.8 %all-gather.11.sums_in_ref = f32[8,2,512]{2,1,0:T(2,128)} all-gather(f32[1,2,512]{2,1,0:T(2,128)} %bitcast.55), channel_id=5, replica_groups=mesh['dp'=8,'branch'=4] {'dp'}, dimensions={0}, use_global_device_ids=true | all-gather | bytes 36864 | tf_op jit(solution)/shard_map/all_gather | solution.py:1354
  225.9 6.7 %shard_map.143 = (bf16[49,8,832]{2,1,0:T(8,128)(2,1)}, bf16[784,896]{1,0:T(8,128)(2,1)}, bf16[784,896]{1,0:T(8,128)(2,1)}, f32[3,896]{1,0:T(4,128)}, f32[2,896]{1,0:T(2,128)}) custom-call(s32[1]{0:T(128)S(6)} %select_n.5.length_ref, f32[784,640]{1,0:T(8,128)} %get-tuple-element.93.q_ref, f32[784,512]{1,0:T(8,128)} %get-tuple-element.98.e_ref, ...), custom_call_target="tpu_custom_call" | custom-call | flops 1000000000 | bytes 16777216 | tf_op jit(solution)/shard_map/pallas_call | solution.py:52
  232.5 9.9 %all-gather.12.sums_in_ref = f32[8,2,896]{2,1,0:T(2,128)} all-gather(f32[1,2,896]{2,1,0:T(2,128)} %bitcast.54), channel_id=6, replica_groups=mesh['dp'=8,'branch'=4] {'dp'}, dimensions={0}, use_global_device_ids=true | all-gather | bytes 64512 | tf_op jit(solution)/shard_map/all_gather | solution.py:1375
  242.4 8.6 %shard_map.144 = (bf16[1184,512]{1,0:T(8,128)(2,1)}, f32[2,896]{1,0:T(2,128)}, bf16[3072,128]{1,0:T(8,128)(2,1)}) custom-call(s32[1]{0:T(128)S(6)} %select_n.5.length_ref, s32[1]{0:T(128)S(6)} %mul.23.first_ref, bf16[784,896]{1,0:T(8,128)(2,1)} %get-tuple-element.104.h_far, f32[3,896]{1,0:T(4,128)} %get-tuple-element.105.outer_ref, ...), custom_call_target="tpu_custom_call" | custom-call | flops 1000000000 | bytes 16777216 | tf_op jit(solution)/shard_map/pallas_call | solution.py:52
  251.0 8.0 %shard_map.145 = (bf16[784,256]{1,0:T(8,128)(2,1)}, f32[2,256]{1,0:T(2,128)}) custom-call(s32[1]{0:T(128)S(6)} %select_n.5.length_ref, bf16[1184,512]{1,0:T(8,128)(2,1)} %get-tuple-element.112.d_ref, bf16[784,256]{1,0:T(8,128)(2,1)} %get-tuple-element.111.reduced_ref.refs_0_, f32[2,256]{1,0:T(2,128)} %get-tuple-element.80.refs_5_.gain_ref.reduced_gain_ref.refs_4_, ...), custom_call_target="tpu_custom_call" | custom-call | flops 1000000000 | bytes 16777216 | tf_op jit(solution)/shard_map/pallas_call | solution.py:52
  259.1 9.7 %all-gather.13.refs_3_ = f32[8,2,256]{2,1,0:T(2,128)} all-gather(f32[1,2,256]{2,1,0:T(2,128)} %bitcast.58), channel_id=7, replica_groups=mesh['dp'=8,'branch'=4] {'dp'}, dimensions={0}, use_global_device_ids=true | all-gather | bytes 18432 | tf_op jit(solution)/shard_map/all_gather | solution.py:1404
  268.8 12.7 %shard_map.146 = (bf16[784,896]{1,0:T(8,128)(2,1)}, bf16[1152,128]{1,0:T(8,128)(2,1)}, f32[2,256]{1,0:T(2,128)}, f32[2,896]{1,0:T(2,128)}) custom-call(s32[1]{0:T(128)S(6)} %select_n.5.length_ref, s32[1]{0:T(128)} %bitcast.place_ref, bf16[784,896]{1,0:T(8,128)(2,1)} %get-tuple-element.104.h_far, f32[3,896]{1,0:T(4,128)} %get-tuple-element.105.outer_ref, ...), custom_call_target="tpu_custom_call" | custom-call | flops 1000000000 | bytes 16777216 | tf_op jit(solution)/shard_map/pallas_call | solution.py:52
  282.5 18.3 %all_to_all.20 = bf16[8,528,128]{2,1,0:T(8,128)(2,1)S(1)} all-to-all(bf16[8,528,128]{2,1,0:T(8,128)(2,1)S(1)} %pad_maximum_fusion), channel_id=1, replica_groups=mesh['dp'=8,'branch'=4] {'dp'}, dimensions={0} | all-to-all | bytes 2162688 | tf_op jit(solution)/shard_map/all_to_all | solution.py:1211
  301.6 9.2 %all-gather.14.sums_in_ref = f32[8,2,896]{2,1,0:T(2,128)} all-gather(f32[1,2,896]{2,1,0:T(2,128)S(1)} %bitcast.53), channel_id=8, replica_groups=mesh['dp'=8,'branch'=4] {'dp'}, dimensions={0}, use_global_device_ids=true | all-gather | bytes 64512 | tf_op jit(solution)/shard_map/all_gather | solution.py:1375
  310.8 19.4 %shard_map.147 = (bf16[3872,512]{1,0:T(8,128)(2,1)}, f32[2,896]{1,0:T(2,128)}, bf16[3072,128]{1,0:T(8,128)(2,1)}) custom-call(s32[1]{0:T(128)S(6)} %copy.35.length_ref, s32[1]{0:T(128)S(6)} %mul.23.first_ref, bf16[3136,896]{1,0:T(8,128)(2,1)} %get-tuple-element.102.h_far, f32[3,896]{1,0:T(4,128)} %get-tuple-element.103.outer_ref, ...), custom_call_target="tpu_custom_call" | custom-call | flops 1000000000 | bytes 16777216 | tf_op jit(solution)/shard_map/pallas_call | solution.py:52
  330.2 3.6 all-to-all-start.3
  333.8 21.6 %shard_map.148 = (bf16[3136,256]{1,0:T(8,128)(2,1)}, f32[2,256]{1,0:T(2,128)}) custom-call(s32[1]{0:T(128)S(6)} %copy.35.length_ref, bf16[3872,512]{1,0:T(8,128)(2,1)} %get-tuple-element.125.d_ref, bf16[3136,256]{1,0:T(8,128)(2,1)} %get-tuple-element.124.reduced_ref.refs_1_, f32[2,256]{1,0:T(2,128)} %get-tuple-element.80.refs_5_.gain_ref.reduced_gain_ref.refs_4_, ...), custom_call_target="tpu_custom_call" | custom-call | flops 20000000000 | bytes 16777216 | tf_op jit(solution)/shard_map/pallas_call | solution.py:52
  355.4 11.0 %all-gather.15.refs_4_ = f32[8,2,256]{2,1,0:T(2,128)} all-gather(f32[1,2,256]{2,1,0:T(2,128)} %bitcast.57), channel_id=9, replica_groups=mesh['dp'=8,'branch'=4] {'dp'}, dimensions={0}, use_global_device_ids=true | all-gather | bytes 18432 | tf_op jit(solution)/shard_map/all_gather | solution.py:1404
  366.4 14.5 %shard_map.149 = (bf16[3136,208]{1,0:T(8,128)(2,1)}, bf16[1152,128]{1,0:T(8,128)(2,1)}, f32[2,256]{1,0:T(2,128)}) custom-call(s32[1]{0:T(128)S(6)} %copy.35.length_ref, s32[1]{0:T(128)} %bitcast.place_ref, bf16[3136,896]{1,0:T(8,128)(2,1)} %get-tuple-element.102.h_far, f32[3,896]{1,0:T(4,128)} %get-tuple-element.103.outer_ref, ...), custom_call_target="tpu_custom_call" | custom-call | flops 1000000000 | bytes 16777216 | tf_op jit(solution)/shard_map/pallas_call | solution.py:52
  380.8 3.4 all-to-all-start.1
  384.5 2.8 collective-permute-start.14
  388.3 3.2 all-to-all-done.1
  391.6 2.8 collective-permute-start.7
  395.5 2.5 collective-permute-start.16
  397.9 1.6 collective-permute-start.17
  399.6 5.9 %collective-permute-done.16 = bf16[1536,128]{1,0:T(8,128)(2,1)S(1)} collective-permute-done((bf16[1536,128]{1,0:T(8,128)(2,1)S(1)}, bf16[1536,128]{1,0:T(8,128)(2,1)S(1)}, u32[]{:S(2)}, u32[]{:S(2)}) %collective-permute-start.16) | collective-permute-done | bytes 393248 | tf_op jit(solution)/shard_map/ppermute | solution.py:1220
  405.6 2.6 collective-permute-start.18
  408.2 5.7 %collective-permute-done.17 = bf16[1536,128]{1,0:T(8,128)(2,1)S(1)} collective-permute-done((bf16[1536,128]{1,0:T(8,128)(2,1)S(1)}, bf16[1536,128]{1,0:T(8,128)(2,1)S(1)}, u32[]{:S(2)}, u32[]{:S(2)}) %collective-permute-start.17) | collective-permute-done | bytes 393248 | tf_op jit(solution)/shard_map/ppermute | solution.py:1220
  417.0 1.4 collective-permute-start.10
  423.5 1.5 collective-permute-done.10
  426.9 8.3 %shard_map.150 = (f32[2,27,160,320]{3,2,1,0:T(8,128)}, f32[2,27,32,128]{3,2,1,0:T(8,128)}, f32[2,576,832]{2,1,0:T(8,128)}) custom-call(bf16[32,528,128]{2,1,0:T(8,128)(2,1)} %bitcast.44), custom_call_target="tpu_custom_call" | custom-call | flops 1000000000 | bytes 16777216 | tf_op jit(solution)/shard_map/pallas_call | solution.py:52
  435.2 3.0 shard_map.151
  439.4 7.9 %shard_map.152 = (f32[2,27,160,320]{3,2,1,0:T(8,128)}, f32[2,27,32,128]{3,2,1,0:T(8,128)}, f32[2,1024]{1,0:T(2,128)}, f32[2,1024]{1,0:T(2,128)}) custom-call(s32[1]{0:T(128)} %bitcast.place_ref, s32[1]{0:T(128)} %bitcast.26.clip_ref, bf16[6144,128]{1,0:T(8,128)(2,1)} %copy-done, ...), custom_call_target="tpu_custom_call", output_to_operand_aliasing={{0}: (8, {}), {1}: (9, {})} | custom-call | flops 1000000000 | bytes 16777216 | tf_op jit(solution)/shard_map/pallas_call | solution.py:52
  (77 shorter events, 21.6 us)
Async XLA Ops:
  9.8 41.5 %all-to-all-start = ((bf16[4,208,784]{2,1,0:T(8,128)(2,1)}), bf16[4,208,784]{2,1,0:T(8,128)(2,1)S(1)}, u32[]{:S(2)}, u32[]{:S(2)}) async-start(bf16[4,208,784]{2,1,0:T(8,128)(2,1)} %bitcast.5), calls=%async_computation | async-start | bytes 2981888 | tf_op jit(solution)/shard_map/all_to_all | solution.py:1244
  16.1 410.7 %all-gather.18.cloned.1.call-start = ((), (), s32[]{:S(2)}) async-start(), calls=%async_computation.4 | async-start | bytes 4460544 | tf_op jit(solution)/shard_map/all_gather | solution.py:1468
  51.3 1.1 copy-start.2
  57.0 14.5 %collective-permute-start = (bf16[800,256]{1,0:T(8,128)(2,1)}, bf16[800,256]{1,0:T(8,128)(2,1)S(1)}, u32[]{:S(2)}, u32[]{:S(2)}) collective-permute-start(bf16[800,256]{1,0:T(8,128)(2,1)} %get-tuple-element.77.refs_0_), channel_id=1, source_target_pairs={{0,1},{1,2},{2,3},{3,0},{4,5},{5,6},{6,7},{7,4},{8,9},{9,10},{10,1... | collective-permute-start | bytes 1228808 | tf_op jit(solution)/shard_map/ppermute | solution.py:1201
  57.0 30.2 %collective-permute-start.1 = (bf16[800,256]{1,0:T(8,128)(2,1)}, bf16[800,256]{1,0:T(8,128)(2,1)S(1)}, u32[]{:S(2)}, u32[]{:S(2)}) collective-permute-start(bf16[800,256]{1,0:T(8,128)(2,1)} %get-tuple-element.77.refs_0_), channel_id=1, source_target_pairs={{0,2},{1,3},{2,0},{3,1},{4,6},{5,7},{6,4},{7,5},{8,10},{9,11},{10,... | collective-permute-start | bytes 1228808 | tf_op jit(solution)/shard_map/ppermute | solution.py:1201
  59.1 28.2 %collective-permute-start.2 = (bf16[800,256]{1,0:T(8,128)(2,1)}, bf16[800,256]{1,0:T(8,128)(2,1)S(1)}, u32[]{:S(2)}, u32[]{:S(2)}) collective-permute-start(bf16[800,256]{1,0:T(8,128)(2,1)} %get-tuple-element.77.refs_0_), channel_id=1, source_target_pairs={{0,3},{1,0},{2,1},{3,2},{4,7},{5,4},{6,5},{7,6},{8,11},{9,8},{10,9... | collective-permute-start | bytes 1228808 | tf_op jit(solution)/shard_map/ppermute | solution.py:1201
  71.5 47.1 %copy-start.9 = (bf16[800,256]{1,0:T(8,128)(2,1)}, bf16[800,256]{1,0:T(8,128)(2,1)S(1)}, u32[]{:S(2)}) copy-start(bf16[800,256]{1,0:T(8,128)(2,1)S(1)} %collective-permute-done.refs_1_) | copy-start | bytes 1228804
  87.2 31.4 %copy-start.10 = (bf16[800,256]{1,0:T(8,128)(2,1)}, bf16[800,256]{1,0:T(8,128)(2,1)S(1)}, u32[]{:S(2)}) copy-start(bf16[800,256]{1,0:T(8,128)(2,1)S(1)} %collective-permute-done.1.refs_2_) | copy-start | bytes 1228804
  87.2 31.4 %copy-start.11 = (bf16[800,256]{1,0:T(8,128)(2,1)}, bf16[800,256]{1,0:T(8,128)(2,1)S(1)}, u32[]{:S(2)}) copy-start(bf16[800,256]{1,0:T(8,128)(2,1)S(1)} %collective-permute-done.2.refs_3_) | copy-start | bytes 1228804
  87.2 70.8 %collective-permute-start.3 = (bf16[800,384]{1,0:T(8,128)(2,1)}, bf16[800,384]{1,0:T(8,128)(2,1)S(1)}, u32[]{:S(2)}, u32[]{:S(2)}) collective-permute-start(bf16[800,384]{1,0:T(8,128)(2,1)} %get-tuple-element.78.refs_0_), channel_id=1, source_target_pairs={{0,1},{1,2},{2,3},{3,0},{4,5},{5,6},{6,7},{7,4},{8,9},{9,10},{10,1... | collective-permute-start | bytes 1843208 | tf_op jit(solution)/shard_map/ppermute | solution.py:1201
  116.2 41.8 %collective-permute-start.4 = (bf16[800,384]{1,0:T(8,128)(2,1)}, bf16[800,384]{1,0:T(8,128)(2,1)S(1)}, u32[]{:S(2)}, u32[]{:S(2)}) collective-permute-start(bf16[800,384]{1,0:T(8,128)(2,1)} %get-tuple-element.78.refs_0_), channel_id=1, source_target_pairs={{0,2},{1,3},{2,0},{3,1},{4,6},{5,7},{6,4},{7,5},{8,10},{9,11},{10,... | collective-permute-start | bytes 1843208 | tf_op jit(solution)/shard_map/ppermute | solution.py:1201
  116.2 41.8 %collective-permute-start.5 = (bf16[800,384]{1,0:T(8,128)(2,1)}, bf16[800,384]{1,0:T(8,128)(2,1)S(1)}, u32[]{:S(2)}, u32[]{:S(2)}) collective-permute-start(bf16[800,384]{1,0:T(8,128)(2,1)} %get-tuple-element.78.refs_0_), channel_id=1, source_target_pairs={{0,3},{1,0},{2,1},{3,2},{4,7},{5,4},{6,5},{7,6},{8,11},{9,8},{10,9... | collective-permute-start | bytes 1843208 | tf_op jit(solution)/shard_map/ppermute | solution.py:1201
  158.0 8.1 %copy-start.5 = (f32[2,512]{1,0:T(2,128)S(1)}, f32[2,512]{1,0:T(2,128)}, u32[]{:S(2)}) copy-start(f32[2,512]{1,0:T(2,128)} %get-tuple-element.87) | copy-start | bytes 12292
  158.0 0.8 copy-start.6
  158.1 1.0 copy-start.7
  159.1 0.8 copy-start.8
  268.8 12.7 %copy-start.3 = (bf16[3072,128]{1,0:T(8,128)(2,1)S(1)}, bf16[3072,128]{1,0:T(8,128)(2,1)}, u32[]{:S(2)}) copy-start(bf16[3072,128]{1,0:T(8,128)(2,1)} %get-tuple-element.131) | copy-start | bytes 2359300
  282.5 19.1 %copy-start.4 = (f32[2,896]{1,0:T(2,128)S(1)}, f32[2,896]{1,0:T(2,128)}, u32[]{:S(2)}) copy-start(f32[2,896]{1,0:T(2,128)} %get-tuple-element.118) | copy-start | bytes 21508
  330.2 50.6 %all-to-all-start.3 = ((bf16[8,384,128]{2,1,0:T(8,128)(2,1)}), bf16[8,384,128]{2,1,0:T(8,128)(2,1)S(1)}, u32[]{:S(2)}, u32[]{:S(2)}) async-start(bf16[8,384,128]{2,1,0:T(8,128)(2,1)} %bitcast.47), calls=%async_computation.3 | async-start | bytes 1572864 | tf_op jit(solution)/shard_map/all_to_all | solution.py:1211
  380.8 10.7 %all-to-all-start.1 = ((bf16[8,144,128]{2,1,0:T(8,128)(2,1)}), bf16[8,144,128]{2,1,0:T(8,128)(2,1)S(1)}, u32[]{:S(2)}, u32[]{:S(2)}) async-start(bf16[8,144,128]{2,1,0:T(8,128)(2,1)} %bitcast.50), calls=%async_computation.1 | async-start | bytes 589824 | tf_op jit(solution)/shard_map/all_to_all | solution.py:1211
  384.4 10.0 %collective-permute-start.13 = (bf16[384,128]{1,0:T(8,128)(2,1)S(1)}, bf16[384,128]{1,0:T(8,128)(2,1)S(1)}, u32[]{:S(2)}, u32[]{:S(2)}) collective-permute-start(bf16[384,128]{1,0:T(8,128)(2,1)S(1)} %reduce_sum.38), channel_id=1, source_target_pairs={{0,1},{1,2},{2,3},{3,0},{4,5},{5,6},{6,7},{7,4},{8,9},{9,10},{10,1... | collective-permute-start | bytes 294920 | tf_op jit(solution)/shard_map/ppermute | solution.py:1201
  384.5 11.0 %collective-permute-start.14 = (bf16[384,128]{1,0:T(8,128)(2,1)S(1)}, bf16[384,128]{1,0:T(8,128)(2,1)S(1)}, u32[]{:S(2)}, u32[]{:S(2)}) collective-permute-start(bf16[384,128]{1,0:T(8,128)(2,1)S(1)} %reduce_sum.38), channel_id=1, source_target_pairs={{0,2},{1,3},{2,0},{3,1},{4,6},{5,7},{6,4},{7,5},{8,10},{9,11},{10,... | collective-permute-start | bytes 294920 | tf_op jit(solution)/shard_map/ppermute | solution.py:1201
  387.3 8.2 %collective-permute-start.15 = (bf16[384,128]{1,0:T(8,128)(2,1)S(1)}, bf16[384,128]{1,0:T(8,128)(2,1)S(1)}, u32[]{:S(2)}, u32[]{:S(2)}) collective-permute-start(bf16[384,128]{1,0:T(8,128)(2,1)S(1)} %reduce_sum.38), channel_id=1, source_target_pairs={{0,3},{1,0},{2,1},{3,2},{4,7},{5,4},{6,5},{7,6},{8,11},{9,8},{10,9... | collective-permute-start | bytes 294920 | tf_op jit(solution)/shard_map/ppermute | solution.py:1201
  391.6 24.5 %collective-permute-start.6 = (bf16[144,128]{1,0:T(8,128)(2,1)S(1)}, bf16[144,128]{1,0:T(8,128)(2,1)S(1)}, u32[]{:S(2)}, u32[]{:S(2)}) collective-permute-start(bf16[144,128]{1,0:T(8,128)(2,1)S(1)} %reduce_sum.36), channel_id=1, source_target_pairs={{0,1},{1,2},{2,3},{3,0},{4,5},{5,6},{6,7},{7,4},{8,9},{9,10},{10,1... | collective-permute-start | bytes 110600 | tf_op jit(solution)/shard_map/ppermute | solution.py:1201
  391.6 24.4 %collective-permute-start.7 = (bf16[144,128]{1,0:T(8,128)(2,1)S(1)}, bf16[144,128]{1,0:T(8,128)(2,1)S(1)}, u32[]{:S(2)}, u32[]{:S(2)}) collective-permute-start(bf16[144,128]{1,0:T(8,128)(2,1)S(1)} %reduce_sum.36), channel_id=1, source_target_pairs={{0,2},{1,3},{2,0},{3,1},{4,6},{5,7},{6,4},{7,5},{8,10},{9,11},{10,... | collective-permute-start | bytes 110600 | tf_op jit(solution)/shard_map/ppermute | solution.py:1201
  394.4 21.6 %collective-permute-start.8 = (bf16[144,128]{1,0:T(8,128)(2,1)S(1)}, bf16[144,128]{1,0:T(8,128)(2,1)S(1)}, u32[]{:S(2)}, u32[]{:S(2)}) collective-permute-start(bf16[144,128]{1,0:T(8,128)(2,1)S(1)} %reduce_sum.36), channel_id=1, source_target_pairs={{0,3},{1,0},{2,1},{3,2},{4,7},{5,4},{6,5},{7,6},{8,11},{9,8},{10,9... | collective-permute-start | bytes 110600 | tf_op jit(solution)/shard_map/ppermute | solution.py:1201
  395.5 10.1 %collective-permute-start.16 = (bf16[1536,128]{1,0:T(8,128)(2,1)S(1)}, bf16[1536,128]{1,0:T(8,128)(2,1)S(1)}, u32[]{:S(2)}, u32[]{:S(2)}) collective-permute-start(bf16[1536,128]{1,0:T(8,128)(2,1)S(1)} %pad_maximum_fusion.1), channel_id=1, source_target_pairs={{0,8},{4,12},{8,0},{12,4},{16,24},{20,28},{24,16},{28,20},{1,9},{5... | collective-permute-start | bytes 1179656 | tf_op jit(solution)/shard_map/ppermute | solution.py:1220
  397.9 16.0 %collective-permute-start.17 = (bf16[1536,128]{1,0:T(8,128)(2,1)S(1)}, bf16[1536,128]{1,0:T(8,128)(2,1)S(1)}, u32[]{:S(2)}, u32[]{:S(2)}) collective-permute-start(bf16[1536,128]{1,0:T(8,128)(2,1)S(1)} %pad_maximum_fusion.1), channel_id=1, source_target_pairs={{0,16},{4,20},{8,24},{12,28},{16,0},{20,4},{24,8},{28,12},{1,17},{... | collective-permute-start | bytes 1179656 | tf_op jit(solution)/shard_map/ppermute | solution.py:1220
  405.6 9.6 %collective-permute-start.18 = (bf16[1536,128]{1,0:T(8,128)(2,1)S(1)}, bf16[1536,128]{1,0:T(8,128)(2,1)S(1)}, u32[]{:S(2)}, u32[]{:S(2)}) collective-permute-start(bf16[1536,128]{1,0:T(8,128)(2,1)S(1)} %pad_maximum_fusion.1), channel_id=1, source_target_pairs={{0,24},{4,28},{8,16},{12,20},{16,8},{20,12},{24,0},{28,4},{1,25},{... | collective-permute-start | bytes 1179656 | tf_op jit(solution)/shard_map/ppermute | solution.py:1220
  415.2 20.0 %copy-start = (bf16[6144,128]{1,0:T(8,128)(2,1)}, bf16[6144,128]{1,0:T(8,128)(2,1)S(1)}, u32[]{:S(2)}) copy-start(bf16[6144,128]{1,0:T(8,128)(2,1)S(1)} %constant_dynamic-update-slice_fusion.7.mine_ref) | copy-start | bytes 4718596
  415.2 23.0 %collective-permute-start.19 = (bf16[6144,128]{1,0:T(8,128)(2,1)S(1)}, bf16[6144,128]{1,0:T(8,128)(2,1)S(1)}, u32[]{:S(2)}, u32[]{:S(2)}) collective-permute-start(bf16[6144,128]{1,0:T(8,128)(2,1)S(1)} %constant_dynamic-update-slice_fusion.7.mine_ref), channel_id=1, source_target_pairs={{0,4},{4,0},{8,12},{12,8},{16,20},{20,16},{24,28},{28,24},{1,5},{5... | collective-permute-start | bytes 4718600 | tf_op jit(solution)/shard_map/ppermute | solution.py:1222
  416.1 6.7 %collective-permute-start.9 = (bf16[576,128]{1,0:T(8,128)(2,1)S(1)}, bf16[576,128]{1,0:T(8,128)(2,1)S(1)}, u32[]{:S(2)}, u32[]{:S(2)}) collective-permute-start(bf16[576,128]{1,0:T(8,128)(2,1)S(1)} %pad_maximum_fusion.2), channel_id=1, source_target_pairs={{0,8},{4,12},{8,0},{12,4},{16,24},{20,28},{24,16},{28,20},{1,9},{5... | collective-permute-start | bytes 442376 | tf_op jit(solution)/shard_map/ppermute | solution.py:1220
  417.0 7.9 %collective-permute-start.10 = (bf16[576,128]{1,0:T(8,128)(2,1)S(1)}, bf16[576,128]{1,0:T(8,128)(2,1)S(1)}, u32[]{:S(2)}, u32[]{:S(2)}) collective-permute-start(bf16[576,128]{1,0:T(8,128)(2,1)S(1)} %pad_maximum_fusion.2), channel_id=1, source_target_pairs={{0,16},{4,20},{8,24},{12,28},{16,0},{20,4},{24,8},{28,12},{1,17},{... | collective-permute-start | bytes 442376 | tf_op jit(solution)/shard_map/ppermute | solution.py:1220
  418.4 7.7 %collective-permute-start.11 = (bf16[576,128]{1,0:T(8,128)(2,1)S(1)}, bf16[576,128]{1,0:T(8,128)(2,1)S(1)}, u32[]{:S(2)}, u32[]{:S(2)}) collective-permute-start(bf16[576,128]{1,0:T(8,128)(2,1)S(1)} %pad_maximum_fusion.2), channel_id=1, source_target_pairs={{0,24},{4,28},{8,16},{12,20},{16,8},{20,12},{24,0},{28,4},{1,25},{... | collective-permute-start | bytes 442376 | tf_op jit(solution)/shard_map/ppermute | solution.py:1220
  426.8 8.4 %collective-permute-start.12 = (bf16[2304,128]{1,0:T(8,128)(2,1)}, bf16[2304,128]{1,0:T(8,128)(2,1)}, u32[]{:S(2)}, u32[]{:S(2)}) collective-permute-start(bf16[2304,128]{1,0:T(8,128)(2,1)} %constant_dynamic-update-slice_fusion.mine_ref), channel_id=1, source_target_pairs={{0,4},{4,0},{8,12},{12,8},{16,20},{20,16},{24,28},{28,24},{1,5},{5... | collective-permute-start | bytes 1769480 | tf_op jit(solution)/shard_map/ppermute | solution.py:1222
  438.3 1.2 copy-start.1
Sparse Core Ops, SparseCore 0:
  301.7 60.3 all-gather.17
